TPU v7x, 32 devices: a whole 2x2x4 slice. The times are simulated.
32 devices in a mesh: ctx: 8 (over z, core), fsdp: 4 (over y, x).
Axes of the slice: x: 2, y: 2, z: 4, core: 2. Of those that a mesh axis runs over, the one named last changes fastest.
Arguments:
- tokens: bfloat16 [4, 1024, 2304], P('fsdp', 'ctx'), may hold values from -36 to 36, as said below
- w_query: bfloat16 [2304, 2048], P(('ctx', 'fsdp')), may hold values from -0.5 to 0.5
- w_key: bfloat16 [2304, 1024], P(('ctx', 'fsdp')), may hold values from -0.125 to 0.125
- w_value: bfloat16 [2304, 1024], P(('ctx', 'fsdp')), may hold values from -0.125 to 0.125
- w_out: bfloat16 [2048, 2304], P(('ctx', 'fsdp')), may hold values from -0.125 to 0.125
- w_gate: bfloat16 [2304, 9216], P(('ctx', 'fsdp')), may hold values from -0.125 to 0.125
- w_up: bfloat16 [2304, 9216], P(('ctx', 'fsdp')), may hold values from -0.125 to 0.125
- w_down: bfloat16 [9216, 2304], P(('ctx', 'fsdp')), may hold values from -0.0625 to 0.0625
- pre_gain: bfloat16 [2304], P(('ctx', 'fsdp')), may hold values from -0.5 to 0.5
- post_gain: bfloat16 [2304], P(('ctx', 'fsdp')), may hold values from -0.5 to 0.5
- pre_ffn_gain: bfloat16 [2304], P(('ctx', 'fsdp')), may hold values from -0.5 to 0.5
- post_ffn_gain: bfloat16 [2304], P(('ctx', 'fsdp')), may hold values from -0.5 to 0.5
- out_grad: bfloat16 [4, 1024, 2304], P('fsdp', 'ctx'), may hold values from -6 to 6
Outputs:
- output: bfloat16 [4, 1024, 2304], P('fsdp', 'ctx')
- token_grad: bfloat16 [4, 1024, 2304], P('fsdp', 'ctx')
- w_query_grad: float32 [2304, 2048], P(('ctx', 'fsdp'))
- w_key_grad: float32 [2304, 1024], P(('ctx', 'fsdp'))
- w_value_grad: float32 [2304, 1024], P(('ctx', 'fsdp'))
- w_out_grad: float32 [2048, 2304], P(('ctx', 'fsdp'))
- w_gate_grad: float32 [2304, 9216], P(('ctx', 'fsdp'))
- w_up_grad: float32 [2304, 9216], P(('ctx', 'fsdp'))
- w_down_grad: float32 [9216, 2304], P(('ctx', 'fsdp'))
- pre_gain_grad: float32 [2304], P(('ctx', 'fsdp'))
- post_gain_grad: float32 [2304], P(('ctx', 'fsdp'))
- pre_ffn_gain_grad: float32 [2304], P(('ctx', 'fsdp'))
- post_ffn_gain_grad: float32 [2304], P(('ctx', 'fsdp'))
Inputs may be any that keep to these rules, and one draw needn't show every extreme that they name: `tokens`: token rows and feature columns carry scales of their own.
All inputs are finite; a program needn't handle non-finite values.
Results may differ from a plain program's by a relative error of at most 0.02.
The roundings to bfloat16 on the way count: a program that leaves them out, or rounds other values in their place, can miss the bound.
Values may be sent and summed in bfloat16 or wider, within the bound.
A program may use at most 640 MiB of HBM per device.

v0:
```python
import jax
import jax.numpy as jnp
from jax import lax
from jax.sharding import PartitionSpec as P

D = 2304
H = 8
KVH = 4
HD = 256
CAP = 50
FF = 9216


EPSILON = 1e-06
ROPE_BASE = 10000.0
ROW_FOLD = 4


def rope_tables(positions, width):
    half_width = width // 2
    inv_freqs = ROPE_BASE ** (-jnp.arange(half_width, dtype=jnp.float32) * 2.0 / width)
    angles = positions.astype(jnp.float32)[:, None] * inv_freqs[None, :]
    return (jnp.cos(angles)[:, None, :], jnp.sin(angles)[:, None, :])


def rotate(heads_in, cos_tab, sine_tab):
    half_width = heads_in.shape[-1] // 2
    front_half = heads_in[..., :half_width]
    back_half = heads_in[..., half_width:]
    return jnp.concatenate(
        [front_half * cos_tab - back_half * sine_tab, back_half * cos_tab + front_half * sine_tab],
        axis=-1,
    )


def unrotate(grad_in, cos_tab, sine_tab):
    half_width = grad_in.shape[-1] // 2
    front_half = grad_in[..., :half_width]
    back_half = grad_in[..., half_width:]
    return jnp.concatenate(
        [front_half * cos_tab + back_half * sine_tab, back_half * cos_tab - front_half * sine_tab],
        axis=-1,
    )


def rms_parts(values_in):
    inverse = lax.rsqrt(jnp.mean(values_in * values_in, axis=-1, keepdims=True) + EPSILON)
    return (inverse, values_in * inverse)


def norm_back(grad_normed, normed, inverse):
    return inverse * (grad_normed - normed * jnp.mean(grad_normed * normed, axis=-1, keepdims=True))


def to_groups(flat_heads, tok_rows, q_group):
    shaped = flat_heads.reshape(tok_rows, KVH, q_group, HD)
    return jnp.transpose(shaped, (1, 2, 0, 3)).reshape(KVH, q_group * tok_rows, HD)


def from_groups(grouped, tok_rows, q_group):
    shaped = grouped.reshape(KVH, q_group, tok_rows, HD)
    return jnp.transpose(shaped, (2, 0, 1, 3)).reshape(tok_rows, KVH * q_group * HD)


def contract_rows(left, right):
    return lax.dot_general(
        left, right, (((0,), (0,)), ((), ())), preferred_element_type=jnp.float32
    )


def contract_cols(left, right):
    return lax.dot_general(
        left, right, (((1,), (1,)), ((), ())), preferred_element_type=jnp.float32
    )


def fold_rows(left, piece):
    return jnp.dot(left, piece, preferred_element_type=jnp.float32)


def grad_rows(left, right, folding, count):
    block = contract_rows(left, right)
    return block.reshape(count, right.shape[1] // folding)


def gated(gate_in, up_in):
    return jax.nn.gelu(gate_in, approximate=True) * up_in


def blockwise(step_fn, carry, piece, width):
    key_count = piece[0].shape[0]
    n_steps = key_count // width
    stacked = tuple((member.reshape(n_steps, width, member.shape[1]) for member in piece))

    def one_step(partial_value, block_item):
        block_index, members = block_item
        return (step_fn(partial_value, members, block_index * width), None)

    carry, unused = lax.scan(one_step, carry, (jnp.arange(n_steps, dtype=jnp.int32), stacked))
    return carry


def block_grads(query_g, query_pos, d_att_g, delta, inv_tot, key_block, value_block, key_first):
    key_count = key_block.shape[0]
    key_grp = key_block.reshape(key_count, KVH, HD)
    value_grp = value_block.reshape(key_count, KVH, HD)
    raw_scores = jnp.einsum("grd,ngd->grn", query_g, key_grp, preferred_element_type=jnp.float32)
    capped = CAP * jnp.tanh(raw_scores / CAP)
    key_pos = key_first + jnp.arange(key_count, dtype=jnp.int32)
    allowed = key_pos[None, None, :] <= query_pos[None, :, None]
    weights = jnp.where(allowed, jnp.exp(capped), 0.0)
    prob_rows = weights * inv_tot[..., None]
    d_probs = jnp.einsum("grd,ngd->grn", d_att_g, value_grp, preferred_element_type=jnp.float32)
    slope = 1.0 - capped / CAP * (capped / CAP)
    d_raw = (prob_rows * (d_probs - delta[..., None]) * slope).astype(jnp.bfloat16)
    d_query = jnp.einsum("grn,ngd->grd", d_raw, key_grp, preferred_element_type=jnp.float32)
    d_key = jnp.einsum("grn,grd->ngd", d_raw, query_g, preferred_element_type=jnp.float32)
    weights_b = weights.astype(jnp.bfloat16)
    d_scaled = d_att_g.astype(jnp.float32) * inv_tot[..., None]
    scaled_high = d_scaled.astype(jnp.bfloat16)
    scaled_rest = (d_scaled - scaled_high.astype(jnp.float32)).astype(jnp.bfloat16)
    d_value = jnp.einsum("grn,grd->ngd", weights_b, scaled_high, preferred_element_type=jnp.float32)
    d_value = d_value + jnp.einsum(
        "grn,grd->ngd", weights_b, scaled_rest, preferred_element_type=jnp.float32
    )
    return (d_query, d_key.reshape(key_count, KVH * HD), d_value.reshape(key_count, KVH * HD))


def on_device(
    tokens,
    w_query,
    w_key,
    w_value,
    w_out,
    w_gate,
    w_up,
    w_down,
    pre_gain,
    post_gain,
    pre_ffn_gain,
    post_ffn_gain,
    out_grad,
):
    tok_rows = tokens.shape[1]
    q_group = H // KVH
    q_scale = HD ** (-0.5)
    width_q = H * HD
    width_kv = KVH * HD
    width_qkv = width_q + 2 * width_kv
    n_ctx = lax.axis_size("ctx")
    my_block = lax.axis_index("ctx")
    my_start = my_block * tok_rows
    positions = my_start + jnp.arange(tok_rows, dtype=jnp.int32)
    cos_tab, sine_tab = rope_tables(positions, HD)
    row_pos = jnp.tile(positions, q_group)
    last_pos = my_start + tok_rows - 1
    resid_in = tokens[0].astype(jnp.float32)
    qkv_shard = jnp.concatenate([w_query, w_key, w_value], axis=1)
    gateup_shard = jnp.concatenate([w_gate, w_up], axis=1)
    shard_rows = qkv_shard.shape[0]
    gains_shard = jnp.stack([pre_gain, post_gain, pre_ffn_gain, post_ffn_gain])
    full_gains, full_qkv, full_out = (
        lax.all_gather(gains_shard, ("ctx", "fsdp"), axis=1, tiled=True),
        lax.all_gather(qkv_shard, ("ctx", "fsdp"), axis=0, tiled=True),
        lax.all_gather(w_out, ("ctx", "fsdp"), axis=0, tiled=True),
    )
    factors = 1.0 + full_gains.astype(jnp.float32)
    pre_factor, post_factor, pre_ffn_factor, post_ffn_factor = (
        factors[0],
        factors[1],
        factors[2],
        factors[3],
    )
    inv_pre, normed_pre = rms_parts(resid_in)
    hidden = (normed_pre * pre_factor).astype(jnp.bfloat16)
    projected = jnp.dot(hidden, full_qkv, preferred_element_type=jnp.float32)
    query_lin = projected[:, :width_q].reshape(tok_rows, H, HD)
    queries = (
        (rotate(query_lin, cos_tab, sine_tab) * q_scale)
        .astype(jnp.bfloat16)
        .reshape(tok_rows, width_q)
    )
    query_grp = to_groups(queries, tok_rows, q_group)
    key_lin = projected[:, width_q : width_q + width_kv].reshape(tok_rows, KVH, HD)
    key_rows = rotate(key_lin, cos_tab, sine_tab).astype(jnp.bfloat16).reshape(tok_rows, width_kv)
    value_rows = projected[:, width_q + width_kv :].astype(jnp.bfloat16)

    def add_block(partial_value, piece, first_row):
        key_block, value_block = piece

        def add_compute_block(state):
            row_total, weighted = state
            key_count = key_block.shape[0]
            key_grp = key_block.reshape(key_count, KVH, HD)
            raw_scores = jnp.einsum(
                "grd,ngd->grn", query_grp, key_grp, preferred_element_type=jnp.float32
            )
            capped = CAP * jnp.tanh(raw_scores / CAP)
            key_pos = first_row + jnp.arange(key_count, dtype=jnp.int32)
            allowed = key_pos[None, None, :] <= row_pos[None, :, None]
            weights = jnp.where(allowed, jnp.exp(capped), 0.0)
            value_grp = value_block.reshape(key_count, KVH, HD)
            weighted = weighted + jnp.einsum(
                "grn,ngd->grd",
                weights.astype(jnp.bfloat16),
                value_grp,
                preferred_element_type=jnp.float32,
            )
            return (row_total + jnp.sum(weights, axis=-1), weighted)

        def add_skip_block(state):
            return state

        return lax.cond(first_row <= last_pos, add_compute_block, add_skip_block, partial_value)

    start_state = (
        jnp.zeros((KVH, q_group * tok_rows), jnp.float32),
        jnp.zeros((KVH, q_group * tok_rows, HD), jnp.float32),
    )
    row_total, weighted = blockwise(
        add_block,
        start_state,
        (
            lax.all_gather(key_rows, "ctx", axis=0, tiled=True),
            lax.all_gather(value_rows, "ctx", axis=0, tiled=True),
        ),
        512,
    )
    inv_total = 1.0 / row_total
    attended_grp = weighted * inv_total[..., None]
    attended_b = from_groups(attended_grp, tok_rows, q_group).astype(jnp.bfloat16)
    branch = jnp.dot(attended_b, full_out, preferred_element_type=jnp.float32)
    inv_post, normed_post = rms_parts(branch)
    middle = resid_in + normed_post * post_factor
    inv_mid, normed_mid = rms_parts(middle)
    hidden_ffn = (normed_mid * pre_ffn_factor).astype(jnp.bfloat16)
    gate_up = fold_rows(
        hidden_ffn, lax.all_gather(gateup_shard, ("ctx", "fsdp"), axis=0, tiled=True)
    )
    gate_lin = gate_up[:, :FF]
    up_lin = gate_up[:, FF:]
    active = gated(gate_lin, up_lin).astype(jnp.bfloat16)
    ffn_branch = fold_rows(active, lax.all_gather(w_down, ("ctx", "fsdp"), axis=0, tiled=True))
    inv_ffn, normed_ffn = rms_parts(ffn_branch)
    output = (middle + normed_ffn * post_ffn_factor).astype(jnp.bfloat16)
    out_cot = out_grad[0].astype(jnp.float32)
    post_ffn_part = jnp.sum(out_cot * normed_ffn, axis=0)
    d_ffn_b = norm_back(out_cot * post_ffn_factor, normed_ffn, inv_ffn).astype(jnp.bfloat16)
    down_total = lax.psum_scatter(
        grad_rows(active, d_ffn_b, 1, lax.axis_size(("ctx", "fsdp")) * w_down.shape[0]),
        ("ctx", "fsdp"),
        scatter_dimension=0,
        tiled=True,
    )
    d_active = contract_cols(d_ffn_b, lax.all_gather(w_down, ("ctx", "fsdp"), axis=0, tiled=True))
    unused_value, gate_pull = jax.vjp(gated, gate_lin, up_lin)
    d_gate, d_up = gate_pull(d_active)
    d_gateup_b = jnp.concatenate([d_gate.astype(jnp.bfloat16), d_up.astype(jnp.bfloat16)], axis=1)
    gateup_folded = lax.psum_scatter(
        grad_rows(
            hidden_ffn,
            d_gateup_b,
            ROW_FOLD,
            lax.axis_size(("ctx", "fsdp")) * (ROW_FOLD * shard_rows),
        ),
        ("ctx", "fsdp"),
        scatter_dimension=0,
        tiled=True,
    )
    gateup_total = gateup_folded.reshape(shard_rows, 2 * FF)
    d_hidden_ffn = contract_cols(
        d_gateup_b, lax.all_gather(gateup_shard, ("ctx", "fsdp"), axis=0, tiled=True)
    )
    pre_ffn_part = jnp.sum(d_hidden_ffn * normed_mid, axis=0)
    d_middle = out_cot + norm_back(d_hidden_ffn * pre_ffn_factor, normed_mid, inv_mid)
    back_qkv, back_out = (
        lax.all_gather(qkv_shard, ("ctx", "fsdp"), axis=0, tiled=True),
        lax.all_gather(w_out, ("ctx", "fsdp"), axis=0, tiled=True),
    )
    post_gain_part = jnp.sum(d_middle * normed_post, axis=0)
    d_branch_b = norm_back(d_middle * post_factor, normed_post, inv_post).astype(jnp.bfloat16)
    w_out_part = contract_rows(attended_b, d_branch_b)
    d_attended = contract_cols(d_branch_b, back_out).astype(jnp.bfloat16)
    d_att_grp = to_groups(d_attended, tok_rows, q_group)
    row_delta = jnp.sum(d_att_grp.astype(jnp.float32) * attended_grp, axis=-1)
    zero_rows = jnp.zeros((tok_rows, width_kv), jnp.float32)
    zero_query = jnp.zeros((KVH, q_group * tok_rows, HD), jnp.float32)
    block_ids = jnp.arange(n_ctx, dtype=jnp.int32)
    all_keys, all_values = (
        lax.all_gather(key_rows, "ctx", axis=0, tiled=True),
        lax.all_gather(value_rows, "ctx", axis=0, tiled=True),
    )

    def returned_step(acc_query, block_item):
        block_index, key_block, value_block = block_item
        first_row = block_index * tok_rows

        def returned_compute_block(acc_in):
            d_query, d_key, d_value = block_grads(
                query_grp,
                row_pos,
                d_att_grp,
                row_delta,
                inv_total,
                key_block,
                value_block,
                first_row,
            )
            return (acc_in + d_query, (d_key, d_value))

        def returned_skip_block(acc_in):
            return (acc_in, (zero_rows, zero_rows))

        return lax.cond(
            first_row <= last_pos, returned_compute_block, returned_skip_block, acc_query
        )

    key_blocks = all_keys.reshape(n_ctx, tok_rows, width_kv)
    value_blocks = all_values.reshape(n_ctx, tok_rows, width_kv)
    d_query_grp, key_terms = lax.scan(
        returned_step, zero_query, (block_ids, key_blocks, value_blocks)
    )
    key_term_rows = key_terms[0].reshape(n_ctx * tok_rows, width_kv)
    value_term_rows = key_terms[1].reshape(n_ctx * tok_rows, width_kv)
    d_keys, d_values = (
        lax.psum_scatter(
            key_term_rows.astype(jnp.bfloat16), "ctx", scatter_dimension=0, tiled=True
        ).astype(jnp.float32),
        lax.psum_scatter(
            value_term_rows.astype(jnp.bfloat16), "ctx", scatter_dimension=0, tiled=True
        ).astype(jnp.float32),
    )
    d_query_flat = from_groups(d_query_grp, tok_rows, q_group).reshape(tok_rows, H, HD) * q_scale
    dq_lin = (
        unrotate(d_query_flat, cos_tab, sine_tab).astype(jnp.bfloat16).reshape(tok_rows, width_q)
    )
    dk_lin = (
        unrotate(d_keys.reshape(tok_rows, KVH, HD), cos_tab, sine_tab)
        .astype(jnp.bfloat16)
        .reshape(tok_rows, width_kv)
    )
    dv_lin = d_values.astype(jnp.bfloat16)
    dqkv_b = jnp.concatenate([dq_lin, dk_lin, dv_lin], axis=1)
    d_hidden = contract_cols(dqkv_b, back_qkv)
    qkv_part = contract_rows(hidden, dqkv_b).reshape(ROW_FOLD * D, width_qkv // ROW_FOLD)
    pre_gain_part = jnp.sum(d_hidden * normed_pre, axis=0)
    token_grad = d_middle + norm_back(d_hidden * pre_factor, normed_pre, inv_pre)
    gain_parts = jnp.stack([pre_gain_part, post_gain_part, pre_ffn_part, post_ffn_part])
    qkv_folded, out_total, gain_totals = (
        lax.psum_scatter(qkv_part, ("ctx", "fsdp"), scatter_dimension=0, tiled=True),
        lax.psum_scatter(w_out_part, ("ctx", "fsdp"), scatter_dimension=0, tiled=True),
        lax.psum_scatter(gain_parts, ("ctx", "fsdp"), scatter_dimension=1, tiled=True),
    )
    qkv_total = qkv_folded.reshape(shard_rows, width_qkv)
    return (
        output[None],
        token_grad.astype(jnp.bfloat16)[None],
        qkv_total[:, :width_q],
        qkv_total[:, width_q : width_q + width_kv],
        qkv_total[:, width_q + width_kv :],
        out_total,
        gateup_total[:, :FF],
        gateup_total[:, FF:],
        down_total,
        gain_totals[0],
        gain_totals[1],
        gain_totals[2],
        gain_totals[3],
    )


def solution(mesh):
    return jax.shard_map(
        on_device,
        mesh=mesh,
        in_specs=(
            P("fsdp", "ctx", None),
            P(("ctx", "fsdp"), None),
            P(("ctx", "fsdp"), None),
            P(("ctx", "fsdp"), None),
            P(("ctx", "fsdp"), None),
            P(("ctx", "fsdp"), None),
            P(("ctx", "fsdp"), None),
            P(("ctx", "fsdp"), None),
            P(("ctx", "fsdp")),
            P(("ctx", "fsdp")),
            P(("ctx", "fsdp")),
            P(("ctx", "fsdp")),
            P("fsdp", "ctx", None),
        ),
        out_specs=(
            P("fsdp", "ctx", None),
            P("fsdp", "ctx", None),
            P(("ctx", "fsdp"), None),
            P(("ctx", "fsdp"), None),
            P(("ctx", "fsdp"), None),
            P(("ctx", "fsdp"), None),
            P(("ctx", "fsdp"), None),
            P(("ctx", "fsdp"), None),
            P(("ctx", "fsdp"), None),
            P(("ctx", "fsdp")),
            P(("ctx", "fsdp")),
            P(("ctx", "fsdp")),
            P(("ctx", "fsdp")),
        ),
        check_vma=False,
    )
```

profile of v0, /device:TPU:1, one launch (start us, length us, event | category | flops | bytes accessed | tf_op | source)
XLA Modules:
  0.0 3979.9 jit_solution(3452549825522971461)
XLA Ops:
  10.0 65.4 %all-gather = bf16[32,72,4]{1,2,0:T(4,128)(2,1)S(1)} all-gather(bf16[1,72,4]{1,2,0:T(4,128)(2,1)S(1)} %maximum_bitcast_fusion), channel_id=1, replica_groups=mesh['ctx'=8,'fsdp'=4] {'ctx','fsdp'}, dimensions={0}, use_global_device_ids=true | all-gather | bytes 19008 | tf_op jit(solution)/shard_map/all_gather | solution.py:163
  76.8 62.2 %all-gather.8.cloned.1.call-done = bf16[2304,4096]{1,0:T(8,128)(2,1)} async-done(((bf16[72,4096]{1,0:T(8,128)(2,1)}), bf16[2304,4096]{1,0:T(8,128)(2,1)}) %all-gather.8.cloned.1.call-update) | async-done | bytes 18874384 | tf_op jit(solution)/shard_map/all_gather | solution.py:164
  157.5 19.4 all-gather.10.cloned.1.call-done
  185.2 22.5 all-gather.12.cloned.1.call-done
  222.5 69.5 %all-gather.14.cloned.1.call-done = bf16[2048,2304]{1,0:T(8,128)(2,1)} async-done(((bf16[64,2304]{1,0:T(8,128)(2,1)}), bf16[2048,2304]{1,0:T(8,128)(2,1)}) %all-gather.14.cloned.1.call-update) | async-done | bytes 9437200 | tf_op jit(solution)/shard_map/all_gather | solution.py:165
  298.3 437.4 %all-gather.16.cloned.1.call-done = bf16[2304,18432]{1,0:T(8,128)(2,1)} async-done(((bf16[72,18432]{1,0:T(8,128)(2,1)}), bf16[2304,18432]{1,0:T(8,128)(2,1)}) %all-gather.16.cloned.1.call-update) | async-done | bytes 84934672 | tf_op jit(solution)/shard_map/all_gather | solution.py:238
  735.6 34.3 fusion.59
  775.5 198.8 %all-gather.18.cloned.1.call-done = bf16[9216,2304]{1,0:T(8,128)(2,1)} async-done(((bf16[288,2304]{1,0:T(8,128)(2,1)}), bf16[9216,2304]{1,0:T(8,128)(2,1)}) %all-gather.18.cloned.1.call-update) | async-done | bytes 42467344 | tf_op jit(solution)/shard_map/all_gather | solution.py:243
  974.3 16.3 multiply_reduce_fusion.4
  993.1 22.9 fusion.28
  1016.0 37.5 multiply_reduce_fusion
  1071.8 47.0 %while.32 = (s32[]{:T(128)}, f32[4,256,256]{2,1,0:T(8,128)S(1)}, bf16[8,128,1024]{2,1,0:T(8,128)(2,1)}, bf16[8,128,1024]{2,1,0:T(8,128)(2,1)}, s32[8]{0:T(128)S(...) while((s32[]{:T(128)}, f32[4,256,256]{2,1,0:T(8,128)S(1)}, ...), condition=%wide.region_16.17_spmd.clone, body=%wide.region_13.16_spmd.clone.sunk | while | flops 407666816 | bytes 19340136 | solution.py:320
  1121.4 68.9 %reduce-scatter.8.cloned.1.call-done = bf16[128,1024]{1,0:T(8,128)(2,1)} async-done(((bf16[1024,1024]{1,0:T(8,128)(2,1)}), bf16[128,1024]{1,0:T(8,128)(2,1)}) %reduce-scatter.8.cloned.1.call-update) | async-done | bytes 262160 | tf_op jit(solution)/shard_map/reduce_scatter | solution.py:326
  1191.9 35.2 reduce-scatter.10.cloned.1.call-done
  1228.1 14.8 fusion.52
  1242.9 42.2 %reshape.345 = f32[9216,1024]{1,0:T(8,128)} reshape(f32[2304,4096]{1,0:T(8,128)} %fusion.52) | data formatting | bytes 75497472 | tf_op jit(solution)/shard_map/reshape | solution.py:345
  1286.7 79.9 %fusion.29 = f32[2304,18432]{1,0:T(8,128)} fusion(bf16[128,9216]{1,0:T(8,128)(2,1)} %get-tuple-element.524, bf16[128,9216]{1,0:T(8,128)(2,1)S(1)} %copy-done.11, f32[128,2304]{1,0:T(8,128)S(1)} %get-tuple-element.514, f32[2304]{0:T(1024)S(1)} %get-tuple-element.465, f32[128]{0:T(128)S(1)} %add_rsqrt_fusion.1), kind=kOutput, calls=%fused_computation.52 | convolution fusion | flops 10881957888 | bytes 175777280 | tf_op jit(solution)/shard_map/dot_general | solution.py:66
  1366.6 180.9 %reshape.347 = f32[9216,4608]{1,0:T(8,128)} reshape(f32[2304,18432]{1,0:T(8,128)} %fusion.29) | data formatting | bytes 339738624 | tf_op jit(solution)/shard_map/reshape | solution.py:83
  1558.5 31.6 fusion.65
  1591.6 14.0 fusion.46
  1605.7 40.6 %all-reduce = f32[4,2304]{1,0:T(4,128)S(1)} all-reduce(f32[4,2304]{1,0:T(4,128)S(1)} %pad_maximum_fusion.8), channel_id=8, replica_groups=mesh['ctx'=8,'fsdp'=4] {'ctx','fsdp'}, use_global_device_ids=true, to_apply=%region_28.29.clone | all-reduce | flops 9216 | bytes 73728
  1652.9 1382.5 %reduce-scatter.16.cloned.1.call-done = f32[288,4608]{1,0:T(8,128)} async-done(((f32[9216,4608]{1,0:T(8,128)}), f32[288,4608]{1,0:T(8,128)}) %reduce-scatter.16.cloned.1.call-update) | async-done | bytes 5308432 | tf_op jit(solution)/shard_map/reduce_scatter | solution.py:259
  3047.9 199.6 %reduce-scatter.14.cloned.1.call-done = f32[64,2304]{1,0:T(8,128)} async-done(((f32[2048,2304]{1,0:T(8,128)}), f32[64,2304]{1,0:T(8,128)}) %reduce-scatter.14.cloned.1.call-update) | async-done | bytes 589840 | tf_op jit(solution)/shard_map/reduce_scatter | solution.py:351
  3247.6 725.1 %reduce-scatter.18.cloned.1.call-done = f32[288,2304]{1,0:T(8,128)} async-done(((f32[9216,2304]{1,0:T(8,128)}), f32[288,2304]{1,0:T(8,128)}) %reduce-scatter.18.cloned.1.call-update) | async-done | bytes 2654224 | tf_op jit(solution)/shard_map/reduce_scatter | solution.py:249
  (350 shorter events, 185.2 us)
Async XLA Ops:
  7.2 69.1 %copy-start.1 = (bf16[1,128,2304]{2,1,0:T(8,128)(2,1)S(1)}, bf16[1,128,2304]{2,1,0:T(8,128)(2,1)}, u32[]{:S(2)}) copy-start(bf16[1,128,2304]{2,1,0:T(8,128)(2,1)} %param.21) | copy-start | bytes 1769476
  7.2 131.8 %all-gather.8.cloned.1.call-start = ((), (), s32[]{:S(2)}) async-start(), calls=%async_computation.6 | async-start | bytes 19464192 | tf_op jit(solution)/shard_map/all_gather | solution.py:164
  9.3 167.6 %all-gather.10.cloned.1.call-start = ((), (), s32[]{:S(2)}) async-start(), calls=%async_computation.7 | async-start | bytes 2359296 | tf_op jit(solution)/shard_map/all_gather | solution.py:224
  76.2 70.5 %copy-start.27 = (f32[2304]{0:T(1024)}, f32[2304]{0:T(1024)S(1)}, u32[]{:S(2)}) copy-start(f32[2304]{0:T(1024)S(1)} %get-tuple-element.467) | copy-start | bytes 27652
  76.4 70.3 %copy-start.39 = (f32[128]{0:T(128)}, f32[128]{0:T(128)S(1)}, u32[]{:S(2)}) copy-start(f32[128]{0:T(128)S(1)} %add_rsqrt_fusion.3) | copy-start | bytes 1540
  76.8 80.3 %copy-start.23 = (f32[128,128]{1,0:T(8,128)}, f32[128,128]{1,0:T(8,128)S(1)}, u32[]{:S(2)}) copy-start(f32[128,128]{1,0:T(8,128)S(1)} %get-tuple-element.545) | copy-start | bytes 196612
  76.8 80.3 %copy-start.25 = (f32[128,128]{1,0:T(8,128)}, f32[128,128]{1,0:T(8,128)S(1)}, u32[]{:S(2)}) copy-start(f32[128,128]{1,0:T(8,128)S(1)} %get-tuple-element.546) | copy-start | bytes 196612
  149.5 58.2 %all-gather.12.cloned.1.call-start = ((), (), s32[]{:S(2)}) async-start(), calls=%async_computation.8 | async-start | bytes 2359296 | tf_op jit(solution)/shard_map/all_gather | solution.py:225
  151.3 140.7 %all-gather.14.cloned.1.call-start = ((), (), s32[]{:S(2)}) async-start(), calls=%async_computation.9 | async-start | bytes 9732096 | tf_op jit(solution)/shard_map/all_gather | solution.py:165
  151.9 583.7 %all-gather.16.cloned.1.call-start = ((), (), s32[]{:S(2)}) async-start(), calls=%async_computation.10 | async-start | bytes 87588864 | tf_op jit(solution)/shard_map/all_gather | solution.py:238
  155.4 818.9 %all-gather.18.cloned.1.call-start = ((), (), s32[]{:S(2)}) async-start(), calls=%async_computation.11 | async-start | bytes 43794432 | tf_op jit(solution)/shard_map/all_gather | solution.py:243
  156.0 1034.4 %reduce-scatter.8.cloned.1.call-start = ((), (), s32[]{:S(2)}) async-start(), calls=%async_computation.12 | async-start | bytes 2359296 | tf_op jit(solution)/shard_map/reduce_scatter | solution.py:326
  218.4 73.6 %copy-start.13 = (bf16[128,4,2,256]{0,3,2,1:T(8,128)(2,1)}, bf16[128,4,2,256]{0,3,2,1:T(8,128)(2,1)S(1)}, u32[]{:S(2)}) copy-start(bf16[128,4,2,256]{0,3,2,1:T(8,128)(2,1)S(1)} %copy.122) | copy-start | bytes 1572868
  775.5 215.1 %copy-start.19 = (bf16[1,128,2304]{2,1,0:T(8,128)(2,1)S(1)}, bf16[1,128,2304]{2,1,0:T(8,128)(2,1)}, u32[]{:S(2)}) copy-start(bf16[1,128,2304]{2,1,0:T(8,128)(2,1)} %param.33) | copy-start | bytes 1769476
  775.5 215.1 %copy-start.35 = (f32[2304]{0:T(1024)S(1)}, f32[2304]{0:T(1024)}, u32[]{:S(2)}) copy-start(f32[2304]{0:T(1024)} %get-tuple-element.464) | copy-start | bytes 27652
  1118.8 108.3 %reduce-scatter.10.cloned.1.call-start = ((), (), s32[]{:S(2)}) async-start(), calls=%async_computation.13 | async-start | bytes 2359296 | tf_op jit(solution)/shard_map/reduce_scatter | solution.py:329
  1119.5 529.8 %reduce-scatter.12.cloned.1.call-start = ((), (), s32[]{:S(2)}) async-start(), calls=%async_computation.14 | async-start | bytes 38928384 | tf_op jit(solution)/shard_map/reduce_scatter | solution.py:350
  1121.4 106.7 %copy-start.2 = (bf16[1,128,2304]{2,1,0:T(8,128)(2,1)S(1)}, bf16[1,128,2304]{2,1,0:T(8,128)(2,1)}, u32[]{:S(2)}) copy-start(bf16[1,128,2304]{2,1,0:T(8,128)(2,1)} %param.21) | copy-start | bytes 1769476
  1121.4 106.7 %copy-start.28 = (f32[2304]{0:T(1024)S(1)}, f32[2304]{0:T(1024)}, u32[]{:S(2)}) copy-start(f32[2304]{0:T(1024)} %copy-done.27) | copy-start | bytes 27652
  1121.4 106.7 %copy-start.40 = (f32[128]{0:T(128)S(1)}, f32[128]{0:T(128)}, u32[]{:S(2)}) copy-start(f32[128]{0:T(128)} %copy-done.39) | copy-start | bytes 1540
  1285.1 1750.3 %reduce-scatter.16.cloned.1.call-start = ((), (), s32[]{:S(2)}) async-start(), calls=%async_computation.16 | async-start | bytes 175177728 | tf_op jit(solution)/shard_map/reduce_scatter | solution.py:259
  1547.6 1700.0 %reduce-scatter.14.cloned.1.call-start = ((), (), s32[]{:S(2)}) async-start(), calls=%async_computation.15 | async-start | bytes 19464192 | tf_op jit(solution)/shard_map/reduce_scatter | solution.py:351
  1556.7 2415.9 %reduce-scatter.18.cloned.1.call-start = ((), (), s32[]{:S(2)}) async-start(), calls=%async_computation.17 | async-start | bytes 87588864 | tf_op jit(solution)/shard_map/reduce_scatter | solution.py:249
  1591.6 55.3 %copy-start.10 = (f32[128,2304]{1,0:T(8,128)S(1)}, f32[128,2304]{1,0:T(8,128)}, u32[]{:S(2)}) copy-start(f32[128,2304]{1,0:T(8,128)} %copy-done.9) | copy-start | bytes 3538948
  (66 other events, 169.8 us)
Sparse Core Ops, SparseCore 0:
  11.5 127.4 all-gather.7
  149.6 27.2 all-gather.9
  179.1 28.5 all-gather.11
  210.4 81.5 all-gather.13
  295.3 440.2 all-gather.15
  738.4 235.8 all-gather.17
  1118.9 71.4 reduce-scatter.7
  1192.6 34.3 reduce-scatter.9
  1285.2 349.8 reduce-scatter.11
  1642.6 1392.7 reduce-scatter.15
  3042.4 205.1 reduce-scatter.13
  3254.4 718.2 reduce-scatter.17
where the time goes:
time: 3990 us; the launch traced here: 3980 us
  waiting for transfers between devices  3220 us (81%)
  local copies, waits for them, and re-layouts  314 us (8%)
  matrix products  289 us (7%)
  blocking collectives  106 us (3%)
    reduce_scatter x1, waiting for transfers between devices, on_device(): lax.psum_scatter(grad_rows(hidden_ffn, d_gateup_b, ROW_FOLD, lax.axis_siz...  1380 us
    reduce_scatter x1, waiting for transfers between devices, on_device(): lax.psum_scatter(grad_rows(active, d_ffn_b, 1, lax.axis_size(('ctx', 'fsd...  725 us
    all_gather x1, waiting for transfers between devices, on_device(): lax.all_gather(gateup_shard, ('ctx', 'fsdp'), axis=0, tiled=True)  437 us
    reduce_scatter x1, waiting for transfers between devices, on_device(): lax.psum_scatter(w_out_part, ('ctx', 'fsdp'), scatter_dimension=0, tiled=...  200 us
    all_gather x1, waiting for transfers between devices, on_device(): lax.all_gather(w_down, ('ctx', 'fsdp'), axis=0, tiled=True)  199 us
    reshape x1, local copies, waits for them, and re-layouts, grad_rows(): return block.reshape(count, right.shape[1] // folding)  181 us
    dot_general x4, matrix products, contract_rows(): lax.dot_general(left, right, (((0,), (0,)), ((), ())), preferred_element_...  134 us
    dot_general x4, matrix products, contract_cols(): lax.dot_general(left, right, (((1,), (1,)), ((), ())), preferred_element_...  82.3 us
  transfers between devices with their start and end apart: 12, of which 11 were waited for; matrix products, arithmetic and copies ran while one was open for 10% of the time, Pallas kernels for 0%

commit v1 on v0

--- a/solution.py
+++ b/solution.py
@@ -1,6 +1,10 @@
+import functools
+
 import jax
 import jax.numpy as jnp
 from jax import lax
+from jax.experimental import pallas as pl
+from jax.experimental.pallas import tpu as pltpu
 from jax.sharding import PartitionSpec as P
 
 D = 2304
@@ -10,20 +14,824 @@
 CAP = 50
 FF = 9216
 
-
 EPSILON = 1e-06
 ROPE_BASE = 10000.0
+
+MESH = pl.DeviceIdType.MESH
+HBM = pl.BlockSpec(memory_space=pl.ANY)
+VMEM = pl.BlockSpec(memory_space=pltpu.VMEM)
+DMA = pltpu.SemaphoreType.DMA
+BF = jnp.bfloat16
+F32 = jnp.float32
+
+
+def rope_tables(positions, width):
+    half_width = width // 2
+    inv_freqs = ROPE_BASE ** (-jnp.arange(half_width, dtype=F32) * 2.0 / width)
+    angles = positions.astype(F32)[:, None] * inv_freqs[None, :]
+    return (jnp.cos(angles), jnp.sin(angles))
+
+
+def rotate(rows, cos_tab, sine_tab):
+    half_width = rows.shape[-1] // 2
+    front, back = rows[..., :half_width], rows[..., half_width:]
+    return jnp.concatenate(
+        [front * cos_tab - back * sine_tab, back * cos_tab + front * sine_tab], axis=-1
+    )
+
+
+def unrotate(rows, cos_tab, sine_tab):
+    half_width = rows.shape[-1] // 2
+    front, back = rows[..., :half_width], rows[..., half_width:]
+    return jnp.concatenate(
+        [front * cos_tab + back * sine_tab, back * cos_tab - front * sine_tab], axis=-1
+    )
+
+
+def rms_parts(values_in):
+    inverse = lax.rsqrt(jnp.mean(values_in * values_in, axis=-1, keepdims=True) + EPSILON)
+    return (inverse, values_in * inverse)
+
+
+def norm_back(grad_normed, normed, inverse):
+    return inverse * (grad_normed - normed * jnp.mean(grad_normed * normed, axis=-1, keepdims=True))
+
+
+def contract_rows(left, right):
+    return lax.dot_general(left, right, (((0,), (0,)), ((), ())), preferred_element_type=F32)
+
+
+def contract_cols(left, right):
+    return lax.dot_general(left, right, (((1,), (1,)), ((), ())), preferred_element_type=F32)
+
+
+def fold_rows(left, right):
+    return jnp.dot(left, right, preferred_element_type=F32)
+
+
+def gated(gate_in, up_in):
+    return jax.nn.gelu(gate_in, approximate=True) * up_in
+
+
+NZ = 4
+RING = 2 * NZ
+
+
+def my_place():
+    c, f = lax.axis_index("ctx"), lax.axis_index("fsdp")
+    return c // 2, c % 2, f // 2, f % 2
+
+
+def ring_index(y, z):
+    return z + y * (RING - 1 - 2 * z)
+
+
+def ring_yz(q):
+    y = q // NZ
+    return y, q + y * (RING - 1 - 2 * q)
+
+
+def device(z, core, y, x):
+    return (2 * z + core, 2 * y + x)
+
+
+def ring_device(q, core, x):
+    y, z = ring_yz(q)
+    return device(z, core, y, x)
+
+
+def remote(src, dst, send_sem, recv_sem, where):
+    return pltpu.make_async_remote_copy(
+        src_ref=src,
+        dst_ref=dst,
+        send_sem=send_sem,
+        recv_sem=recv_sem,
+        device_id=where,
+        device_id_type=MESH,
+    )
+
+
+def greet(places):
+    barrier = pltpu.get_barrier_semaphore()
+    for place in places:
+        pl.semaphore_signal(barrier, inc=1, device_id=place, device_id_type=MESH)
+    pl.semaphore_wait(barrier, len(places))
+
+
+def params(collective_id, vmem_mib=56):
+    return pltpu.CompilerParams(
+        collective_id=collective_id,
+        has_side_effects=True,
+        vmem_limit_bytes=vmem_mib * 2**20,
+    )
+
+
+SUB = 4
+
+
+def ring_parts(direction, step, half_step):
+    if step != half_step:
+        return list(range(SUB))
+    half = SUB // 2
+    return list(range(half)) if direction == 0 else list(range(half, SUB))
+
+
+def gather_kernel(paired, x_ref, *refs):
+    if paired:
+        ring_ref, seq_ref, loc_sem, ss, rs, sib_ss, sib_rs = refs
+    else:
+        ring_ref, loc_sem, ss, rs = refs
+    z, core, y, x = my_place()
+    p = ring_index(y, z)
+    right, left = (p + 1) % RING, (p + RING - 1) % RING
+    sibling = device(z, 1 - core, y, x)
+    piece = x_ref.shape[0] // SUB
+    greet(
+        [ring_device(right, core, x), ring_device(left, core, x)] + ([sibling] if paired else [])
+    )
+    local = pltpu.make_async_copy(x_ref, ring_ref.at[p], loc_sem.at[RING])
+    local.start()
+
+    def copy(direction, step, k):
+        q = (p + (RING - step if direction == 0 else step)) % RING
+        rows = pl.ds(k * piece, piece)
+        src = x_ref.at[rows] if step == 0 else ring_ref.at[q, rows]
+        return remote(
+            src,
+            ring_ref.at[q, rows],
+            ss.at[direction, step, k],
+            rs.at[direction, step, k],
+            ring_device(right if direction == 0 else left, core, x),
+        )
+
+    def place_block(q, act):
+        if not paired:
+            return
+        yq, zq = ring_yz(q)
+
+        @pl.when(yq == core)
+        def _():
+            act(pltpu.make_async_copy(ring_ref.at[q], seq_ref.at[2 * zq + core], loc_sem.at[q]))
+
+        @pl.when(yq != core)
+        def _():
+            act(remote(ring_ref.at[q], seq_ref.at[2 * zq + core], sib_ss.at[zq], sib_rs.at[zq], sibling))
+
+    pending = []
+    for step in range(4):
+        for k in range(SUB):
+            for direction in (0, 1):
+                if k not in ring_parts(direction, step, 3):
+                    continue
+                if step > 0:
+                    copy(direction, step - 1, k).wait_recv()
+                c = copy(direction, step, k)
+                c.start()
+                pending.append(c)
+        if step == 0:
+            local.wait()
+            place_block(p, lambda c: c.start())
+        elif step < 3:
+            for direction in (0, 1):
+                q = (p + (RING - step if direction == 0 else step)) % RING
+                place_block(q, lambda c: c.start())
+    for direction in (0, 1):
+        for k in range(SUB):
+            if k not in ring_parts(direction, 3, 3):
+                copy(direction, 2, k).wait_recv()
+    for direction in (0, 1):
+        place_block((p + (RING - 3 if direction == 0 else 3)) % RING, lambda c: c.start())
+    for direction in (0, 1):
+        for k in ring_parts(direction, 3, 3):
+            copy(direction, 3, k).wait_recv()
+    place_block((p + 4) % RING, lambda c: c.start())
+    for c in pending:
+        c.wait_send()
+
+    def finish(c):
+        if c.is_remote:
+            c.wait_send()
+        else:
+            c.wait()
+
+    if paired:
+        for q in range(RING):
+            place_block((p + q) % RING, finish)
+        for zq in range(NZ):
+            remote(ring_ref.at[zq], seq_ref.at[2 * zq + 1 - core], sib_ss.at[zq], sib_rs.at[zq], sibling).wait_recv()
+
+
+def ring_gather(block, collective_id, paired):
+    rows, width = block.shape
+    whole = jax.ShapeDtypeStruct((RING, rows, width), block.dtype)
+    sems = [DMA((RING + 1,)), DMA((2, 4, SUB)), DMA((2, 4, SUB))]
+    out = pl.pallas_call(
+        functools.partial(gather_kernel, paired),
+        out_shape=[whole, whole] if paired else [whole],
+        in_specs=[HBM],
+        out_specs=[HBM, HBM] if paired else [HBM],
+        scratch_shapes=sems + ([DMA((NZ,)), DMA((NZ,))] if paired else []),
+        compiler_params=params(collective_id),
+    )(block)
+    return out[-1].reshape(RING * rows, width)
+
+
+def scatter_kernel(paired, part_ref, o_ref, *refs):
+    if paired:
+        mine_ref, buf, ss, rs, sib_ss, sib_rs, loc_sem = refs
+    else:
+        buf, ss, rs = refs
+        mine_ref = part_ref
+    z, core, y, x = my_place()
+    p = ring_index(y, z)
+    right, left = (p + 1) % RING, (p + RING - 1) % RING
+    sibling = device(z, 1 - core, y, x)
+    piece = o_ref.shape[0] // SUB
+    greet(
+        [ring_device(right, core, x), ring_device(left, core, x)] + ([sibling] if paired else [])
+    )
+    if paired:
+        swaps, copies = [], []
+        for zq in range(NZ):
+            q = ring_index(core, zq)
+            swaps.append(remote(part_ref.at[2 * zq + 1 - core], mine_ref.at[q], sib_ss.at[zq], sib_rs.at[zq], sibling))
+            swaps[-1].start()
+            copies.append(pltpu.make_async_copy(part_ref.at[2 * zq + core], mine_ref.at[q], loc_sem.at[zq]))
+            copies[-1].start()
+        for c in copies:
+            c.wait()
+        for zq in range(NZ):
+            q = ring_index(1 - core, zq)
+            remote(part_ref.at[zq], mine_ref.at[q], sib_ss.at[zq], sib_rs.at[zq], sibling).wait_recv()
+        for c in swaps:
+            c.wait_send()
+
+    def copy(direction, step, k, src):
+        rows = pl.ds(k * piece, piece)
+        return remote(
+            src,
+            buf.at[direction, step, rows],
+            ss.at[direction, step, k],
+            rs.at[direction, step, k],
+            ring_device(right if direction == 0 else left, core, x),
+        )
+
+    pending = []
+    for step in range(4):
+        for k in range(SUB):
+            rows = pl.ds(k * piece, piece)
+            for direction in (0, 1):
+                if k not in ring_parts(direction, step, 0):
+                    continue
+                far = 4 - step
+                q = (p + (far if direction == 0 else RING - far)) % RING
+                src = mine_ref.at[q, rows]
+                if step > 0 and k in ring_parts(direction, step - 1, 0):
+                    src = buf.at[direction, step - 1, rows]
+                    copy(direction, step - 1, k, src).wait_recv()
+                    total = src[...].astype(F32) + mine_ref[q, rows].astype(F32)
+                    src[...] = total.astype(BF)
+                c = copy(direction, step, k, src)
+                c.start()
+                pending.append(c)
+    for k in range(SUB):
+        rows = pl.ds(k * piece, piece)
+        total = mine_ref[p, rows].astype(F32)
+        for direction in (0, 1):
+            src = buf.at[direction, 3, rows]
+            copy(direction, 3, k, src).wait_recv()
+            total = total + src[...].astype(F32)
+        o_ref[rows] = total
+    for c in pending:
+        c.wait_send()
+
+
+def ring_scatter(part, collective_id, paired):
+    rows, width = part.shape[0] // RING, part.shape[1]
+    blocks = (RING, rows, width)
+    sems = [DMA((2, 4, SUB)), DMA((2, 4, SUB))]
+    return pl.pallas_call(
+        functools.partial(scatter_kernel, paired),
+        out_shape=jax.ShapeDtypeStruct((rows, width), F32),
+        in_specs=[VMEM],
+        out_specs=VMEM,
+        scratch_shapes=([pltpu.VMEM(blocks, BF)] if paired else [])
+        + [pltpu.VMEM((2, 4, rows, width), BF)]
+        + sems
+        + ([DMA((NZ,)), DMA((NZ,)), DMA((NZ,))] if paired else []),
+        compiler_params=params(collective_id),
+    )(part.astype(BF).reshape(blocks))
+
+
+UNITS = FF // RING
+WIDTHS = (UNITS, UNITS, HD, HD, HD)
+STARTS = (0, UNITS, 2 * UNITS, 2 * UNITS + HD, 2 * UNITS + 2 * HD)
+WIDE = 2 * UNITS + 3 * HD
+
+
+def member_place(t, core, x):
+    return device(t // 2, core, t % 2, x)
+
+
+def column_start(which, t):
+    if which < 2:
+        return pl.multiple_of(t * UNITS, 128)
+    return pl.multiple_of((t if which == 2 else t // 2) * HD, 128)
+
+
+def weights_in_kernel(gate, up, query, key, value, down, out, gains, w_ref, d_ref, o_ref, g_ref,
+                      loc, s1, r1, s2, r2, s3, r3, s4, r4, s5, r5):
+    z, core, y, x = my_place()
+    t = 2 * z + y
+    sibling, across = device(z, 1 - core, y, x), device(z, core, y, 1 - x)
+
+    def slot(tq, corq, xq):
+        return (2 * (tq // 2) + corq) * 4 + 2 * (tq % 2) + xq
+
+    me = slot(t, core, x)
+    others = [(t + j) % RING for j in range(1, RING)]
+    plane = []
+    for dc in (0, 1):
+        for dy in (0, 1):
+            for dx in (0, 1):
+                if (dc, dy, dx) != (0, 0, 0):
+                    plane.append((dc, dy, dx))
+    places = [member_place(tq, core, x) for tq in others] + [
+        device(z, (core + dc) % 2, (y + dy) % 2, (x + dx) % 2)
+        for dc, dy, dx in plane
+        if (dc, dx) != (0, 0)
+    ]
+    greet(places)
+    sources = (gate, up, query, key, value)
+
+    def first(tq, a, wait=False):
+        if a == 5:
+            src, dst = gains, g_ref.at[slot(tq, core, x) if wait else me]
+        else:
+            src = sources[a].at[:, pl.ds(column_start(a, tq), WIDTHS[a])]
+            dst = w_ref.at[slot(tq, core, x) if wait else me, :, pl.ds(STARTS[a], WIDTHS[a])]
+        i = tq if wait else t
+        return remote(src, dst, s1.at[tq, a], r1.at[i, a], member_place(tq, core, x))
+
+    pending = []
+    locals_ = [pltpu.make_async_copy(gains, g_ref.at[me], loc.at[5])]
+    for a in range(5):
+        locals_.append(
+            pltpu.make_async_copy(
+                sources[a].at[:, pl.ds(column_start(a, t), WIDTHS[a])],
+                w_ref.at[me, :, pl.ds(STARTS[a], WIDTHS[a])],
+                loc.at[a],
+            )
+        )
+    for c in locals_:
+        c.start()
+    pair = ((down, d_ref), (out, o_ref))
+    mine = 2 * y + x
+    for xq in (0, 1):
+        to_self = (x == core) & (y == core) & (xq == x)
+        for a, (src, dst) in enumerate(pair):
+            @pl.when(to_self)
+            def _():
+                pltpu.make_async_copy(src, dst.at[mine], s4.at[xq, a]).start()
+
+            @pl.when(jnp.logical_not(to_self))
+            def _():
+                remote(src, dst.at[mine], s4.at[xq, a], r4.at[y, a], device(z, x, core, xq)).start()
+    for a in (5, 2, 3, 4, 0, 1):
+        for tq in others:
+            c = first(tq, a)
+            c.start()
+            pending.append(c)
+
+    def second(tq, wait=False):
+        i = slot(tq, core, 1 - x if wait else x)
+        return [
+            remote(w_ref.at[i], w_ref.at[i], s2.at[tq, 0], r2.at[tq, 0], across),
+            remote(g_ref.at[i], g_ref.at[i], s2.at[tq, 1], r2.at[tq, 1], across),
+        ]
+
+    def third(tq, flip, wait=False):
+        i = slot(tq, 1 - core if wait else core, 1 - x if flip else x)
+        return [
+            remote(w_ref.at[i], w_ref.at[i], s3.at[tq, flip, 0], r3.at[tq, flip, 0], sibling),
+            remote(g_ref.at[i], g_ref.at[i], s3.at[tq, flip, 1], r3.at[tq, flip, 1], sibling),
+        ]
+
+    for yq in (0, 1):
+        from_self = (core == y) & (yq == y) & (core == x)
+        for a, (src, dst) in enumerate(pair):
+            @pl.when(from_self)
+            def _():
+                pltpu.make_async_copy(src, dst.at[mine], s4.at[x, a]).wait()
+
+            @pl.when(jnp.logical_not(from_self))
+            def _():
+                remote(src, dst.at[2 * yq + core], s4.at[0, a], r4.at[yq, a], sibling).wait_recv()
+
+            c = remote(dst.at[2 * yq + core], dst.at[2 * yq + core], s5.at[yq, a], r5.at[yq, a], sibling)
+            c.start()
+            pending.append(c)
+    for c in locals_:
+        c.wait()
+    for tq in [t] + others:
+        if tq is not t:
+            for a in range(6):
+                first(tq, a, True).wait_recv()
+        for c in second(tq) + third(tq, 0):
+            c.start()
+            pending.append(c)
+    for tq in [t] + others:
+        for c in second(tq, True):
+            c.wait_recv()
+        for c in third(tq, 1):
+            c.start()
+            pending.append(c)
+    for tq in [t] + others:
+        for flip in (0, 1):
+            for c in third(tq, flip, True):
+                c.wait_recv()
+    for yq in (0, 1):
+        for a, (src, dst) in enumerate(pair):
+            remote(src, dst.at[2 * yq + 1 - core], s5.at[yq, a], r5.at[yq, a], sibling).wait_recv()
+    for c in pending:
+        c.wait_send()
+    for xq in (0, 1):
+        to_self = (x == core) & (y == core) & (xq == x)
+        for a, (src, dst) in enumerate(pair):
+            @pl.when(jnp.logical_not(to_self))
+            def _():
+                remote(src, dst.at[mine], s4.at[xq, a], r4.at[y, a], device(z, x, core, xq)).wait_send()
+
+
+def weights_in(gate, up, query, key, value, down, out, gains, collective_id):
+    n = 4 * RING
+    shapes = [
+        jax.ShapeDtypeStruct((n, gate.shape[0], WIDE), BF),
+        jax.ShapeDtypeStruct((4,) + down.shape, BF),
+        jax.ShapeDtypeStruct((4,) + out.shape, BF),
+        jax.ShapeDtypeStruct((n,) + gains.shape, gains.dtype),
+    ]
+    return pl.pallas_call(
+        weights_in_kernel,
+        out_shape=shapes,
+        in_specs=[HBM] * 8,
+        out_specs=[HBM] * 4,
+        scratch_shapes=[
+            DMA((6,)),
+            DMA((RING, 6)), DMA((RING, 6)),
+            DMA((RING, 2)), DMA((RING, 2)),
+            DMA((RING, 2, 2)), DMA((RING, 2, 2)),
+            DMA((2, 2)), DMA((2, 2)),
+            DMA((2, 2)), DMA((2, 2)),
+        ],
+        compiler_params=params(collective_id, 16),
+    )(gate, up, query, key, value, down, out, gains)
+
+
+def add_into(dst, index, src, other):
+    dst[index] = (dst[index].astype(F32) + src[other].astype(F32)).astype(BF)
+
+
+def weights_out_kernel(gu_in, qkv_in, down_in, out_in, gain_in,
+                       gate_o, up_o, query_o, key_o, value_o, down_o, out_o, gain_o,
+                       a_buf, b_buf, c_buf, acc, da, db, dacc, dd, oa, ob, oacc, od, ga, gsum,
+                       loc, sa, ra, sb, rb, sc, rc, sx, rx, sg, rg):
+    z, core, y, x = my_place()
+    t = 2 * z + y
+    sibling, across = device(z, 1 - core, y, x), device(z, core, y, 1 - x)
+    diagonal = device(z, 1 - core, 1 - y, x)
+    others = [(t + j) % RING for j in range(1, RING)]
+    greet([member_place(tq, core, x) for tq in others] + [sibling, across, diagonal])
+
+    def slot(tq, corq, xq):
+        return (2 * (tq // 2) + corq) * 4 + 2 * (tq % 2) + xq
+
+    def load(tq, xq):
+        i = slot(tq, core, xq)
+        return [
+            pltpu.make_async_copy(gu_in.at[i], acc.at[xq, tq, :, pl.ds(0, 2 * UNITS)], loc.at[xq, tq, 0]),
+            pltpu.make_async_copy(qkv_in.at[i], acc.at[xq, tq, :, pl.ds(2 * UNITS, 3 * HD)], loc.at[xq, tq, 1]),
+        ]
+
+    def to_sibling(tq, xq):
+        i = slot(tq, 1 - core, xq)
+        return [
+            remote(gu_in.at[i], a_buf.at[xq, tq, :, pl.ds(0, 2 * UNITS)], sa.at[xq, tq, 0], ra.at[xq, tq, 0], sibling),
+            remote(qkv_in.at[i], a_buf.at[xq, tq, :, pl.ds(2 * UNITS, 3 * HD)], sa.at[xq, tq, 1], ra.at[xq, tq, 1], sibling),
+        ]
+
+    def to_across(tq):
+        return remote(acc.at[1 - x, tq], b_buf.at[tq], sb.at[tq], rb.at[tq], across)
+
+    def to_member(tq, wait=False):
+        return remote(acc.at[x, tq], c_buf.at[tq if wait else t], sc.at[tq], rc.at[tq if wait else t], member_place(tq, core, x))
+
+    def each(body):
+        lax.fori_loop(0, RING, lambda j, carry: (body((t + 1 + j) % RING, j), carry)[1], 0)
+
+    small = ((down_in, da, db, dacc, dd, down_o), (out_in, oa, ob, oacc, od, out_o))
+
+    def small_a(a, xo):
+        src, buf = small[a][0], small[a][1]
+        return remote(src.at[2 * (1 - core) + xo], buf.at[xo], sx.at[a, xo], rx.at[a, xo], sibling)
+
+    def small_b(a):
+        return remote(small[a][3].at[1 - x], small[a][2], sx.at[a, 2], rx.at[a, 2], across)
+
+    def small_c(a):
+        return remote(small[a][3].at[x], small[a][4], sx.at[a, 3], rx.at[a, 3], diagonal)
+
+    def small_load(a, xo):
+        return pltpu.make_async_copy(small[a][0].at[2 * core + xo], small[a][3].at[xo], loc.at[a, xo, 2])
+
+    def gain_a():
+        return remote(gain_in, ga.at[RING], sg.at[RING], rg.at[RING], sibling)
+
+    def gain_b():
+        return remote(gsum.at[0], ga.at[RING + 1], sg.at[RING + 1], rg.at[RING + 1], across)
+
+    def gain_c(tq, wait=False):
+        return remote(gsum.at[1], ga.at[tq if wait else t], sg.at[tq], rg.at[tq if wait else t], member_place(tq, core, x))
+
+    def start_a(xq):
+        def body(tq, j):
+            for c in load(tq, xq) + to_sibling(tq, xq):
+                c.start()
+
+        each(body)
+
+    start_a(1 - x)
+    gain_a().start()
+    for a in (0, 1):
+        for xo in (0, 1):
+            small_a(a, xo).start()
+            small_load(a, xo).start()
+    start_a(x)
+
+    def sum_a(xq, tq):
+        for c in load(tq, xq):
+            c.wait()
+        for c in to_sibling(tq, xq):
+            c.wait_recv()
+        acc[xq, tq] = (acc[xq, tq].astype(F32) + a_buf[xq, tq].astype(F32)).astype(BF)
+
+    def step_one(tq, j):
+        sum_a(1 - x, tq)
+        to_across(tq).start()
+
+    each(step_one)
+    gain_a().wait_recv()
+    gsum[0] = gain_in[...] + ga[RING]
+    gain_b().start()
+    for a in (0, 1):
+        buf, total = small[a][1], small[a][3]
+        for xo in (0, 1):
+            small_load(a, xo).wait()
+            small_a(a, xo).wait_recv()
+            total[xo] = (total[xo].astype(F32) + buf[xo].astype(F32)).astype(BF)
+        small_b(a).start()
+    each(lambda tq, j: sum_a(x, tq))
+    gain_b().wait_recv()
+    gsum[1] = gsum[0] + ga[RING + 1]
+    for tq in others:
+        gain_c(tq).start()
+
+    def step_two(tq, j):
+        to_across(tq).wait_recv()
+        acc[x, tq] = (acc[x, tq].astype(F32) + b_buf[tq].astype(F32)).astype(BF)
+
+        @pl.when(j < RING - 1)
+        def _():
+            to_member(tq).start()
+
+    each(step_two)
+    for a in (0, 1):
+        other, total = small[a][2:4]
+        small_b(a).wait_recv()
+        total[x] = (total[x].astype(F32) + other[...].astype(F32)).astype(BF)
+        for xo in (0, 1):
+            small_a(a, xo).wait_send()
+
+    @pl.when(core == y)
+    def _():
+        for a in (0, 1):
+            small[a][5][...] = small[a][3][x].astype(F32)
+
+    @pl.when(core != y)
+    def _():
+        for a in (0, 1):
+            small_c(a).start()
+        for a in (0, 1):
+            small_c(a).wait_recv()
+            small[a][5][...] = small[a][4][...].astype(F32)
+        for a in (0, 1):
+            small_c(a).wait_send()
+
+    total = gsum[1]
+    for tq in others:
+        gain_c(tq, True).wait_recv()
+        total = total + ga[tq]
+    gain_o[...] = total
+    c_buf[t] = acc[x, t]
+    for tq in others:
+        to_member(tq, True).wait_recv()
+    for tq in range(RING):
+        units = pl.ds(tq * UNITS, UNITS)
+        gate_o[:, units] = c_buf[tq, :, pl.ds(0, UNITS)].astype(F32)
+        up_o[:, units] = c_buf[tq, :, pl.ds(UNITS, UNITS)].astype(F32)
+        query_o[:, pl.ds(tq * HD, HD)] = c_buf[tq, :, pl.ds(STARTS[2], HD)].astype(F32)
+    for g in range(KVH):
+        for start, result in ((STARTS[3], key_o), (STARTS[4], value_o)):
+            columns = pl.ds(start, HD)
+            result[:, pl.ds(g * HD, HD)] = c_buf[2 * g, :, columns].astype(F32) + c_buf[2 * g + 1, :, columns].astype(F32)
+
+    def drain(tq, j):
+        for xq in (0, 1):
+            for c in to_sibling(tq, xq):
+                c.wait_send()
+        to_across(tq).wait_send()
+
+        @pl.when(j < RING - 1)
+        def _():
+            to_member(tq).wait_send()
+
+    each(drain)
+    gain_a().wait_send()
+    gain_b().wait_send()
+    for tq in others:
+        gain_c(tq).wait_send()
+    for a in (0, 1):
+        small_b(a).wait_send()
+
+
+def weights_out(gu, qkv, down, out, gains, collective_id):
+    n = 4 * RING
+    rows, width = gu.shape[0] // n, gains.shape[1]
+    gu, qkv = gu.reshape(n, rows, 2 * UNITS), qkv.reshape(n, rows, 3 * HD)
+    down, out = down.reshape(4, -1, width), out.reshape(4, -1, width)
+    down_rows, out_rows = down.shape[1], out.shape[1]
+    wide = (RING, rows, WIDE)
+
+    def full(*shape):
+        return jax.ShapeDtypeStruct(shape, F32)
+
+    return pl.pallas_call(
+        weights_out_kernel,
+        out_shape=[
+            full(rows, FF), full(rows, FF), full(rows, H * HD), full(rows, KVH * HD), full(rows, KVH * HD),
+            full(down_rows, width), full(out_rows, width), full(*gains.shape),
+        ],
+        in_specs=[HBM] * 4 + [VMEM],
+        out_specs=[VMEM] * 8,
+        scratch_shapes=[
+            pltpu.VMEM((2,) + wide, BF), pltpu.VMEM(wide, BF), pltpu.VMEM(wide, BF), pltpu.VMEM((2,) + wide, BF),
+            pltpu.VMEM((2, down_rows, width), BF), pltpu.VMEM((down_rows, width), BF), pltpu.VMEM((2, down_rows, width), BF), pltpu.VMEM((down_rows, width), BF),
+            pltpu.VMEM((2, out_rows, width), BF), pltpu.VMEM((out_rows, width), BF), pltpu.VMEM((2, out_rows, width), BF), pltpu.VMEM((out_rows, width), BF),
+            pltpu.VMEM((RING + 2,) + gains.shape, F32), pltpu.VMEM((2,) + gains.shape, F32),
+            DMA((2, RING, 3)),
+            DMA((2, RING, 2)), DMA((2, RING, 2)),
+            DMA((RING,)), DMA((RING,)),
+            DMA((RING,)), DMA((RING,)),
+            DMA((2, 4)), DMA((2, 4)),
+            DMA((RING + 2,)), DMA((RING + 2,)),
+        ],
+        compiler_params=params(collective_id),
+    )(gu, qkv, down, out, gains)
+
+
+def attend(queries, keys, values, positions):
+    raw = contract_cols(queries, keys)
+    capped = CAP * jnp.tanh(raw / CAP)
+    allowed = positions[None, :] <= positions[:, None]
+    weights = jnp.where(allowed, jnp.exp(capped), 0.0)
+    inv_total = 1.0 / jnp.sum(weights, axis=-1, keepdims=True)
+    attended = fold_rows(weights.astype(BF), values) * inv_total
+    return attended, inv_total
+
+
+def attend_back(queries, keys, values, positions, attended, inv_total, d_attended):
+    raw = contract_cols(queries, keys)
+    capped = CAP * jnp.tanh(raw / CAP)
+    allowed = positions[None, :] <= positions[:, None]
+    weights = jnp.where(allowed, jnp.exp(capped), 0.0)
+    delta = jnp.sum(d_attended.astype(F32) * attended, axis=-1, keepdims=True)
+    d_probs = contract_cols(d_attended, values)
+    slope = 1.0 - capped / CAP * (capped / CAP)
+    d_raw = (weights * inv_total * (d_probs - delta) * slope).astype(BF)
+    d_query = fold_rows(d_raw, keys)
+    d_key = contract_rows(d_raw, queries)
+    weights_b = weights.astype(BF)
+    d_scaled = d_attended.astype(F32) * inv_total
+    scaled_high = d_scaled.astype(BF)
+    scaled_rest = (d_scaled - scaled_high.astype(F32)).astype(BF)
+    d_value = contract_rows(weights_b, scaled_high) + contract_rows(weights_b, scaled_rest)
+    return d_query, d_key, d_value
+
+
+def on_ring(
+    tokens, w_query, w_key, w_value, w_out, w_gate, w_up, w_down,
+    pre_gain, post_gain, pre_ffn_gain, post_ffn_gain, out_grad,
+):
+    ids = iter(range(32))
+    n_shards = 4 * RING
+    length = RING * tokens.shape[1]
+    shard_gain = pre_gain.shape[0]
+    gains = jnp.stack([pre_gain, post_gain, pre_ffn_gain, post_ffn_gain]).astype(F32)
+    gains = jnp.pad(gains, ((0, 4), (0, 128 - shard_gain)))
+    w_in, down_in, out_in, gains_in = weights_in(
+        w_gate, w_up, w_query, w_key, w_value, w_down, w_out, gains, next(ids)
+    )
+    w_in = w_in.reshape(-1, WIDE)
+    w_gu, w_qkv = w_in[:, : 2 * UNITS], w_in[:, 2 * UNITS :]
+    w_dn = down_in.reshape(UNITS, D)
+    w_ot = out_in.reshape(HD, D)
+    factors = 1.0 + jnp.transpose(gains_in[:, :4, :shard_gain], (1, 0, 2)).reshape(4, D)
+    pre_factor, post_factor, pre_ffn_factor, post_ffn_factor = (factors[i] for i in range(4))
+    positions = jnp.arange(length, dtype=jnp.int32)
+    cos_tab, sine_tab = rope_tables(positions, HD)
+    q_scale = HD ** (-0.5)
+
+    resid_in = tokens[0].astype(F32)
+    inv_pre, normed_pre = rms_parts(resid_in)
+    sequence = ring_gather(tokens[0], next(ids), True).astype(F32)
+    hidden = (rms_parts(sequence)[1] * pre_factor).astype(BF)
+    projected = fold_rows(hidden, w_qkv)
+    queries = (rotate(projected[:, :HD], cos_tab, sine_tab) * q_scale).astype(BF)
+    keys = rotate(projected[:, HD : 2 * HD], cos_tab, sine_tab).astype(BF)
+    values = projected[:, 2 * HD :].astype(BF)
+    attended, inv_total = attend(queries, keys, values, positions)
+    attended_b = attended.astype(BF)
+    branch = ring_scatter(fold_rows(attended_b, w_ot), next(ids), True)
+    inv_post, normed_post = rms_parts(branch)
+    middle = resid_in + normed_post * post_factor
+    inv_mid, normed_mid = rms_parts(middle)
+    hidden_ffn = ring_gather((normed_mid * pre_ffn_factor).astype(BF), next(ids), False)
+    gate_up = fold_rows(hidden_ffn, w_gu)
+    gate_lin, up_lin = gate_up[:, :UNITS], gate_up[:, UNITS:]
+    active = gated(gate_lin, up_lin).astype(BF)
+    ffn_branch = ring_scatter(fold_rows(active, w_dn), next(ids), False)
+    inv_ffn, normed_ffn = rms_parts(ffn_branch)
+    output = (middle + normed_ffn * post_ffn_factor).astype(BF)
+
+    out_cot = out_grad[0].astype(F32)
+    post_ffn_part = jnp.sum(out_cot * normed_ffn, axis=0)
+    d_ffn = norm_back(out_cot * post_ffn_factor, normed_ffn, inv_ffn).astype(BF)
+    d_ffn = ring_gather(d_ffn, next(ids), False)
+    down_part = contract_rows(active, d_ffn)
+    d_active = contract_cols(d_ffn, w_dn)
+    unused_value, gate_pull = jax.vjp(gated, gate_lin, up_lin)
+    d_gate, d_up = gate_pull(d_active)
+    d_gu = jnp.concatenate([d_gate.astype(BF), d_up.astype(BF)], axis=1)
+    d_hidden_ffn = ring_scatter(contract_cols(d_gu, w_gu), next(ids), False)
+    gu_part = contract_rows(hidden_ffn, d_gu)
+    pre_ffn_part = jnp.sum(d_hidden_ffn * normed_mid, axis=0)
+    d_middle = out_cot + norm_back(d_hidden_ffn * pre_ffn_factor, normed_mid, inv_mid)
+    post_part = jnp.sum(d_middle * normed_post, axis=0)
+    d_branch = norm_back(d_middle * post_factor, normed_post, inv_post).astype(BF)
+    d_branch = ring_gather(d_branch, next(ids), True)
+    out_part = contract_rows(attended_b, d_branch)
+    d_attended = contract_cols(d_branch, w_ot).astype(BF)
+    d_query, d_key, d_value = attend_back(
+        queries, keys, values, positions, attended, inv_total, d_attended
+    )
+    d_qkv = jnp.concatenate(
+        [
+            unrotate(d_query * q_scale, cos_tab, sine_tab).astype(BF),
+            unrotate(d_key, cos_tab, sine_tab).astype(BF),
+            d_value.astype(BF),
+        ],
+        axis=1,
+    )
+    d_hidden = ring_scatter(contract_cols(d_qkv, w_qkv), next(ids), True)
+    qkv_part = contract_rows(hidden, d_qkv)
+    pre_part = jnp.sum(d_hidden * normed_pre, axis=0)
+    token_grad = d_middle + norm_back(d_hidden * pre_factor, normed_pre, inv_pre)
+    gain_parts = jnp.pad(jnp.stack([pre_part, post_part, pre_ffn_part, post_ffn_part]), ((0, 4), (0, 0)))
+    results = weights_out(
+        gu_part.astype(BF), qkv_part.astype(BF), down_part.astype(BF), out_part.astype(BF),
+        gain_parts, next(ids),
+    )
+    gate_g, up_g, query_g, key_g, value_g, down_g, out_g, gain_g = results
+    mine = lax.axis_index("ctx") * 4 + lax.axis_index("fsdp")
+    gain_g = lax.dynamic_slice(gain_g, (0, mine * shard_gain), (4, shard_gain))
+    return (
+        output[None], token_grad.astype(BF)[None],
+        query_g, key_g, value_g, out_g, gate_g, up_g, down_g,
+        gain_g[0], gain_g[1], gain_g[2], gain_g[3],
+    )
+
+
 ROW_FOLD = 4
 
 
-def rope_tables(positions, width):
+def head_tables(positions, width):
     half_width = width // 2
     inv_freqs = ROPE_BASE ** (-jnp.arange(half_width, dtype=jnp.float32) * 2.0 / width)
     angles = positions.astype(jnp.float32)[:, None] * inv_freqs[None, :]
     return (jnp.cos(angles)[:, None, :], jnp.sin(angles)[:, None, :])
 
 
-def rotate(heads_in, cos_tab, sine_tab):
+def rotate_heads(heads_in, cos_tab, sine_tab):
     half_width = heads_in.shape[-1] // 2
     front_half = heads_in[..., :half_width]
     back_half = heads_in[..., half_width:]
@@ -33,7 +841,7 @@
     )
 
 
-def unrotate(grad_in, cos_tab, sine_tab):
+def unrotate_heads(grad_in, cos_tab, sine_tab):
     half_width = grad_in.shape[-1] // 2
     front_half = grad_in[..., :half_width]
     back_half = grad_in[..., half_width:]
@@ -43,15 +851,6 @@
     )
 
 
-def rms_parts(values_in):
-    inverse = lax.rsqrt(jnp.mean(values_in * values_in, axis=-1, keepdims=True) + EPSILON)
-    return (inverse, values_in * inverse)
-
-
-def norm_back(grad_normed, normed, inverse):
-    return inverse * (grad_normed - normed * jnp.mean(grad_normed * normed, axis=-1, keepdims=True))
-
-
 def to_groups(flat_heads, tok_rows, q_group):
     shaped = flat_heads.reshape(tok_rows, KVH, q_group, HD)
     return jnp.transpose(shaped, (1, 2, 0, 3)).reshape(KVH, q_group * tok_rows, HD)
@@ -62,29 +861,9 @@
     return jnp.transpose(shaped, (2, 0, 1, 3)).reshape(tok_rows, KVH * q_group * HD)
 
 
-def contract_rows(left, right):
-    return lax.dot_general(
-        left, right, (((0,), (0,)), ((), ())), preferred_element_type=jnp.float32
-    )
-
-
-def contract_cols(left, right):
-    return lax.dot_general(
-        left, right, (((1,), (1,)), ((), ())), preferred_element_type=jnp.float32
-    )
-
-
-def fold_rows(left, piece):
-    return jnp.dot(left, piece, preferred_element_type=jnp.float32)
-
-
 def grad_rows(left, right, folding, count):
     block = contract_rows(left, right)
     return block.reshape(count, right.shape[1] // folding)
-
-
-def gated(gate_in, up_in):
-    return jax.nn.gelu(gate_in, approximate=True) * up_in
 
 
 def blockwise(step_fn, carry, piece, width):
@@ -126,7 +905,7 @@
     return (d_query, d_key.reshape(key_count, KVH * HD), d_value.reshape(key_count, KVH * HD))
 
 
-def on_device(
+def on_any_mesh(
     tokens,
     w_query,
     w_key,
@@ -151,7 +930,7 @@
     my_block = lax.axis_index("ctx")
     my_start = my_block * tok_rows
     positions = my_start + jnp.arange(tok_rows, dtype=jnp.int32)
-    cos_tab, sine_tab = rope_tables(positions, HD)
+    cos_tab, sine_tab = head_tables(positions, HD)
     row_pos = jnp.tile(positions, q_group)
     last_pos = my_start + tok_rows - 1
     resid_in = tokens[0].astype(jnp.float32)
@@ -176,13 +955,13 @@
     projected = jnp.dot(hidden, full_qkv, preferred_element_type=jnp.float32)
     query_lin = projected[:, :width_q].reshape(tok_rows, H, HD)
     queries = (
-        (rotate(query_lin, cos_tab, sine_tab) * q_scale)
+        (rotate_heads(query_lin, cos_tab, sine_tab) * q_scale)
         .astype(jnp.bfloat16)
         .reshape(tok_rows, width_q)
     )
     query_grp = to_groups(queries, tok_rows, q_group)
     key_lin = projected[:, width_q : width_q + width_kv].reshape(tok_rows, KVH, HD)
-    key_rows = rotate(key_lin, cos_tab, sine_tab).astype(jnp.bfloat16).reshape(tok_rows, width_kv)
+    key_rows = rotate_heads(key_lin, cos_tab, sine_tab).astype(jnp.bfloat16).reshape(tok_rows, width_kv)
     value_rows = projected[:, width_q + width_kv :].astype(jnp.bfloat16)
 
     def add_block(partial_value, piece, first_row):
@@ -332,10 +1111,10 @@
     )
     d_query_flat = from_groups(d_query_grp, tok_rows, q_group).reshape(tok_rows, H, HD) * q_scale
     dq_lin = (
-        unrotate(d_query_flat, cos_tab, sine_tab).astype(jnp.bfloat16).reshape(tok_rows, width_q)
+        unrotate_heads(d_query_flat, cos_tab, sine_tab).astype(jnp.bfloat16).reshape(tok_rows, width_q)
     )
     dk_lin = (
-        unrotate(d_keys.reshape(tok_rows, KVH, HD), cos_tab, sine_tab)
+        unrotate_heads(d_keys.reshape(tok_rows, KVH, HD), cos_tab, sine_tab)
         .astype(jnp.bfloat16)
         .reshape(tok_rows, width_kv)
     )
@@ -370,38 +1149,12 @@
 
 
 def solution(mesh):
+    ring = mesh.shape["ctx"] == RING and mesh.shape["fsdp"] == 4
+    tokens, rows, gains = P("fsdp", "ctx", None), P(("ctx", "fsdp"), None), P(("ctx", "fsdp"))
     return jax.shard_map(
-        on_device,
+        on_ring if ring else on_any_mesh,
         mesh=mesh,
-        in_specs=(
-            P("fsdp", "ctx", None),
-            P(("ctx", "fsdp"), None),
-            P(("ctx", "fsdp"), None),
-            P(("ctx", "fsdp"), None),
-            P(("ctx", "fsdp"), None),
-            P(("ctx", "fsdp"), None),
-            P(("ctx", "fsdp"), None),
-            P(("ctx", "fsdp"), None),
-            P(("ctx", "fsdp")),
-            P(("ctx", "fsdp")),
-            P(("ctx", "fsdp")),
-            P(("ctx", "fsdp")),
-            P("fsdp", "ctx", None),
-        ),
-        out_specs=(
-            P("fsdp", "ctx", None),
-            P("fsdp", "ctx", None),
-            P(("ctx", "fsdp"), None),
-            P(("ctx", "fsdp"), None),
-            P(("ctx", "fsdp"), None),
-            P(("ctx", "fsdp"), None),
-            P(("ctx", "fsdp"), None),
-            P(("ctx", "fsdp"), None),
-            P(("ctx", "fsdp"), None),
-            P(("ctx", "fsdp")),
-            P(("ctx", "fsdp")),
-            P(("ctx", "fsdp")),
-            P(("ctx", "fsdp")),
-        ),
+        in_specs=(tokens,) + (rows,) * 7 + (gains,) * 4 + (tokens,),
+        out_specs=(tokens, tokens) + (rows,) * 7 + (gains,) * 4,
         check_vma=False,
     )

time: 3990 us -> 1060 us (0.27)
  the two profiles are of different devices: /device:TPU:1 before, /device:TPU:13 now
where the time goes in v1:
time: 1060 us; the launch traced here: 1050 us
  Pallas kernels  867 us (82%)
  matrix products  116 us (11%)
  other arithmetic  41.6 us (4%)
  local copies, waits for them, and re-layouts  27.3 us (3%)
    pallas_call x4, Pallas kernels, ring_gather(): pl.pallas_call(functools.partial(gather_kernel, paired), out_shape=[whole...  295 us
    pallas_call x4, Pallas kernels, ring_scatter(): pl.pallas_call(functools.partial(scatter_kernel, paired), out_shape=jax.S...  222 us
    pallas_call x1, Pallas kernels, weights_out(): pl.pallas_call(weights_out_kernel, out_shape=[full(rows, FF), full(rows,...  183 us
    pallas_call x1, Pallas kernels, weights_in(): pl.pallas_call(weights_in_kernel, out_shape=shapes, in_specs=[HBM] * 8, o...  167 us
    dot_general x6, matrix products, contract_cols(): lax.dot_general(left, right, (((1,), (1,)), ((), ())), preferred_element_...  44.5 us
    dot_general x6, matrix products, fold_rows(): return jnp.dot(left, right, preferred_element_type=F32)  36 us
    dot_general x7, matrix products, contract_rows(): lax.dot_general(left, right, (((0,), (0,)), ((), ())), preferred_element_...  35.7 us
    unnamed x125, local copies, waits for them, and re-layouts  25.3 us

profile of v1, /device:TPU:13, one launch (start us, length us, event | category | flops | bytes accessed | tf_op | source)
XLA Modules:
  0.0 1054.2 jit_solution(11935643341084424694)
XLA Ops:
  1.6 93.6 %shard_map.228 = (bf16[8,128,2304]{2,1,0:T(8,128)(2,1)}, bf16[8,128,2304]{2,1,0:T(8,128)(2,1)}) custom-call(bf16[128,2304]{1,0:T(8,128)(2,1)} %bitcast.87), custom_call_target="tpu_custom_call" | custom-call | tf_op jit(solution)/shard_map/pallas_call | solution.py:228
  95.2 3.3 multiply_reduce_fusion
  98.6 167.2 %shard_map.229 = (bf16[32,72,3072]{2,1,0:T(8,128)(2,1)S(1)}, bf16[4,288,2304]{2,1,0:T(8,128)(2,1)S(1)}, bf16[4,64,2304]{2,1,0:T(8,128)(2,1)S(1)}, f32[32,8,128]{2,1,0:T(8,128)S(1)}) custom-call(bf16[72,9216]{1,0:T(8,128)(2,1)S(1)} %copy-done, bf16[72,9216]{1,0:T(8,128)(2,1)S(1)} %copy-done.1, bf16[72,2048]{1,0:T(8,128)(2,1)S(1)} %copy-done.5, ...), custom_call_target="tpu_custom_call" | custom-call | tf_op jit(solution)/shard_map/pallas_call | solution.py:474
  266.8 5.1 copy-done.9
  274.8 3.5 fusion.1
  278.3 7.6 fusion.19
  293.0 3.6 convolution_convert_fusion.4
  296.5 55.1 %shard_map.230 = f32[128,2304]{1,0:T(8,128)} custom-call(bf16[8,128,2304]{2,1,0:T(8,128)(2,1)} %bitcast.85), custom_call_target="tpu_custom_call" | custom-call | tf_op jit(solution)/shard_map/pallas_call | solution.py:313
  356.3 53.1 %shard_map.231 = bf16[8,128,2304]{2,1,0:T(8,128)(2,1)} custom-call(bf16[128,2304]{1,0:T(8,128)(2,1)} %multiply_convert_fusion.4.x_ref), custom_call_target="tpu_custom_call" | custom-call | tf_op jit(solution)/shard_map/pallas_call | solution.py:228
  409.4 15.0 %fusion.4 = f32[1024,2304]{1,0:T(8,128)S(1)} fusion(bf16[1024,2304]{1,0:T(8,128)(2,1)} %bitcast.94, bf16[2304,3072]{1,0:T(8,128)(2,1)} %bitcast.76), kind=kOutput, calls=%fused_computation.8 | convolution fusion | flops 10871635968 | bytes 24772608 | tf_op jit(solution)/shard_map/dot_general | solution.py:69
  428.2 8.1 convolution_convert_fusion.3
  436.3 48.9 %shard_map.232 = f32[128,2304]{1,0:T(8,128)} custom-call(bf16[8,128,2304]{2,1,0:T(8,128)(2,1)} %bitcast.92), custom_call_target="tpu_custom_call" | custom-call | tf_op jit(solution)/shard_map/pallas_call | solution.py:313
  491.3 51.2 %shard_map.233 = bf16[8,128,2304]{2,1,0:T(8,128)(2,1)} custom-call(bf16[128,2304]{1,0:T(8,128)(2,1)} %get-tuple-element.62.x_ref), custom_call_target="tpu_custom_call" | custom-call | tf_op jit(solution)/shard_map/pallas_call | solution.py:228
  542.6 15.3 %fusion.15 = (bf16[1024,1152]{1,0:T(8,128)(2,1)}, bf16[1024,1152]{1,0:T(8,128)(2,1)}) fusion(f32[1024,2304]{1,0:T(8,128)} %copy-done.13, bf16[1024,2304]{1,0:T(8,128)(2,1)} %bitcast.98, bf16[1152,2304]{1,0:T(8,128)(2,1)S(1)} %bitcast.84), kind=kOutput, calls=%fused_computation.23 | convolution fusion | flops 5464129536 | bytes 24182784 | tf_op jit(solution)/shard_map/dot_general | solution.py:65
  557.9 10.7 %convolution_convert_fusion.1 = bf16[1152,2304]{1,0:T(8,128)(2,1)} fusion(bf16[1024,1152]{1,0:T(8,128)(2,1)} %copy-done.21, bf16[1024,2304]{1,0:T(8,128)(2,1)} %bitcast.99), kind=kOutput, calls=%fused_computation.1 | convolution fusion | flops 5438472192 | bytes 12386304 | tf_op jit(solution)/shard_map/dot_general | solution.py:61
  568.6 13.3 %fusion.6 = bf16[1024,2304]{1,0:T(8,128)(2,1)} fusion(bf16[2304,3072]{1,0:T(8,128)(2,1)S(1)} %bitcast.80, bf16[1024,1152]{1,0:T(8,128)(2,1)S(1)} %copy-done.47, bf16[1024,1152]{1,0:T(8,128)(2,1)S(1)} %copy-done.45), kind=kOutput, calls=%fused_computation.13 | convolution fusion | flops 10883432448 | bytes 20054016 | tf_op jit(solution)/shard_map/dot_general | solution.py:65
  581.9 46.4 %shard_map.234 = f32[128,2304]{1,0:T(8,128)} custom-call(bf16[8,128,2304]{2,1,0:T(8,128)(2,1)} %bitcast.93), custom_call_target="tpu_custom_call" | custom-call | tf_op jit(solution)/shard_map/pallas_call | solution.py:313
  633.5 14.3 %convolution_convert_fusion = bf16[2304,2304]{1,0:T(8,128)(2,1)} fusion(bf16[1024,2304]{1,0:T(8,128)(2,1)S(1)} %bitcast.97, bf16[1024,1152]{1,0:T(8,128)(2,1)S(1)} %copy-done.48, bf16[1024,1152]{1,0:T(8,128)(2,1)S(1)} %copy-done.46), kind=kOutput, calls=%fused_computation | convolution fusion | flops 10886381568 | bytes 20054016 | tf_op jit(solution)/shard_map/dot_general | solution.py:61
  647.7 97.5 %shard_map.235 = (bf16[8,128,2304]{2,1,0:T(8,128)(2,1)}, bf16[8,128,2304]{2,1,0:T(8,128)(2,1)}) custom-call(bf16[128,2304]{1,0:T(8,128)(2,1)} %multiply_convert_fusion.3.x_ref), custom_call_target="tpu_custom_call" | custom-call | tf_op jit(solution)/shard_map/pallas_call | solution.py:228
  745.3 3.9 fusion.42
  767.5 7.9 convolution_convert_fusion.2
  775.4 5.6 convolution_convert_fusion.5
  781.0 71.6 %shard_map.236 = f32[128,2304]{1,0:T(8,128)} custom-call(bf16[8,128,2304]{2,1,0:T(8,128)(2,1)} %bitcast.91), custom_call_target="tpu_custom_call" | custom-call | tf_op jit(solution)/shard_map/pallas_call | solution.py:313
  857.5 182.8 %shard_map.237 = (f32[72,9216]{1,0:T(8,128)}, f32[72,9216]{1,0:T(8,128)}, f32[72,2048]{1,0:T(8,128)}, f32[72,1024]{1,0:T(8,128)}, f32[72,1024]{1,0:T(8,128)}, /*...) custom-call(bf16[32,72,2304]{2,1,0:T(8,128)(2,1)} %bitcast.86, bf16[32,72,768]{2,1,0:T(8,128)(2,1)} %bitcast.100, ...), custom_call_target="tpu_custom_call" | custom-call | tf_op jit(solution)/shard_map/pallas_call | solution.py:678
  (178 shorter events, 67.9 us)
Async XLA Ops:
  0.6 97.9 %copy-start.1 = (bf16[72,9216]{1,0:T(8,128)(2,1)S(1)}, bf16[72,9216]{1,0:T(8,128)(2,1)}, u32[]{:S(2)}) copy-start(bf16[72,9216]{1,0:T(8,128)(2,1)} %up.1) | copy-start | bytes 3981316
  0.7 97.9 %copy-start = (bf16[72,9216]{1,0:T(8,128)(2,1)S(1)}, bf16[72,9216]{1,0:T(8,128)(2,1)}, u32[]{:S(2)}) copy-start(bf16[72,9216]{1,0:T(8,128)(2,1)} %gate.1) | copy-start | bytes 3981316
  0.7 97.9 %copy-start.6 = (bf16[64,2304]{1,0:T(8,128)(2,1)S(1)}, bf16[64,2304]{1,0:T(8,128)(2,1)}, u32[]{:S(2)}) copy-start(bf16[64,2304]{1,0:T(8,128)(2,1)} %out.1) | copy-start | bytes 884740
  0.7 97.9 %copy-start.8 = (bf16[72,1024]{1,0:T(8,128)(2,1)S(1)}, bf16[72,1024]{1,0:T(8,128)(2,1)}, u32[]{:S(2)}) copy-start(bf16[72,1024]{1,0:T(8,128)(2,1)} %value.1) | copy-start | bytes 442372
  0.7 97.9 %copy-start.7 = (bf16[72,1024]{1,0:T(8,128)(2,1)S(1)}, bf16[72,1024]{1,0:T(8,128)(2,1)}, u32[]{:S(2)}) copy-start(bf16[72,1024]{1,0:T(8,128)(2,1)} %key.1) | copy-start | bytes 442372
  0.7 97.9 %copy-start.5 = (bf16[72,2048]{1,0:T(8,128)(2,1)S(1)}, bf16[72,2048]{1,0:T(8,128)(2,1)}, u32[]{:S(2)}) copy-start(bf16[72,2048]{1,0:T(8,128)(2,1)} %query.1) | copy-start | bytes 884740
  0.7 97.9 %copy-start.2 = (bf16[288,2304]{1,0:T(8,128)(2,1)S(1)}, bf16[288,2304]{1,0:T(8,128)(2,1)}, u32[]{:S(2)}) copy-start(bf16[288,2304]{1,0:T(8,128)(2,1)} %down.1) | copy-start | bytes 3981316
  0.7 285.1 %copy-start.33 = (f32[128]{0:T(128)}, f32[128]{0:T(128)S(1)}, u32[]{:S(2)}) copy-start(f32[128]{0:T(128)S(1)} %multiply_power_fusion) | copy-start | bytes 1540
  296.5 56.6 %copy-start.12 = (bf16[1,128,2304]{2,1,0:T(8,128)(2,1)S(1)}, bf16[1,128,2304]{2,1,0:T(8,128)(2,1)}, u32[]{:S(2)}) copy-start(bf16[1,128,2304]{2,1,0:T(8,128)(2,1)} %param.13) | copy-start | bytes 1769476
  355.4 69.1 %copy-start.35 = (f32[128]{0:T(128)}, f32[128]{0:T(128)S(1)}, u32[]{:S(2)}) copy-start(f32[128]{0:T(128)S(1)} %get-tuple-element.74) | copy-start | bytes 1540
  356.3 71.8 %slice-start.4 = ((s8[5308416]{0:T(1024)(128)(4,1)}), s8[4194304]{0:T(1024)(128)(4,1)S(1)}, s32[]{:S(2)}) async-start(s8[5308416]{0:T(1024)(128)(4,1)} %bitcast.81), calls=%async_computation.4 | async-start | bytes 8388608
  409.4 18.7 %slice-start.5 = ((s8[5308416]{0:T(1024)(128)(4,1)}), s8[1114112]{0:T(1024)(128)(4,1)S(1)}, s32[]{:S(2)}) async-start(s8[5308416]{0:T(1024)(128)(4,1)} %bitcast.81), calls=%async_computation.5 | async-start | bytes 2228224
  542.5 26.0 %slice-start = ((s8[14155776]{0:T(1024)(128)(4,1)}), s8[4194304]{0:T(1024)(128)(4,1)S(1)}, s32[]{:S(2)}) async-start(s8[14155776]{0:T(1024)(128)(4,1)} %bitcast.78), calls=%async_computation | async-start | bytes 8388608
  542.5 26.0 %slice-start.1 = ((s8[14155776]{0:T(1024)(128)(4,1)}), s8[4194304]{0:T(1024)(128)(4,1)S(1)}, s32[]{:S(2)}) async-start(s8[14155776]{0:T(1024)(128)(4,1)} %bitcast.78), calls=%async_computation.1 | async-start | bytes 8388608
  542.6 26.0 %slice-start.2 = ((s8[14155776]{0:T(1024)(128)(4,1)}), s8[1572864]{0:T(1024)(128)(4,1)S(1)}, s32[]{:S(2)}) async-start(s8[14155776]{0:T(1024)(128)(4,1)} %bitcast.78), calls=%async_computation.2 | async-start | bytes 3145728
  557.8 10.7 %copy-start.45 = (bf16[1024,1152]{1,0:T(8,128)(2,1)S(1)}, bf16[1024,1152]{1,0:T(8,128)(2,1)}, u32[]{:S(2)}) copy-start(bf16[1024,1152]{1,0:T(8,128)(2,1)} %get-tuple-element.56) | copy-start | bytes 7077892
  557.8 10.7 %copy-start.47 = (bf16[1024,1152]{1,0:T(8,128)(2,1)S(1)}, bf16[1024,1152]{1,0:T(8,128)(2,1)}, u32[]{:S(2)}) copy-start(bf16[1024,1152]{1,0:T(8,128)(2,1)} %get-tuple-element.57) | copy-start | bytes 7077892
  581.9 46.4 %copy-start.36 = (f32[128]{0:T(128)S(1)}, f32[128]{0:T(128)}, u32[]{:S(2)}) copy-start(f32[128]{0:T(128)} %copy-done.35) | copy-start | bytes 1540
  581.9 48.3 %copy-start.11 = (f32[128,2304]{1,0:T(8,128)S(1)}, f32[128,2304]{1,0:T(8,128)}, u32[]{:S(2)}) copy-start(f32[128,2304]{1,0:T(8,128)} %shard_map.230) | copy-start | bytes 3538948
  581.9 48.3 %copy-start.14 = (bf16[1,128,2304]{2,1,0:T(8,128)(2,1)S(1)}, bf16[1,128,2304]{2,1,0:T(8,128)(2,1)}, u32[]{:S(2)}) copy-start(bf16[1,128,2304]{2,1,0:T(8,128)(2,1)} %param.25) | copy-start | bytes 1769476
  581.9 48.3 %copy-start.39 = (f32[128]{0:T(128)S(1)}, f32[128]{0:T(128)}, u32[]{:S(2)}) copy-start(f32[128]{0:T(128)} %copy-done.38) | copy-start | bytes 1540
  633.5 111.8 %copy-start.20 = (f32[1024,256]{0,1:T(8,128)S(1)}, f32[1024,256]{0,1:T(8,128)}, u32[]{:S(2)}) copy-start(f32[1024,256]{0,1:T(8,128)} %copy-done.19) | copy-start | bytes 3145732
  781.0 71.6 %copy-start.32 = (f32[2304]{0:T(1024)S(1)}, f32[2304]{0:T(1024)}, u32[]{:S(2)}) copy-start(f32[2304]{0:T(1024)} %copy-done.31) | copy-start | bytes 27652
  781.0 71.6 %copy-start.37 = (f32[128]{0:T(128)S(1)}, f32[128]{0:T(128)}, u32[]{:S(2)}) copy-start(f32[128]{0:T(128)} %get-tuple-element.73) | copy-start | bytes 1540
  (35 other events, 130.4 us)

commit v2 on v1

--- a/solution.py
+++ b/solution.py
@@ -136,104 +136,118 @@
     return list(range(half)) if direction == 0 else list(range(half, SUB))
 
 
+class RingGather:
+    def __init__(self, x_ref, ring_ref, seq_ref, loc_sem, ss, rs, sib_ss=None, sib_rs=None):
+        self.x_ref, self.ring_ref, self.seq_ref, self.loc_sem = x_ref, ring_ref, seq_ref, loc_sem
+        self.ss, self.rs, self.sib_ss, self.sib_rs = ss, rs, sib_ss, sib_rs
+        self.z, self.core, self.y, self.x = my_place()
+        self.p = ring_index(self.y, self.z)
+        self.right, self.left = (self.p + 1) % RING, (self.p + RING - 1) % RING
+        self.sibling = device(self.z, 1 - self.core, self.y, self.x)
+        self.piece = x_ref.shape[0] // SUB
+        self.pending = []
+        self.local = pltpu.make_async_copy(x_ref, ring_ref.at[self.p], loc_sem.at[RING])
+
+    def places(self):
+        near = [ring_device(self.right, self.core, self.x), ring_device(self.left, self.core, self.x)]
+        return near + ([self.sibling] if self.seq_ref is not None else [])
+
+    def origin(self, direction, step):
+        return (self.p + (RING - step if direction == 0 else step)) % RING
+
+    def copy(self, direction, step, k):
+        q = self.origin(direction, step)
+        rows = pl.ds(k * self.piece, self.piece)
+        src = self.x_ref.at[rows] if step == 0 else self.ring_ref.at[q, rows]
+        return remote(
+            src,
+            self.ring_ref.at[q, rows],
+            self.ss.at[direction, step, k],
+            self.rs.at[direction, step, k],
+            ring_device(self.right if direction == 0 else self.left, self.core, self.x),
+        )
+
+    def place(self, q, act):
+        if self.seq_ref is None:
+            return
+        yq, zq = ring_yz(q)
+        src, dst = self.ring_ref.at[q], self.seq_ref.at[2 * zq + self.core]
+
+        @pl.when(yq == self.core)
+        def _():
+            act(pltpu.make_async_copy(src, dst, self.loc_sem.at[q]))
+
+        @pl.when(yq != self.core)
+        def _():
+            act(remote(src, dst, self.sib_ss.at[zq], self.sib_rs.at[zq], self.sibling))
+
+    def step(self, step):
+        if step == 0:
+            self.local.start()
+        for k in range(SUB):
+            for direction in (0, 1):
+                if step > 0 and (step < 3 or k in ring_parts(direction, 3, 3)):
+                    self.copy(direction, step - 1, k).wait_recv()
+                if k in ring_parts(direction, step, 3):
+                    c = self.copy(direction, step, k)
+                    c.start()
+                    self.pending.append(c)
+        if step == 1:
+            self.local.wait()
+            self.place(self.p, lambda c: c.start())
+        if step == 3:
+            for direction in (0, 1):
+                for k in range(SUB):
+                    if k not in ring_parts(direction, 3, 3):
+                        self.copy(direction, 2, k).wait_recv()
+        if step > 0:
+            for direction in (0, 1):
+                self.place(self.origin(direction, step), lambda c: c.start())
+
+    def finish(self):
+        for direction in (0, 1):
+            for k in ring_parts(direction, 3, 3):
+                self.copy(direction, 3, k).wait_recv()
+        self.place((self.p + 4) % RING, lambda c: c.start())
+        for c in self.pending:
+            c.wait_send()
+        if self.seq_ref is None:
+            return
+        for q in range(RING):
+            self.place((self.p + q) % RING, lambda c: c.wait_send() if c.is_remote else c.wait())
+        for zq in range(NZ):
+            dst = self.seq_ref.at[2 * zq + 1 - self.core]
+            remote(self.ring_ref.at[zq], dst, self.sib_ss.at[zq], self.sib_rs.at[zq], self.sibling).wait_recv()
+
+
 def gather_kernel(paired, x_ref, *refs):
     if paired:
-        ring_ref, seq_ref, loc_sem, ss, rs, sib_ss, sib_rs = refs
+        seq_ref, ring_ref, *sems = refs
     else:
-        ring_ref, loc_sem, ss, rs = refs
-    z, core, y, x = my_place()
-    p = ring_index(y, z)
-    right, left = (p + 1) % RING, (p + RING - 1) % RING
-    sibling = device(z, 1 - core, y, x)
-    piece = x_ref.shape[0] // SUB
-    greet(
-        [ring_device(right, core, x), ring_device(left, core, x)] + ([sibling] if paired else [])
-    )
-    local = pltpu.make_async_copy(x_ref, ring_ref.at[p], loc_sem.at[RING])
-    local.start()
-
-    def copy(direction, step, k):
-        q = (p + (RING - step if direction == 0 else step)) % RING
-        rows = pl.ds(k * piece, piece)
-        src = x_ref.at[rows] if step == 0 else ring_ref.at[q, rows]
-        return remote(
-            src,
-            ring_ref.at[q, rows],
-            ss.at[direction, step, k],
-            rs.at[direction, step, k],
-            ring_device(right if direction == 0 else left, core, x),
-        )
-
-    def place_block(q, act):
-        if not paired:
-            return
-        yq, zq = ring_yz(q)
-
-        @pl.when(yq == core)
-        def _():
-            act(pltpu.make_async_copy(ring_ref.at[q], seq_ref.at[2 * zq + core], loc_sem.at[q]))
-
-        @pl.when(yq != core)
-        def _():
-            act(remote(ring_ref.at[q], seq_ref.at[2 * zq + core], sib_ss.at[zq], sib_rs.at[zq], sibling))
-
-    pending = []
+        ring_ref, *sems = refs
+        seq_ref = None
+    ring = RingGather(x_ref, ring_ref, seq_ref, *sems)
+    greet(ring.places())
     for step in range(4):
-        for k in range(SUB):
-            for direction in (0, 1):
-                if k not in ring_parts(direction, step, 3):
-                    continue
-                if step > 0:
-                    copy(direction, step - 1, k).wait_recv()
-                c = copy(direction, step, k)
-                c.start()
-                pending.append(c)
-        if step == 0:
-            local.wait()
-            place_block(p, lambda c: c.start())
-        elif step < 3:
-            for direction in (0, 1):
-                q = (p + (RING - step if direction == 0 else step)) % RING
-                place_block(q, lambda c: c.start())
-    for direction in (0, 1):
-        for k in range(SUB):
-            if k not in ring_parts(direction, 3, 3):
-                copy(direction, 2, k).wait_recv()
-    for direction in (0, 1):
-        place_block((p + (RING - 3 if direction == 0 else 3)) % RING, lambda c: c.start())
-    for direction in (0, 1):
-        for k in ring_parts(direction, 3, 3):
-            copy(direction, 3, k).wait_recv()
-    place_block((p + 4) % RING, lambda c: c.start())
-    for c in pending:
-        c.wait_send()
-
-    def finish(c):
-        if c.is_remote:
-            c.wait_send()
-        else:
-            c.wait()
-
-    if paired:
-        for q in range(RING):
-            place_block((p + q) % RING, finish)
-        for zq in range(NZ):
-            remote(ring_ref.at[zq], seq_ref.at[2 * zq + 1 - core], sib_ss.at[zq], sib_rs.at[zq], sibling).wait_recv()
+        ring.step(step)
+    ring.finish()
 
 
 def ring_gather(block, collective_id, paired):
     rows, width = block.shape
     whole = jax.ShapeDtypeStruct((RING, rows, width), block.dtype)
     sems = [DMA((RING + 1,)), DMA((2, 4, SUB)), DMA((2, 4, SUB))]
+    if paired:
+        sems = [pltpu.VMEM(whole.shape, whole.dtype)] + sems + [DMA((NZ,)), DMA((NZ,))]
     out = pl.pallas_call(
         functools.partial(gather_kernel, paired),
-        out_shape=[whole, whole] if paired else [whole],
-        in_specs=[HBM],
-        out_specs=[HBM, HBM] if paired else [HBM],
-        scratch_shapes=sems + ([DMA((NZ,)), DMA((NZ,))] if paired else []),
+        out_shape=whole,
+        in_specs=[VMEM],
+        out_specs=VMEM if paired else HBM,
+        scratch_shapes=sems,
         compiler_params=params(collective_id),
     )(block)
-    return out[-1].reshape(RING * rows, width)
+    return out.reshape(RING * rows, width)
 
 
 def scatter_kernel(paired, part_ref, o_ref, *refs):
@@ -333,14 +347,22 @@
     return device(t // 2, core, t % 2, x)
 
 
+def partner(t, j):
+    out = 0
+    for bit in (1, 2, 4):
+        on = (t // bit) % 2
+        out = out + bit * (1 - on if j & bit else on)
+    return out
+
+
 def column_start(which, t):
     if which < 2:
         return pl.multiple_of(t * UNITS, 128)
     return pl.multiple_of((t if which == 2 else t // 2) * HD, 128)
 
 
-def weights_in_kernel(gate, up, query, key, value, down, out, gains, w_ref, d_ref, o_ref, g_ref,
-                      loc, s1, r1, s2, r2, s3, r3, s4, r4, s5, r5):
+def weights_in_kernel(gate, up, query, key, value, down, out, gains, x_ref, w_ref, d_ref, o_ref, g_ref, seq_ref,
+                      ring_ref, loc, s1, r1, s2, r2, s3, r3, s4, r4, s5, r5, ring_loc, ss, rs, sib_ss, sib_rs):
     z, core, y, x = my_place()
     t = 2 * z + y
     sibling, across = device(z, 1 - core, y, x), device(z, core, y, 1 - x)
@@ -349,31 +371,63 @@
         return (2 * (tq // 2) + corq) * 4 + 2 * (tq % 2) + xq
 
     me = slot(t, core, x)
-    others = [(t + j) % RING for j in range(1, RING)]
+    member = [partner(t, j) for j in range(RING)]
     plane = []
     for dc in (0, 1):
         for dy in (0, 1):
             for dx in (0, 1):
-                if (dc, dy, dx) != (0, 0, 0):
-                    plane.append((dc, dy, dx))
-    places = [member_place(tq, core, x) for tq in others] + [
-        device(z, (core + dc) % 2, (y + dy) % 2, (x + dx) % 2)
-        for dc, dy, dx in plane
-        if (dc, dx) != (0, 0)
-    ]
-    greet(places)
+                if (dc, dx) != (0, 0):
+                    plane.append(device(z, (core + dc) % 2, (y + dy) % 2, (x + dx) % 2))
+    greet([member_place(member[j], core, x) for j in range(1, RING)] + plane)
     sources = (gate, up, query, key, value)
-
-    def first(tq, a, wait=False):
+    ring = RingGather(x_ref, ring_ref, seq_ref, ring_loc, ss, rs, sib_ss, sib_rs)
+
+    def first(j, a, wait=False):
+        tq = member[j]
         if a == 5:
             src, dst = gains, g_ref.at[slot(tq, core, x) if wait else me]
         else:
             src = sources[a].at[:, pl.ds(column_start(a, tq), WIDTHS[a])]
             dst = w_ref.at[slot(tq, core, x) if wait else me, :, pl.ds(STARTS[a], WIDTHS[a])]
-        i = tq if wait else t
-        return remote(src, dst, s1.at[tq, a], r1.at[i, a], member_place(tq, core, x))
+        return remote(src, dst, s1.at[j, a], r1.at[j, a], member_place(tq, core, x))
 
     pending = []
+
+    def go(copies):
+        for c in copies:
+            c.start()
+            pending.append(c)
+
+    def second(j, wait=False):
+        i = slot(member[j], core, 1 - x if wait else x)
+        return [
+            remote(w_ref.at[i], w_ref.at[i], s2.at[j, 0], r2.at[j, 0], across),
+            remote(g_ref.at[i], g_ref.at[i], s2.at[j, 1], r2.at[j, 1], across),
+        ]
+
+    def third(j, flip, wait=False):
+        i = slot(member[j], 1 - core if wait else core, 1 - x if flip else x)
+        return [
+            remote(w_ref.at[i], w_ref.at[i], s3.at[j, flip, 0], r3.at[j, flip, 0], sibling),
+            remote(g_ref.at[i], g_ref.at[i], s3.at[j, flip, 1], r3.at[j, flip, 1], sibling),
+        ]
+
+    def start_round(j):
+        go([first(j, a) for a in (5, 2, 3, 4, 0, 1)])
+
+    def end_round(j):
+        for a in range(6):
+            first(j, a, True).wait_recv()
+        go(second(j) + third(j, 0))
+
+    def end_across(j):
+        for c in second(j, True):
+            c.wait_recv()
+        go(third(j, 1))
+
+    ring.step(0)
+    start_round(4)
+    start_round(1)
     locals_ = [pltpu.make_async_copy(gains, g_ref.at[me], loc.at[5])]
     for a in range(5):
         locals_.append(
@@ -397,26 +451,25 @@
             @pl.when(jnp.logical_not(to_self))
             def _():
                 remote(src, dst.at[mine], s4.at[xq, a], r4.at[y, a], device(z, x, core, xq)).start()
-    for a in (5, 2, 3, 4, 0, 1):
-        for tq in others:
-            c = first(tq, a)
-            c.start()
-            pending.append(c)
-
-    def second(tq, wait=False):
-        i = slot(tq, core, 1 - x if wait else x)
-        return [
-            remote(w_ref.at[i], w_ref.at[i], s2.at[tq, 0], r2.at[tq, 0], across),
-            remote(g_ref.at[i], g_ref.at[i], s2.at[tq, 1], r2.at[tq, 1], across),
-        ]
-
-    def third(tq, flip, wait=False):
-        i = slot(tq, 1 - core if wait else core, 1 - x if flip else x)
-        return [
-            remote(w_ref.at[i], w_ref.at[i], s3.at[tq, flip, 0], r3.at[tq, flip, 0], sibling),
-            remote(g_ref.at[i], g_ref.at[i], s3.at[tq, flip, 1], r3.at[tq, flip, 1], sibling),
-        ]
-
+    for c in locals_:
+        c.wait()
+    go(second(0) + third(0, 0))
+    ring.step(1)
+    end_round(1)
+    start_round(2)
+    end_round(4)
+    start_round(5)
+    ring.step(2)
+    end_round(2)
+    start_round(3)
+    end_across(0)
+    end_across(1)
+    end_round(5)
+    start_round(6)
+    ring.step(3)
+    end_round(3)
+    start_round(7)
+    end_across(4)
     for yq in (0, 1):
         from_self = (core == y) & (yq == y) & (core == x)
         for a, (src, dst) in enumerate(pair):
@@ -428,27 +481,18 @@
             def _():
                 remote(src, dst.at[2 * yq + core], s4.at[0, a], r4.at[yq, a], sibling).wait_recv()
 
-            c = remote(dst.at[2 * yq + core], dst.at[2 * yq + core], s5.at[yq, a], r5.at[yq, a], sibling)
-            c.start()
-            pending.append(c)
-    for c in locals_:
-        c.wait()
-    for tq in [t] + others:
-        if tq is not t:
-            for a in range(6):
-                first(tq, a, True).wait_recv()
-        for c in second(tq) + third(tq, 0):
-            c.start()
-            pending.append(c)
-    for tq in [t] + others:
-        for c in second(tq, True):
-            c.wait_recv()
-        for c in third(tq, 1):
-            c.start()
-            pending.append(c)
-    for tq in [t] + others:
+            go([remote(dst.at[2 * yq + core], dst.at[2 * yq + core], s5.at[yq, a], r5.at[yq, a], sibling)])
+    end_across(2)
+    end_across(5)
+    ring.finish()
+    end_round(6)
+    end_across(3)
+    end_round(7)
+    end_across(6)
+    end_across(7)
+    for j in range(RING):
         for flip in (0, 1):
-            for c in third(tq, flip, True):
+            for c in third(j, flip, True):
                 c.wait_recv()
     for yq in (0, 1):
         for a, (src, dst) in enumerate(pair):
@@ -463,29 +507,34 @@
                 remote(src, dst.at[mine], s4.at[xq, a], r4.at[y, a], device(z, x, core, xq)).wait_send()
 
 
-def weights_in(gate, up, query, key, value, down, out, gains, collective_id):
+def weights_in(gate, up, query, key, value, down, out, gains, block, collective_id):
     n = 4 * RING
+    whole = (RING,) + block.shape
     shapes = [
         jax.ShapeDtypeStruct((n, gate.shape[0], WIDE), BF),
         jax.ShapeDtypeStruct((4,) + down.shape, BF),
         jax.ShapeDtypeStruct((4,) + out.shape, BF),
         jax.ShapeDtypeStruct((n,) + gains.shape, gains.dtype),
+        jax.ShapeDtypeStruct(whole, BF),
     ]
-    return pl.pallas_call(
+    results = pl.pallas_call(
         weights_in_kernel,
         out_shape=shapes,
-        in_specs=[HBM] * 8,
-        out_specs=[HBM] * 4,
+        in_specs=[VMEM] * 9,
+        out_specs=[HBM] * 4 + [VMEM],
         scratch_shapes=[
+            pltpu.VMEM(whole, BF),
             DMA((6,)),
             DMA((RING, 6)), DMA((RING, 6)),
             DMA((RING, 2)), DMA((RING, 2)),
             DMA((RING, 2, 2)), DMA((RING, 2, 2)),
             DMA((2, 2)), DMA((2, 2)),
             DMA((2, 2)), DMA((2, 2)),
+            DMA((RING + 1,)), DMA((2, 4, SUB)), DMA((2, 4, SUB)), DMA((NZ,)), DMA((NZ,)),
         ],
-        compiler_params=params(collective_id, 16),
-    )(gate, up, query, key, value, down, out, gains)
+        compiler_params=params(collective_id, 32),
+    )(gate, up, query, key, value, down, out, gains, block)
+    return list(results[:4]) + [results[4].reshape(RING * block.shape[0], block.shape[1])]
 
 
 def add_into(dst, index, src, other):
@@ -526,8 +575,7 @@
     def to_member(tq, wait=False):
         return remote(acc.at[x, tq], c_buf.at[tq if wait else t], sc.at[tq], rc.at[tq if wait else t], member_place(tq, core, x))
 
-    def each(body):
-        lax.fori_loop(0, RING, lambda j, carry: (body((t + 1 + j) % RING, j), carry)[1], 0)
+    order = [partner(t, j) for j in (4, 5, 6, 7, 2, 3, 1, 0)]
 
     small = ((down_in, da, db, dacc, dd, down_o), (out_in, oa, ob, oacc, od, out_o))
 
@@ -553,59 +601,60 @@
     def gain_c(tq, wait=False):
         return remote(gsum.at[1], ga.at[tq if wait else t], sg.at[tq], rg.at[tq if wait else t], member_place(tq, core, x))
 
-    def start_a(xq):
-        def body(tq, j):
-            for c in load(tq, xq) + to_sibling(tq, xq):
-                c.start()
-
-        each(body)
-
-    start_a(1 - x)
-    gain_a().start()
-    for a in (0, 1):
-        for xo in (0, 1):
-            small_a(a, xo).start()
-            small_load(a, xo).start()
-    start_a(x)
-
-    def sum_a(xq, tq):
+    def start_a(tq, xq):
+        for c in load(tq, xq) + to_sibling(tq, xq):
+            c.start()
+
+    def sum_a(tq, xq):
         for c in load(tq, xq):
             c.wait()
         for c in to_sibling(tq, xq):
             c.wait_recv()
         acc[xq, tq] = (acc[xq, tq].astype(F32) + a_buf[xq, tq].astype(F32)).astype(BF)
 
-    def step_one(tq, j):
-        sum_a(1 - x, tq)
-        to_across(tq).start()
-
-    each(step_one)
-    gain_a().wait_recv()
-    gsum[0] = gain_in[...] + ga[RING]
-    gain_b().start()
-    for a in (0, 1):
+    def small_start(a):
         buf, total = small[a][1], small[a][3]
         for xo in (0, 1):
             small_load(a, xo).wait()
             small_a(a, xo).wait_recv()
             total[xo] = (total[xo].astype(F32) + buf[xo].astype(F32)).astype(BF)
         small_b(a).start()
-    each(lambda tq, j: sum_a(x, tq))
-    gain_b().wait_recv()
-    gsum[1] = gsum[0] + ga[RING + 1]
-    for tq in others:
-        gain_c(tq).start()
-
-    def step_two(tq, j):
+
+    for tq in order:
+        start_a(tq, 1 - x)
+    gain_a().start()
+    for a in (1, 0):
+        for xo in (0, 1):
+            small_a(a, xo).start()
+            small_load(a, xo).start()
+    for tq in order:
+        start_a(tq, x)
+    ahead = 2
+    for tq in order[:ahead]:
+        sum_a(tq, 1 - x)
+        to_across(tq).start()
+    gain_a().wait_recv()
+    gsum[0] = gain_in[...] + ga[RING]
+    gain_b().start()
+    small_start(1)
+    for tq in order[ahead:]:
+        sum_a(tq, 1 - x)
+    for j, tq in enumerate(order):
+        sum_a(tq, x)
         to_across(tq).wait_recv()
+        if j + ahead < RING:
+            to_across(order[j + ahead]).start()
+        elif j + ahead == RING:
+            small_start(0)
+        if j == 0:
+            gain_b().wait_recv()
+            gsum[1] = gsum[0] + ga[RING + 1]
+            for other in others:
+                gain_c(other).start()
         acc[x, tq] = (acc[x, tq].astype(F32) + b_buf[tq].astype(F32)).astype(BF)
-
-        @pl.when(j < RING - 1)
-        def _():
+        if j < RING - 1:
             to_member(tq).start()
-
-    each(step_two)
-    for a in (0, 1):
+    for a in (1, 0):
         other, total = small[a][2:4]
         small_b(a).wait_recv()
         total[x] = (total[x].astype(F32) + other[...].astype(F32)).astype(BF)
@@ -645,17 +694,13 @@
             columns = pl.ds(start, HD)
             result[:, pl.ds(g * HD, HD)] = c_buf[2 * g, :, columns].astype(F32) + c_buf[2 * g + 1, :, columns].astype(F32)
 
-    def drain(tq, j):
+    for j, tq in enumerate(order):
         for xq in (0, 1):
             for c in to_sibling(tq, xq):
                 c.wait_send()
         to_across(tq).wait_send()
-
-        @pl.when(j < RING - 1)
-        def _():
+        if j < RING - 1:
             to_member(tq).wait_send()
-
-    each(drain)
     gain_a().wait_send()
     gain_b().wait_send()
     for tq in others:
@@ -738,8 +783,8 @@
     shard_gain = pre_gain.shape[0]
     gains = jnp.stack([pre_gain, post_gain, pre_ffn_gain, post_ffn_gain]).astype(F32)
     gains = jnp.pad(gains, ((0, 4), (0, 128 - shard_gain)))
-    w_in, down_in, out_in, gains_in = weights_in(
-        w_gate, w_up, w_query, w_key, w_value, w_down, w_out, gains, next(ids)
+    w_in, down_in, out_in, gains_in, sequence = weights_in(
+        w_gate, w_up, w_query, w_key, w_value, w_down, w_out, gains, tokens[0], next(ids)
     )
     w_in = w_in.reshape(-1, WIDE)
     w_gu, w_qkv = w_in[:, : 2 * UNITS], w_in[:, 2 * UNITS :]
@@ -753,8 +798,7 @@
 
     resid_in = tokens[0].astype(F32)
     inv_pre, normed_pre = rms_parts(resid_in)
-    sequence = ring_gather(tokens[0], next(ids), True).astype(F32)
-    hidden = (rms_parts(sequence)[1] * pre_factor).astype(BF)
+    hidden = (rms_parts(sequence.astype(F32))[1] * pre_factor).astype(BF)
     projected = fold_rows(hidden, w_qkv)
     queries = (rotate(projected[:, :HD], cos_tab, sine_tab) * q_scale).astype(BF)
     keys = rotate(projected[:, HD : 2 * HD], cos_tab, sine_tab).astype(BF)

time: 1060 us -> 851 us (0.80)
  the two profiles are of different devices: /device:TPU:13 before, /device:TPU:1 now
where the time goes in v2:
time: 851 us; the launch traced here: 844 us
  Pallas kernels  654 us (77%)
  matrix products  115 us (14%)
  other arithmetic  41.2 us (5%)
  local copies, waits for them, and re-layouts  31.7 us (4%)
    pallas_call x4, Pallas kernels, ring_scatter(): pl.pallas_call(functools.partial(scatter_kernel, paired), out_shape=jax.S...  206 us
    pallas_call x1, Pallas kernels, weights_in(): pl.pallas_call(weights_in_kernel, out_shape=shapes, in_specs=[VMEM] * 9,...  153 us
    pallas_call x3, Pallas kernels, ring_gather(): pl.pallas_call(functools.partial(gather_kernel, paired), out_shape=whole,...  151 us
    pallas_call x1, Pallas kernels, weights_out(): pl.pallas_call(weights_out_kernel, out_shape=[full(rows, FF), full(rows,...  145 us
    dot_general x6, matrix products, contract_cols(): lax.dot_general(left, right, (((1,), (1,)), ((), ())), preferred_element_...  46.3 us
    dot_general x6, matrix products, fold_rows(): return jnp.dot(left, right, preferred_element_type=F32)  36.2 us
    dot_general x7, matrix products, contract_rows(): lax.dot_general(left, right, (((0,), (0,)), ((), ())), preferred_element_...  32.2 us
    unnamed x109, local copies, waits for them, and re-layouts  29.7 us

profile of v2, /device:TPU:1, one launch (start us, length us, event | category | flops | bytes accessed | tf_op | source)
XLA Modules:
  0.0 843.6 jit_solution(17864651999699271127)
XLA Ops:
  10.2 152.7 %shard_map.228 = (bf16[32,72,3072]{2,1,0:T(8,128)(2,1)}, bf16[4,288,2304]{2,1,0:T(8,128)(2,1)S(1)}, bf16[4,64,2304]{2,1,0:T(8,128)(2,1)S(1)}, f32[32,8,128]{2,1,0:T(8,128)S(1)}, bf16[8,128,2304]{2,1,0:T(8,128)(2,1)S(1)}) custom-call(bf16[72,9216]{1,0:T(8,128)(2,1)S(1)} %copy-done.3, bf16[72,9216]{1,0:T(8,128)(2,1)S(1)} %copy-done.4, ...), custom_call_target="tpu_custom_call" | custom-call | tf_op jit(solution)/shard_map/pallas_call | solution.py:520
  167.7 3.3 multiply_reduce_fusion
  171.3 3.5 fusion.1
  174.8 7.6 fusion.19
  189.2 3.6 convolution_convert_fusion.4
  192.7 55.1 %shard_map.229 = f32[128,2304]{1,0:T(8,128)} custom-call(bf16[8,128,2304]{2,1,0:T(8,128)(2,1)} %bitcast.80), custom_call_target="tpu_custom_call" | custom-call | tf_op jit(solution)/shard_map/pallas_call | solution.py:327
  252.0 47.7 %shard_map.230 = bf16[8,128,2304]{2,1,0:T(8,128)(2,1)} custom-call(bf16[128,2304]{1,0:T(8,128)(2,1)} %multiply_convert_fusion.4.x_ref), custom_call_target="tpu_custom_call" | custom-call | tf_op jit(solution)/shard_map/pallas_call | solution.py:242
  299.8 15.0 %fusion.4 = f32[1024,2304]{1,0:T(8,128)S(1)} fusion(bf16[1024,2304]{1,0:T(8,128)(2,1)} %bitcast.88, bf16[2304,3072]{1,0:T(8,128)(2,1)} %bitcast.103), kind=kOutput, calls=%fused_computation.8 | convolution fusion | flops 10871635968 | bytes 24772608 | tf_op jit(solution)/shard_map/dot_general | solution.py:69
  318.4 8.3 convolution_convert_fusion.3
  326.7 48.9 %shard_map.231 = f32[128,2304]{1,0:T(8,128)} custom-call(bf16[8,128,2304]{2,1,0:T(8,128)(2,1)} %bitcast.86), custom_call_target="tpu_custom_call" | custom-call | tf_op jit(solution)/shard_map/pallas_call | solution.py:327
  379.0 2.8 fusion.32
  381.8 45.7 %shard_map.232 = bf16[8,128,2304]{2,1,0:T(8,128)(2,1)} custom-call(bf16[128,2304]{1,0:T(8,128)(2,1)} %get-tuple-element.60.x_ref), custom_call_target="tpu_custom_call" | custom-call | tf_op jit(solution)/shard_map/pallas_call | solution.py:242
  427.6 15.6 %fusion.15 = (bf16[1024,1152]{1,0:T(8,128)(2,1)S(1)}, bf16[1024,1152]{1,0:T(8,128)(2,1)}) fusion(f32[1024,2304]{1,0:T(8,128)} %copy-done.12, bf16[1024,2304]{1,0:T(8,128)(2,1)} %bitcast.92, bf16[1152,2304]{1,0:T(8,128)(2,1)S(1)} %bitcast.79), kind=kOutput, calls=%fused_computation.23 | convolution fusion | flops 5464129536 | bytes 24182784 | tf_op jit(solution)/shard_map/dot_general | solution.py:65
  443.2 7.6 convolution_convert_fusion.1
  450.7 15.0 %fusion.6 = bf16[1024,2304]{1,0:T(8,128)(2,1)} fusion(bf16[2304,3072]{1,0:T(8,128)(2,1)} %bitcast.104, bf16[1024,1152]{1,0:T(8,128)(2,1)S(1)} %copy-done.43, bf16[1024,1152]{1,0:T(8,128)(2,1)S(1)} %get-tuple-element.54), kind=kOutput, calls=%fused_computation.13 | convolution fusion | flops 10883432448 | bytes 20054016 | tf_op jit(solution)/shard_map/dot_general | solution.py:65
  465.7 46.3 %shard_map.233 = f32[128,2304]{1,0:T(8,128)} custom-call(bf16[8,128,2304]{2,1,0:T(8,128)(2,1)} %bitcast.87), custom_call_target="tpu_custom_call" | custom-call | tf_op jit(solution)/shard_map/pallas_call | solution.py:327
  517.2 14.1 %convolution_convert_fusion = bf16[2304,2304]{1,0:T(8,128)(2,1)} fusion(bf16[1024,2304]{1,0:T(8,128)(2,1)S(1)} %bitcast.91, bf16[1024,1152]{1,0:T(8,128)(2,1)S(1)} %copy-done.44, bf16[1024,1152]{1,0:T(8,128)(2,1)S(1)} %copy-done.42), kind=kOutput, calls=%fused_computation | convolution fusion | flops 10886381568 | bytes 20054016 | tf_op jit(solution)/shard_map/dot_general | solution.py:61
  531.3 57.8 %shard_map.234 = bf16[8,128,2304]{2,1,0:T(8,128)(2,1)} custom-call(bf16[128,2304]{1,0:T(8,128)(2,1)} %multiply_convert_fusion.3.x_ref), custom_call_target="tpu_custom_call" | custom-call | tf_op jit(solution)/shard_map/pallas_call | solution.py:242
  589.1 3.9 fusion.42
  595.5 3.0 multiply_convert_fusion.2
  611.5 7.8 convolution_convert_fusion.2
  619.3 5.4 convolution_convert_fusion.5
  624.7 55.3 %shard_map.235 = f32[128,2304]{1,0:T(8,128)} custom-call(bf16[8,128,2304]{2,1,0:T(8,128)(2,1)} %bitcast.85), custom_call_target="tpu_custom_call" | custom-call | tf_op jit(solution)/shard_map/pallas_call | solution.py:327
  684.9 144.6 %shard_map.236 = (f32[72,9216]{1,0:T(8,128)}, f32[72,9216]{1,0:T(8,128)}, f32[72,2048]{1,0:T(8,128)}, f32[72,1024]{1,0:T(8,128)}, f32[72,1024]{1,0:T(8,128)}, /*...) custom-call(bf16[32,72,2304]{2,1,0:T(8,128)(2,1)} %bitcast.81, bf16[32,72,768]{2,1,0:T(8,128)(2,1)} %bitcast.96, ...), custom_call_target="tpu_custom_call" | custom-call | tf_op jit(solution)/shard_map/pallas_call | solution.py:723
  (160 shorter events, 71.2 us)
Async XLA Ops:
  174.8 7.6 copy-start.14
  182.4 3.8 copy-start.24
  189.2 3.6 copy-start.20
  192.7 56.6 %copy-start.2 = (bf16[1,128,2304]{2,1,0:T(8,128)(2,1)S(1)}, bf16[1,128,2304]{2,1,0:T(8,128)(2,1)}, u32[]{:S(2)}) copy-start(bf16[1,128,2304]{2,1,0:T(8,128)(2,1)} %param.13) | copy-start | bytes 1769476
  249.3 50.4 %copy-start.35 = (f32[128]{0:T(128)}, f32[128]{0:T(128)S(1)}, u32[]{:S(2)}) copy-start(f32[128]{0:T(128)S(1)} %add_rsqrt_fusion.3) | copy-start | bytes 1540
  252.0 66.4 %slice-start = ((s8[5308416]{0:T(1024)(128)(4,1)}), s8[4194304]{0:T(1024)(128)(4,1)S(1)}, s32[]{:S(2)}) async-start(s8[5308416]{0:T(1024)(128)(4,1)} %bitcast.76), calls=%async_computation | async-start | bytes 8388608
  299.7 18.7 %slice-start.1 = ((s8[5308416]{0:T(1024)(128)(4,1)}), s8[1114112]{0:T(1024)(128)(4,1)S(1)}, s32[]{:S(2)}) async-start(s8[5308416]{0:T(1024)(128)(4,1)} %bitcast.76), calls=%async_computation.1 | async-start | bytes 2228224
  314.8 3.6 copy-start.12
  318.4 8.3 copy-start.22
  427.5 15.6 %copy-start.15 = (bf16[8,128,2304]{2,1,0:T(8,128)(2,1)S(1)}, bf16[8,128,2304]{2,1,0:T(8,128)(2,1)}, u32[]{:S(2)}) copy-start(bf16[8,128,2304]{2,1,0:T(8,128)(2,1)} %shard_map.232) | copy-start | bytes 14155780
  427.6 15.6 %copy-start.23 = (bf16[1024,1152]{1,0:T(8,128)(2,1)S(1)}, bf16[1024,1152]{1,0:T(8,128)(2,1)}, u32[]{:S(2)}) copy-start(bf16[1024,1152]{1,0:T(8,128)(2,1)} %copy-done.22) | copy-start | bytes 7077892
  443.1 7.6 copy-start.41
  443.1 7.6 copy-start.43
  465.7 48.2 %copy-start.11 = (f32[128,2304]{1,0:T(8,128)S(1)}, f32[128,2304]{1,0:T(8,128)}, u32[]{:S(2)}) copy-start(f32[128,2304]{1,0:T(8,128)} %shard_map.229) | copy-start | bytes 3538948
  465.7 48.2 %copy-start.13 = (bf16[1,128,2304]{2,1,0:T(8,128)(2,1)S(1)}, bf16[1,128,2304]{2,1,0:T(8,128)(2,1)}, u32[]{:S(2)}) copy-start(bf16[1,128,2304]{2,1,0:T(8,128)(2,1)} %param.25) | copy-start | bytes 1769476
  465.7 48.2 %copy-start.36 = (f32[128]{0:T(128)S(1)}, f32[128]{0:T(128)}, u32[]{:S(2)}) copy-start(f32[128]{0:T(128)} %copy-done.35) | copy-start | bytes 1540
  512.1 5.1 slice-start.4
  531.3 57.8 %copy-start.21 = (f32[1024,256]{0,1:T(8,128)S(1)}, f32[1024,256]{0,1:T(8,128)}, u32[]{:S(2)}) copy-start(f32[1024,256]{0,1:T(8,128)} %copy-done.20) | copy-start | bytes 3145732
  589.1 3.9 copy-start.16
  610.5 8.8 %slice-start.2 = ((s8[4718592]{0:T(1024)(128)(4,1)}), s8[4194304]{0:T(1024)(128)(4,1)S(1)}, s32[]{:S(2)}) async-start(s8[4718592]{0:T(1024)(128)(4,1)} %bitcast.83), calls=%async_computation.2 | async-start | bytes 8388608
  611.5 7.8 slice-start.3
  624.7 55.3 %copy-start.34 = (f32[2304]{0:T(1024)S(1)}, f32[2304]{0:T(1024)}, u32[]{:S(2)}) copy-start(f32[2304]{0:T(1024)} %copy-done.33) | copy-start | bytes 27652
  829.5 8.8 %copy-start.19 = (f32[72,9216]{1,0:T(8,128)S(1)}, f32[72,9216]{1,0:T(8,128)}, u32[]{:S(2)}) copy-start(f32[72,9216]{1,0:T(8,128)} %get-tuple-element.92) | copy-start | bytes 7962628
  831.0 8.9 %copy-start.18 = (f32[72,9216]{1,0:T(8,128)S(1)}, f32[72,9216]{1,0:T(8,128)}, u32[]{:S(2)}) copy-start(f32[72,9216]{1,0:T(8,128)} %get-tuple-element.93) | copy-start | bytes 7962628
  (27 other events, 50.2 us)

commit v3 on v2

--- a/solution.py
+++ b/solution.py
@@ -337,7 +337,275 @@
     )(part.astype(BF).reshape(blocks))
 
 
+TOK = 128
 UNITS = FF // RING
+TILE = 128
+GELU_K = 0.7978845608028654
+GELU_A = 0.044715
+
+
+class SlotGather:
+    def __init__(self, buf, ss, rs):
+        z, core, y, x = my_place()
+        p = ring_index(y, z)
+        self.buf, self.ss, self.rs = buf, ss, rs
+        self.near = (ring_device((p + 1) % RING, core, x), ring_device((p + RING - 1) % RING, core, x))
+        self.pending = []
+
+    def copy(self, direction, step, k):
+        piece = TOK // SUB
+        src = 0 if step == 0 else 2 * step - 1 + direction
+        dst = 7 if step == 3 else 2 * step + 1 + direction
+        return remote(
+            self.buf.at[pl.ds(src * TOK + k * piece, piece)],
+            self.buf.at[pl.ds(dst * TOK + k * piece, piece)],
+            self.ss.at[direction, step, k],
+            self.rs.at[direction, step, k],
+            self.near[direction],
+        )
+
+    def step(self, step):
+        for k in range(SUB):
+            for direction in (0, 1):
+                if step > 0:
+                    self.copy(direction, step - 1, k).wait_recv()
+                if k in ring_parts(direction, step, 3):
+                    c = self.copy(direction, step, k)
+                    c.start()
+                    self.pending.append(c)
+
+    def finish(self):
+        for direction in (0, 1):
+            for k in ring_parts(direction, 3, 3):
+                self.copy(direction, 3, k).wait_recv()
+
+    def drain(self):
+        for c in self.pending:
+            c.wait_send()
+
+
+class SlotScatter:
+    def __init__(self, part, buf, ss, rs):
+        z, core, y, x = my_place()
+        p = ring_index(y, z)
+        self.part, self.buf, self.ss, self.rs = part, buf, ss, rs
+        self.near = (ring_device((p + 1) % RING, core, x), ring_device((p + RING - 1) % RING, core, x))
+        self.pending = []
+
+    def copy(self, direction, step, k, src):
+        rows = pl.ds(k * (TOK // SUB), TOK // SUB)
+        return remote(
+            src,
+            self.buf.at[direction, step, rows],
+            self.ss.at[direction, step, k],
+            self.rs.at[direction, step, k],
+            self.near[direction],
+        )
+
+    def step(self, step):
+        piece = TOK // SUB
+        for k in range(SUB):
+            rows = pl.ds(k * piece, piece)
+            for direction in (0, 1):
+                if k not in ring_parts(direction, step, 0):
+                    continue
+                slot = 7 if step == 0 else 2 * (4 - step) - direction
+                mine = pl.ds(slot * TOK + k * piece, piece)
+                src = self.part.at[mine]
+                if step > 0 and k in ring_parts(direction, step - 1, 0):
+                    src = self.buf.at[direction, step - 1, rows]
+                    self.copy(direction, step - 1, k, src).wait_recv()
+                    src[...] = (src[...].astype(F32) + self.part[mine].astype(F32)).astype(BF)
+                c = self.copy(direction, step, k, src)
+                c.start()
+                self.pending.append(c)
+
+    def finish(self, total):
+        for k in range(SUB):
+            rows = pl.ds(k * (TOK // SUB), TOK // SUB)
+            for direction in (0, 1):
+                src = self.buf.at[direction, 3, rows]
+                self.copy(direction, 3, k, src).wait_recv()
+                total[rows] = total[rows] + src[...].astype(F32)
+
+    def drain(self):
+        for c in self.pending:
+            c.wait_send()
+
+
+def tiles(count, width, body):
+    def step(i, carry):
+        body(pl.ds(pl.multiple_of(i * width, width), width))
+        return carry
+
+    lax.fori_loop(0, count, step, 0)
+
+
+def gelu_parts(v):
+    bent = jnp.tanh(GELU_K * (v + GELU_A * (v * v * v)))
+    value = 0.5 * v * (1.0 + bent)
+    slope = 0.5 * (1.0 + bent) + 0.5 * v * (1.0 - bent * bent) * (GELU_K * (1.0 + 3.0 * GELU_A * (v * v)))
+    return value, slope
+
+
+PAIRS = ((128, 256), (384, 256), (640, 256))
+LAST = (896, 128)
+OWN = (0, 128)
+
+
+def feed_forward_kernel(hid, middle, factor, cot, w_hbm, wd_hbm,
+                        out_o, d_hid_o, gain_o, wd_grad, gu_grad,
+                        wgu, wd, ha, gu, act, part, buf, df, dgu, total, stage,
+                        w_sem, ags, agr, rss, rsr, out_sem):
+    gather = [SlotGather(b, ags.at[i], agr.at[i]) for i, b in enumerate((ha, df))]
+    scatter = [SlotScatter(part, buf, rss.at[i], rsr.at[i]) for i in range(2)]
+    greet(gather[0].near)
+    loads = [
+        pltpu.make_async_copy(w_hbm.at[:, pl.ds(0, 2 * UNITS)], wgu, w_sem.at[0]),
+        pltpu.make_async_copy(wd_hbm, wd, w_sem.at[1]),
+    ]
+    ha[0:TOK] = hid[...]
+    gather[0].step(0)
+    for c in loads:
+        c.start()
+    loads[0].wait()
+
+    def gate_up(first, count):
+        rows = pl.ds(first, count)
+
+        def column(cols):
+            gu[rows, cols] = fold_rows(ha[rows], wgu[:, cols])
+
+        tiles(3, 768, column)
+
+        def finish(i, carry):
+            r = pl.ds(pl.multiple_of(first + i * 32, 32), 32)
+            act[r] = (gelu_parts(gu[r, 0:UNITS])[0] * gu[r, UNITS : 2 * UNITS]).astype(BF)
+            return carry
+
+        lax.fori_loop(0, count // 32, finish, 0)
+
+    def down_part(first, count, dst):
+        def column(cols):
+            value = fold_rows(act[pl.ds(first, count)], wd[:, cols])
+            dst[pl.ds(first, count), cols] = value.astype(dst.dtype)
+
+        tiles(3, 768, column)
+
+    def active_back(first, count):
+        rows = pl.ds(first, count)
+        for n in range(3):
+            cols, up_cols = pl.ds(n * 384, 384), pl.ds(UNITS + n * 384, 384)
+            d_active = contract_cols(df[rows], wd[cols])
+            value, slope = gelu_parts(gu[rows, cols])
+            dgu[rows, cols] = (d_active * gu[rows, up_cols] * slope).astype(BF)
+            dgu[rows, up_cols] = (d_active * value).astype(BF)
+
+    def hidden_part(first, count, dst):
+        def column(cols):
+            value = contract_cols(dgu[pl.ds(first, count)], wgu[cols])
+            dst[pl.ds(first, count), cols] = value.astype(dst.dtype)
+
+        tiles(9, 256, column)
+
+    n_down = UNITS // TILE
+
+    def grad_out(i):
+        slot = i % 2
+        if i < n_down:
+            return pltpu.make_async_copy(stage.at[slot], wd_grad.at[pl.ds(i * TILE, TILE)], out_sem.at[slot])
+        return pltpu.make_async_copy(stage.at[slot], gu_grad.at[pl.ds((i - n_down) * TILE, TILE)], out_sem.at[slot])
+
+    def grad_tiles(first, last):
+        for i in range(first, last):
+            if i >= 2:
+                grad_out(i - 2).wait()
+            if i < n_down:
+                value = contract_rows(act[:, pl.ds(i * TILE, TILE)], df[...])
+            else:
+                value = contract_rows(ha[:, pl.ds((i - n_down) * TILE, TILE)], dgu[...])
+            stage[i % 2] = value.astype(BF)
+            grad_out(i).start()
+
+    gate_up(*OWN)
+    for step, pair in enumerate(PAIRS):
+        gather[0].step(step + 1)
+        if step == 0:
+            loads[1].wait()
+        gate_up(*pair)
+    gather[0].finish()
+    gate_up(*LAST)
+    down_part(*LAST, part)
+    scatter[0].step(0)
+    for step, pair in enumerate(PAIRS[::-1]):
+        down_part(*pair, part)
+        scatter[0].step(step + 1)
+    down_part(*OWN, total)
+    scatter[0].finish(total)
+    gather[0].drain()
+    scatter[0].drain()
+
+    branch = total[...]
+    inverse, normed = rms_parts(branch)
+    out_cot = cot[...].astype(F32)
+    scale = factor[...]
+    df[0:TOK] = norm_back(out_cot * scale, normed, inverse).astype(BF)
+    gather[1].step(0)
+    out_o[...] = (middle[...] + normed * scale).astype(BF)
+    gain_o[...] = jnp.sum(out_cot * normed, axis=0, keepdims=True)
+    active_back(*OWN)
+    for step, pair in enumerate(PAIRS):
+        gather[1].step(step + 1)
+        active_back(*pair)
+    gather[1].finish()
+    active_back(*LAST)
+    hidden_part(*LAST, part)
+    scatter[1].step(0)
+    done = 0
+    for step, pair in enumerate(PAIRS[::-1]):
+        hidden_part(*pair, part)
+        scatter[1].step(step + 1)
+        grad_tiles(done, done + 6)
+        done += 6
+    hidden_part(*OWN, d_hid_o)
+    scatter[1].finish(d_hid_o)
+    n_tiles = n_down + ha.shape[1] // TILE
+    grad_tiles(done, n_tiles)
+    for i in (n_tiles - 2, n_tiles - 1):
+        grad_out(i).wait()
+    gather[1].drain()
+    scatter[1].drain()
+
+
+def feed_forward(hidden_ffn, middle, factor, out_grad, w_in, w_down, collective_id):
+    rows, width = hidden_ffn.shape
+    total = RING * rows
+
+    def full(*shape, dtype=F32):
+        return jax.ShapeDtypeStruct(shape, dtype)
+
+    return pl.pallas_call(
+        feed_forward_kernel,
+        out_shape=[
+            full(rows, width, dtype=BF), full(rows, width), full(1, width),
+            full(UNITS, width, dtype=BF), full(width, 2 * UNITS, dtype=BF),
+        ],
+        in_specs=[VMEM] * 4 + [HBM] * 2,
+        out_specs=[VMEM] * 3 + [HBM] * 2,
+        scratch_shapes=[
+            pltpu.VMEM((width, 2 * UNITS), BF), pltpu.VMEM((UNITS, width), BF),
+            pltpu.VMEM((total, width), BF), pltpu.VMEM((total, 2 * UNITS), F32), pltpu.VMEM((total, UNITS), BF),
+            pltpu.VMEM((total, width), BF), pltpu.VMEM((2, 4, rows, width), BF),
+            pltpu.VMEM((total, width), BF), pltpu.VMEM((total, 2 * UNITS), BF),
+            pltpu.VMEM((rows, width), F32), pltpu.VMEM((2, TILE, width), BF),
+            DMA((2,)),
+            DMA((2, 2, 4, SUB)), DMA((2, 2, 4, SUB)), DMA((2, 2, 4, SUB)), DMA((2, 2, 4, SUB)),
+            DMA((2,)),
+        ],
+        compiler_params=params(collective_id, 60),
+    )(hidden_ffn, middle, factor, out_grad, w_in, w_down)
+
+
 WIDTHS = (UNITS, UNITS, HD, HD, HD)
 STARTS = (0, UNITS, 2 * UNITS, 2 * UNITS + HD, 2 * UNITS + 2 * HD)
 WIDE = 2 * UNITS + 3 * HD
@@ -787,7 +1055,7 @@
         w_gate, w_up, w_query, w_key, w_value, w_down, w_out, gains, tokens[0], next(ids)
     )
     w_in = w_in.reshape(-1, WIDE)
-    w_gu, w_qkv = w_in[:, : 2 * UNITS], w_in[:, 2 * UNITS :]
+    w_qkv = w_in[:, 2 * UNITS :]
     w_dn = down_in.reshape(UNITS, D)
     w_ot = out_in.reshape(HD, D)
     factors = 1.0 + jnp.transpose(gains_in[:, :4, :shard_gain], (1, 0, 2)).reshape(4, D)
@@ -809,25 +1077,12 @@
     inv_post, normed_post = rms_parts(branch)
     middle = resid_in + normed_post * post_factor
     inv_mid, normed_mid = rms_parts(middle)
-    hidden_ffn = ring_gather((normed_mid * pre_ffn_factor).astype(BF), next(ids), False)
-    gate_up = fold_rows(hidden_ffn, w_gu)
-    gate_lin, up_lin = gate_up[:, :UNITS], gate_up[:, UNITS:]
-    active = gated(gate_lin, up_lin).astype(BF)
-    ffn_branch = ring_scatter(fold_rows(active, w_dn), next(ids), False)
-    inv_ffn, normed_ffn = rms_parts(ffn_branch)
-    output = (middle + normed_ffn * post_ffn_factor).astype(BF)
-
+    hidden_ffn = (normed_mid * pre_ffn_factor).astype(BF)
+    output, d_hidden_ffn, post_ffn_part, down_part, gu_part = feed_forward(
+        hidden_ffn, middle, post_ffn_factor[None], out_grad[0], w_in, w_dn, next(ids)
+    )
+    post_ffn_part = post_ffn_part[0]
     out_cot = out_grad[0].astype(F32)
-    post_ffn_part = jnp.sum(out_cot * normed_ffn, axis=0)
-    d_ffn = norm_back(out_cot * post_ffn_factor, normed_ffn, inv_ffn).astype(BF)
-    d_ffn = ring_gather(d_ffn, next(ids), False)
-    down_part = contract_rows(active, d_ffn)
-    d_active = contract_cols(d_ffn, w_dn)
-    unused_value, gate_pull = jax.vjp(gated, gate_lin, up_lin)
-    d_gate, d_up = gate_pull(d_active)
-    d_gu = jnp.concatenate([d_gate.astype(BF), d_up.astype(BF)], axis=1)
-    d_hidden_ffn = ring_scatter(contract_cols(d_gu, w_gu), next(ids), False)
-    gu_part = contract_rows(hidden_ffn, d_gu)
     pre_ffn_part = jnp.sum(d_hidden_ffn * normed_mid, axis=0)
     d_middle = out_cot + norm_back(d_hidden_ffn * pre_ffn_factor, normed_mid, inv_mid)
     post_part = jnp.sum(d_middle * normed_post, axis=0)
@@ -852,7 +1107,7 @@
     token_grad = d_middle + norm_back(d_hidden * pre_factor, normed_pre, inv_pre)
     gain_parts = jnp.pad(jnp.stack([pre_part, post_part, pre_ffn_part, post_ffn_part]), ((0, 4), (0, 0)))
     results = weights_out(
-        gu_part.astype(BF), qkv_part.astype(BF), down_part.astype(BF), out_part.astype(BF),
+        gu_part, qkv_part.astype(BF), down_part, out_part.astype(BF),
         gain_parts, next(ids),
     )
     gate_g, up_g, query_g, key_g, value_g, down_g, out_g, gain_g = results

time: 851 us -> 775 us (0.911)
  matrix products: 115 us -> 39.9 us
  Pallas kernels: 654 us -> 666 us
  other arithmetic: 41.2 us -> 31.8 us
    pallas_call x0 -> x1, Pallas kernels: none -> 203 us  [feed_forward(): pl.pallas_call(feed_forward_kernel, out_shape=[full(rows, width, dtype=BF...]
    pallas_call x3 -> x1, Pallas kernels: 151 us -> 54.6 us  [ring_gather(): pl.pallas_call(functools.partial(gather_kernel, paired), out_shape=whole,...]
    pallas_call x4 -> x2, Pallas kernels: 206 us -> 110 us  [ring_scatter(): pl.pallas_call(functools.partial(scatter_kernel, paired), out_shape=jax.S...]
    dot_general x6 -> x4, matrix products: 46.3 us -> 16.4 us  [contract_cols(): lax.dot_general(left, right, (((1,), (1,)), ((), ())), preferred_element_...]
    dot_general x6 -> x4, matrix products: 36.2 us -> 12.9 us  [fold_rows(): return jnp.dot(left, right, preferred_element_type=F32)]
    dot_general x7 -> x5, matrix products: 32.2 us -> 10.6 us  [contract_rows(): lax.dot_general(left, right, (((0,), (0,)), ((), ())), preferred_element_...]
    unnamed x109 -> x128, local copies, waits for them, and re-layouts: 29.7 us -> 25.7 us
where the time goes in v3:
time: 775 us; the launch traced here: 768 us
  Pallas kernels  666 us (86%)
  matrix products  39.9 us (5%)
  other arithmetic  31.8 us (4%)
  local copies, waits for them, and re-layouts  28.3 us (4%)
    pallas_call x1, Pallas kernels, feed_forward(): pl.pallas_call(feed_forward_kernel, out_shape=[full(rows, width, dtype=BF...  203 us
    pallas_call x1, Pallas kernels, weights_in(): pl.pallas_call(weights_in_kernel, out_shape=shapes, in_specs=[VMEM] * 9,...  153 us
    pallas_call x1, Pallas kernels, weights_out(): pl.pallas_call(weights_out_kernel, out_shape=[full(rows, FF), full(rows,...  145 us
    pallas_call x2, Pallas kernels, ring_scatter(): pl.pallas_call(functools.partial(scatter_kernel, paired), out_shape=jax.S...  110 us
    pallas_call x1, Pallas kernels, ring_gather(): pl.pallas_call(functools.partial(gather_kernel, paired), out_shape=whole,...  54.6 us
    unnamed x128, local copies, waits for them, and re-layouts  25.7 us
    dot_general x4, matrix products, contract_cols(): lax.dot_general(left, right, (((1,), (1,)), ((), ())), preferred_element_...  16.4 us

profile of v3, /device:TPU:1, one launch (start us, length us, event | category | flops | bytes accessed | tf_op | source)
XLA Modules:
  0.0 767.7 jit_solution(9198644146539904016)
XLA Ops:
  10.1 152.7 %shard_map.228 = (bf16[32,72,3072]{2,1,0:T(8,128)(2,1)}, bf16[4,288,2304]{2,1,0:T(8,128)(2,1)S(1)}, bf16[4,64,2304]{2,1,0:T(8,128)(2,1)S(1)}, f32[32,8,128]{2,1,0:T(8,128)S(1)}, bf16[8,128,2304]{2,1,0:T(8,128)(2,1)S(1)}) custom-call(bf16[72,9216]{1,0:T(8,128)(2,1)S(1)} %copy-done.5, bf16[72,9216]{1,0:T(8,128)(2,1)S(1)} %copy-done.6, ...), custom_call_target="tpu_custom_call" | custom-call | tf_op jit(solution)/shard_map/pallas_call | solution.py:788
  162.9 2.1 copy-done
  165.0 2.3 copy-done.4
  167.6 3.5 multiply_reduce_fusion
  172.5 7.6 fusion.5
  180.1 2.6 fusion.41
  185.9 3.6 convolution_convert_fusion.1
  189.5 55.1 %shard_map.229 = f32[128,2304]{1,0:T(8,128)} custom-call(bf16[8,128,2304]{2,1,0:T(8,128)(2,1)} %bitcast.60), custom_call_target="tpu_custom_call" | custom-call | tf_op jit(solution)/shard_map/pallas_call | solution.py:327
  250.2 203.2 %shard_map.230 = (bf16[128,2304]{1,0:T(8,128)(2,1)}, f32[128,2304]{1,0:T(8,128)}, f32[1,2304]{1,0:T(1,128)}, bf16[1152,2304]{1,0:T(8,128)(2,1)}, bf16[2304,2304]{1,0:T(8,128)(2,1)}) custom-call(bf16[128,2304]{1,0:T(8,128)(2,1)} %multiply_convert_fusion.2.hid, f32[128,2304]{1,0:T(8,128)} %copy-done.12, f32[1,2304]{1,0:T(1,128)} %slice.81.factor, ...), custom_call_target="tpu_custom_call" | custom-call | tf_op jit(solution)/shard_map/pallas_call | solution.py:587
  453.5 2.2 multiply_reduce_fusion.1
  455.8 2.0 multiply_reduce_fusion.2
  458.9 54.6 %shard_map.231 = bf16[8,128,2304]{2,1,0:T(8,128)(2,1)} custom-call(bf16[128,2304]{1,0:T(8,128)(2,1)} %multiply_convert_fusion.1.x_ref), custom_call_target="tpu_custom_call" | custom-call | tf_op jit(solution)/shard_map/pallas_call | solution.py:242
  513.6 3.9 fusion.22
  518.5 3.0 multiply_convert_fusion
  523.3 2.2 fusion.64
  525.6 2.2 fusion.63
  527.8 2.2 fusion.62
  530.1 2.2 fusion.61
  533.4 8.4 %convolution_convert_fusion = bf16[1024,2304]{1,0:T(8,128)(2,1)} fusion(bf16[1024,768]{0,1:T(8,128)(2,1)S(1)} %fusion.11, bf16[2304,3072]{1,0:T(8,128)(2,1)} %bitcast.63), kind=kOutput, calls=%fused_computation.4 | convolution fusion | flops 3626237952 | bytes 9830400 | tf_op jit(solution)/shard_map/dot_general | solution.py:65
  541.8 55.4 %shard_map.232 = f32[128,2304]{1,0:T(8,128)} custom-call(bf16[8,128,2304]{2,1,0:T(8,128)(2,1)} %bitcast.68), custom_call_target="tpu_custom_call" | custom-call | tf_op jit(solution)/shard_map/pallas_call | solution.py:327
  597.2 2.3 fusion.19
  600.3 2.4 convolution_convert_fusion.3
  602.7 5.5 convolution_convert_fusion.2
  608.3 145.1 %shard_map.233 = (f32[72,9216]{1,0:T(8,128)}, f32[72,9216]{1,0:T(8,128)}, f32[72,2048]{1,0:T(8,128)}, f32[72,1024]{1,0:T(8,128)}, f32[72,1024]{1,0:T(8,128)}, /*...) custom-call(bf16[32,72,2304]{2,1,0:T(8,128)(2,1)} %bitcast.64, bf16[32,72,768]{2,1,0:T(8,128)(2,1)} %bitcast.73, ...), custom_call_target="tpu_custom_call" | custom-call | tf_op jit(solution)/shard_map/pallas_call | solution.py:991
  (162 shorter events, 39.6 us)
Async XLA Ops:
  167.6 3.8 copy-start.1
  172.5 7.6 copy-start.16
  180.1 3.9 copy-start.24
  180.1 3.7 copy-start.44
  189.5 56.6 %copy-start.3 = (bf16[1,128,2304]{2,1,0:T(8,128)(2,1)S(1)}, bf16[1,128,2304]{2,1,0:T(8,128)(2,1)}, u32[]{:S(2)}) copy-start(bf16[1,128,2304]{2,1,0:T(8,128)(2,1)} %param.13) | copy-start | bytes 1769476
  246.1 4.0 copy-start.38
  250.2 203.3 %copy-start.41 = (f32[2304]{0:T(1024)S(1)}, f32[2304]{0:T(1024)}, u32[]{:S(2)}) copy-start(f32[2304]{0:T(1024)} %copy-done.40) | copy-start | bytes 27652
  250.2 203.3 %copy-start.48 = (f32[128]{0:T(128)S(1)}, f32[128]{0:T(128)}, u32[]{:S(2)}) copy-start(f32[128]{0:T(128)} %copy-done.47) | copy-start | bytes 1540
  250.2 205.5 %copy-start.23 = (bf16[1,128,2304]{2,1,0:T(8,128)(2,1)S(1)}, bf16[1,128,2304]{2,1,0:T(8,128)(2,1)}, u32[]{:S(2)}) copy-start(bf16[1,128,2304]{2,1,0:T(8,128)(2,1)} %param.25) | copy-start | bytes 1769476
  250.2 205.5 %copy-start.39 = (f32[2304]{0:T(1024)S(1)}, f32[2304]{0:T(1024)}, u32[]{:S(2)}) copy-start(f32[2304]{0:T(1024)} %copy-done.38) | copy-start | bytes 27652
  250.2 205.5 %copy-start.51 = (f32[128]{0:T(128)S(1)}, f32[128]{0:T(128)}, u32[]{:S(2)}) copy-start(f32[128]{0:T(128)} %copy-done.50) | copy-start | bytes 1540
  458.9 54.6 %copy-start.21 = (f32[1024,256]{0,1:T(8,128)S(1)}, f32[1024,256]{0,1:T(8,128)}, u32[]{:S(2)}) copy-start(f32[1024,256]{0,1:T(8,128)} %copy-done.20) | copy-start | bytes 3145732
  513.6 3.9 copy-start.53
  513.6 3.9 copy-start.55
  532.3 67.9 %slice-start.2 = ((s8[4718592]{0:T(1024)(128)(4,1)}), s8[4194304]{0:T(1024)(128)(4,1)S(1)}, s32[]{:S(2)}) async-start(s8[4718592]{0:T(1024)(128)(4,1)} %bitcast.70), calls=%async_computation.2 | async-start | bytes 8388608
  533.3 8.4 %copy-start.42 = (bf16[1024,768]{0,1:T(8,128)(2,1)}, bf16[1024,768]{0,1:T(8,128)(2,1)S(1)}, u32[]{:S(2)}) copy-start(bf16[1024,768]{0,1:T(8,128)(2,1)S(1)} %fusion.11) | copy-start | bytes 4718596
  533.3 66.9 %slice-start.3 = ((s8[4718592]{0:T(1024)(128)(4,1)}), s8[524288]{0:T(1024)(128)(4,1)S(1)}, s32[]{:S(2)}) async-start(s8[4718592]{0:T(1024)(128)(4,1)} %bitcast.70), calls=%async_computation.3 | async-start | bytes 1048576
  541.8 55.4 %copy-start.49 = (f32[128]{0:T(128)S(1)}, f32[128]{0:T(128)}, u32[]{:S(2)}) copy-start(f32[128]{0:T(128)} %get-tuple-element.75) | copy-start | bytes 1540
  541.8 57.8 %copy-start.46 = (f32[1,2304]{1,0:T(1,128)S(1)}, f32[1,2304]{1,0:T(1,128)}, u32[]{:S(2)}) copy-start(f32[1,2304]{1,0:T(1,128)} %get-tuple-element.40) | copy-start | bytes 27652
  541.8 58.5 %copy-start.22 = (f32[1024,256]{0,1:T(8,128)S(1)}, f32[1024,256]{0,1:T(8,128)}, u32[]{:S(2)}) copy-start(f32[1024,256]{0,1:T(8,128)} %copy-done.20) | copy-start | bytes 3145732
  597.2 5.5 slice-start
  608.3 147.2 %copy-start.15 = (f32[128,2304]{1,0:T(8,128)S(1)}, f32[128,2304]{1,0:T(8,128)}, u32[]{:S(2)}) copy-start(f32[128,2304]{1,0:T(8,128)} %shard_map.232) | copy-start | bytes 3538948
  753.4 4.1 copy-start.27
  756.6 3.9 copy-start.19
  (36 other events, 69.7 us)

commit v4 on v3

--- a/solution.py
+++ b/solution.py
@@ -805,60 +805,106 @@
     return list(results[:4]) + [results[4].reshape(RING * block.shape[0], block.shape[1])]
 
 
-def add_into(dst, index, src, other):
-    dst[index] = (dst[index].astype(F32) + src[other].astype(F32)).astype(BF)
-
-
-def weights_out_kernel(gu_in, qkv_in, down_in, out_in, gain_in,
-                       gate_o, up_o, query_o, key_o, value_o, down_o, out_o, gain_o,
-                       a_buf, b_buf, c_buf, acc, da, db, dacc, dd, oa, ob, oacc, od, ga, gsum,
-                       loc, sa, ra, sb, rb, sc, rc, sx, rx, sg, rg):
+ROUNDS = (4, 5, 6, 7, 2, 3, 1, 0)
+AHEAD = 2
+
+
+def slot_of(q, p):
+    d = (q - p + RING) % RING
+    return jnp.where(d == 0, 0, jnp.where(d < 4, 2 * d, jnp.where(d == 4, 7, 15 - 2 * d)))
+
+
+def backward_kernel(d_branch, gu_in, down_in, hidden, w_hbm, wo, q_in, k_in, v_in, att, inv, cos, sine, normed, gain_in,
+                    d_hid_o, gain_o, c_gu, c_q, down_o, out_o,
+                    ring, seq, part, buf, wq, d_att, d_qkv, dk, dv, grad_q, aq, bq,
+                    own, a_gu, b_gu, down_own, da, db, og, oa, ob, ga, gsum,
+                    load, ags, agr, pls, plr, rss, rsr, sws, swr, s1, r1, s2, r2, s3, r3,
+                    q1, t1, q2, t2, q3, t3, sx, rx, sg, rg):
     z, core, y, x = my_place()
-    t = 2 * z + y
+    t, p = 2 * z + y, ring_index(y, z)
     sibling, across = device(z, 1 - core, y, x), device(z, core, y, 1 - x)
     diagonal = device(z, 1 - core, 1 - y, x)
-    others = [(t + j) % RING for j in range(1, RING)]
-    greet([member_place(tq, core, x) for tq in others] + [sibling, across, diagonal])
-
-    def slot(tq, corq, xq):
+    members = [member_place(partner(t, j), core, x) for j in range(RING)]
+    order = [partner(t, j) for j in ROUNDS]
+    greet(members[1:] + [sibling, across, diagonal])
+    pending = []
+
+    def go(*copies):
+        for c in copies:
+            c.start()
+            pending.append(c)
+
+    def owner(tq, corq, xq):
         return (2 * (tq // 2) + corq) * 4 + 2 * (tq % 2) + xq
 
-    def load(tq, xq):
-        i = slot(tq, core, xq)
-        return [
-            pltpu.make_async_copy(gu_in.at[i], acc.at[xq, tq, :, pl.ds(0, 2 * UNITS)], loc.at[xq, tq, 0]),
-            pltpu.make_async_copy(qkv_in.at[i], acc.at[xq, tq, :, pl.ds(2 * UNITS, 3 * HD)], loc.at[xq, tq, 1]),
-        ]
-
-    def to_sibling(tq, xq):
-        i = slot(tq, 1 - core, xq)
-        return [
-            remote(gu_in.at[i], a_buf.at[xq, tq, :, pl.ds(0, 2 * UNITS)], sa.at[xq, tq, 0], ra.at[xq, tq, 0], sibling),
-            remote(qkv_in.at[i], a_buf.at[xq, tq, :, pl.ds(2 * UNITS, 3 * HD)], sa.at[xq, tq, 1], ra.at[xq, tq, 1], sibling),
-        ]
-
-    def to_across(tq):
-        return remote(acc.at[1 - x, tq], b_buf.at[tq], sb.at[tq], rb.at[tq], across)
-
-    def to_member(tq, wait=False):
-        return remote(acc.at[x, tq], c_buf.at[tq if wait else t], sc.at[tq], rc.at[tq if wait else t], member_place(tq, core, x))
-
-    order = [partner(t, j) for j in (4, 5, 6, 7, 2, 3, 1, 0)]
-
-    small = ((down_in, da, db, dacc, dd, down_o), (out_in, oa, ob, oacc, od, out_o))
+    side_x = (1 - x, x)
+
+    def gu_a(side, j):
+        src = gu_in.at[owner(order[j], 1 - core, side_x[side])]
+        return remote(src, a_gu.at[side, j], s1.at[side, j], r1.at[side, j], sibling)
+
+    def gu_own(side, j):
+        return pltpu.make_async_copy(gu_in.at[owner(order[j], core, side_x[side])], own.at[j % 2], load.at[j % 2])
+
+    def gu_b(j):
+        return remote(a_gu.at[0, j], b_gu.at[j], s2.at[j], r2.at[j], across)
+
+    def gu_c(j, wait=False):
+        dst = c_gu.at[order[j] if wait else t]
+        if ROUNDS[j] == 0:
+            return pltpu.make_async_copy(a_gu.at[1, j], dst, load.at[2])
+        return remote(a_gu.at[1, j], dst, s3.at[j], r3.at[j], members[ROUNDS[j]])
+
+    def sum_own(side, j, more=None):
+        gu_own(side, j).wait()
+        gu_a(side, j).wait_recv()
+        total = a_gu[side, j].astype(F32) + own[j % 2].astype(F32)
+        if more is not None:
+            total = total + more[j].astype(F32)
+        a_gu[side, j] = total.astype(BF)
+
+    def pump(first, last):
+        for j in range(first, last):
+            gu_own(1, j).start()
+        for j in range(first, last):
+            gu_b(j).wait_recv()
+            if j + AHEAD < RING:
+                go(gu_b(j + AHEAD))
+            sum_own(1, j, b_gu)
+
+    small = ((down_in, down_own, da, db, down_o), (og, None, oa, ob, out_o))
 
     def small_a(a, xo):
-        src, buf = small[a][0], small[a][1]
-        return remote(src.at[2 * (1 - core) + xo], buf.at[xo], sx.at[a, xo], rx.at[a, xo], sibling)
+        return remote(small[a][0].at[2 * (1 - core) + xo], small[a][2].at[xo], sx.at[a, xo], rx.at[a, xo], sibling)
 
     def small_b(a):
-        return remote(small[a][3].at[1 - x], small[a][2], sx.at[a, 2], rx.at[a, 2], across)
-
-    def small_c(a):
-        return remote(small[a][3].at[x], small[a][4], sx.at[a, 3], rx.at[a, 3], diagonal)
-
-    def small_load(a, xo):
-        return pltpu.make_async_copy(small[a][0].at[2 * core + xo], small[a][3].at[xo], loc.at[a, xo, 2])
+        return remote(small[a][2].at[1 - x], small[a][3], sx.at[a, 2], rx.at[a, 2], across)
+
+    def small_c(a, act):
+        src, dst = small[a][2].at[x], small[a][4]
+
+        @pl.when(core == y)
+        def _():
+            c = pltpu.make_async_copy(src, dst, load.at[3 + a])
+            c.start() if act == 0 else c.wait()
+
+        @pl.when(core != y)
+        def _():
+            c = remote(src, dst, sx.at[a, 3], rx.at[a, 3], diagonal)
+            c.start() if act == 0 else c.wait()
+
+    def q_a(side, j):
+        src = grad_q.at[owner(order[j], 1 - core, side_x[side])]
+        return remote(src, aq.at[side, j], q1.at[side, j], t1.at[side, j], sibling)
+
+    def q_b(j):
+        return remote(grad_q.at[owner(order[j], core, 1 - x)], bq.at[j], q2.at[j], t2.at[j], across)
+
+    def q_c(j, wait=False):
+        src, dst = grad_q.at[owner(order[j], core, x)], c_q.at[order[j] if wait else t]
+        if ROUNDS[j] == 0:
+            return pltpu.make_async_copy(src, dst, load.at[5])
+        return remote(src, dst, q3.at[j], t3.at[j], members[ROUNDS[j]])
 
     def gain_a():
         return remote(gain_in, ga.at[RING], sg.at[RING], rg.at[RING], sibling)
@@ -866,150 +912,301 @@
     def gain_b():
         return remote(gsum.at[0], ga.at[RING + 1], sg.at[RING + 1], rg.at[RING + 1], across)
 
-    def gain_c(tq, wait=False):
-        return remote(gsum.at[1], ga.at[tq if wait else t], sg.at[tq], rg.at[tq if wait else t], member_place(tq, core, x))
-
-    def start_a(tq, xq):
-        for c in load(tq, xq) + to_sibling(tq, xq):
+    def gain_c(j):
+        return remote(gsum.at[1], ga.at[j], sg.at[j], rg.at[j], members[j])
+
+    gather = SlotGather(ring, ags, agr)
+
+    def block(slot):
+        if slot == 0:
+            return p
+        if slot == 7:
+            return (p + 4) % RING
+        s = (slot + 1) // 2
+        return (p + (RING - s if slot % 2 else s)) % RING
+
+    def place(slot, act):
+        yq, zq = ring_yz(block(slot))
+        src, dst = ring.at[pl.ds(slot * TOK, TOK)], seq.at[2 * zq + core]
+
+        @pl.when(yq == core)
+        def _():
+            c = pltpu.make_async_copy(src, dst, load.at[6 + slot])
+            c.start() if act == 0 else c.wait()
+
+        @pl.when(yq != core)
+        def _():
+            c = remote(src, dst, pls.at[zq], plr.at[zq], sibling)
+            c.start() if act == 0 else c.wait_send()
+
+    first = pltpu.make_async_copy(d_branch, ring.at[pl.ds(0, TOK)], load.at[14])
+    first.start()
+    wq_load = pltpu.make_async_copy(w_hbm.at[:, pl.ds(2 * UNITS, 3 * HD)], wq, load.at[15])
+    first.wait()
+    gather.step(0)
+    place(0, 0)
+    for side in (0, 1):
+        go(*[gu_a(side, j) for j in range(RING)])
+        if side == 0:
+            go(small_a(0, 0), small_a(0, 1))
+    wq_load.start()
+    for j in range(RING):
+        if j < 2:
+            gu_own(0, j).start()
+        sum_own(0, j)
+        if j + 2 < RING:
+            gu_own(0, j + 2).start()
+        if j < AHEAD:
+            go(gu_b(j))
+
+    def down_sum(xo):
+        c = pltpu.make_async_copy(down_in.at[2 * core + xo], down_own, load.at[16])
+        c.start()
+        small_a(0, xo).wait_recv()
+        c.wait()
+        da[xo] = (da[xo].astype(F32) + down_own[...].astype(F32)).astype(BF)
+
+    down_sum(0)
+    gather.step(1)
+    place(1, 0)
+    place(2, 0)
+    pump(0, 1)
+    down_sum(1)
+    pump(1, 2)
+    gather.step(2)
+    place(3, 0)
+    place(4, 0)
+    pump(2, 4)
+    gather.step(3)
+    place(5, 0)
+    place(6, 0)
+    pump(4, 5)
+    gather.finish()
+    place(7, 0)
+    for j in range(5):
+        go(gu_c(j))
+    for zq in range(NZ):
+        dst = seq.at[2 * zq + 1 - core]
+        remote(dst, dst, pls.at[zq], plr.at[zq], sibling).wait_recv()
+    for slot in range(RING):
+        place(slot, 1)
+    gather.drain()
+    hidden_load = pltpu.make_async_copy(hidden, ring, load.at[14])
+    hidden_load.start()
+
+    for c in range(0, RING, 2):
+        rows = pl.ds(c * TOK, 2 * TOK)
+        d_att[rows] = contract_cols(seq[c : c + 2].reshape(2 * TOK, -1), wo[...]).astype(BF)
+
+    def out_columns(cols):
+        value = contract_rows(att[...].astype(BF), seq[:, :, cols].reshape(RING * TOK, 768))
+        for f in range(4):
+            og[f, :, cols] = value[64 * f : 64 * (f + 1)].astype(BF)
+
+    tiles(3, 768, out_columns)
+    go(small_a(1, 0), small_a(1, 1))
+    pump(5, 6)
+    go(gu_c(5))
+    dk[...] = jnp.zeros_like(dk)
+    dv[...] = jnp.zeros_like(dv)
+    for i in range(4):
+        r, upto = pl.ds(i * 256, 256), (i + 1) * 256
+        keys, vals, query = k_in[0:upto], v_in[0:upto], q_in[r]
+        bent = jnp.tanh(contract_cols(query, keys) / CAP)
+        seen = lax.broadcasted_iota(jnp.int32, bent.shape, 1) <= i * 256 + lax.broadcasted_iota(jnp.int32, bent.shape, 0)
+        weights = jnp.where(seen, jnp.exp(CAP * bent), 0.0)
+        grad = d_att[r].astype(F32)
+        delta = jnp.sum(grad * att[r], axis=-1, keepdims=True)
+        d_probs = contract_cols(d_att[r], vals)
+        d_raw = (weights * inv[r] * (d_probs - delta) * (1.0 - bent * bent)).astype(BF)
+        dq = fold_rows(d_raw, keys) * (HD ** (-0.5))
+        d_qkv[r, 0:HD] = unrotate(dq, cos[r], sine[r]).astype(BF)
+        dk[0:upto] = dk[0:upto] + contract_rows(d_raw, query)
+        scaled = grad * inv[r]
+        high = scaled.astype(BF)
+        rest = (scaled - high.astype(F32)).astype(BF)
+        weights_b = weights.astype(BF)
+        dv[0:upto] = dv[0:upto] + contract_rows(weights_b, high) + contract_rows(weights_b, rest)
+        if i == 1:
+            pump(6, 7)
+            go(gu_c(6))
+            go(small_b(0))
+        if i == 3:
+            pump(7, 8)
+            go_self = gu_c(7)
+            go_self.start()
+    d_qkv[:, HD : 2 * HD] = unrotate(dk[...], cos[...], sine[...]).astype(BF)
+    d_qkv[:, 2 * HD : 3 * HD] = dv[...].astype(BF)
+
+    wq_load.wait()
+    scatter = SlotScatter(part, buf, rss, rsr)
+
+    def swap(zq):
+        where = pl.ds(pl.multiple_of(slot_of(ring_index(core, zq), p) * TOK, TOK), TOK)
+        keep = pltpu.make_async_copy(seq.at[2 * zq + core], part.at[where], load.at[17 + zq])
+        return keep, remote(seq.at[2 * zq + 1 - core], part.at[where], sws.at[zq], swr.at[zq], sibling)
+
+    def swapped(zq):
+        where = pl.ds(pl.multiple_of(slot_of(ring_index(1 - core, zq), p) * TOK, TOK), TOK)
+        return remote(seq.at[0], part.at[where], sws.at[zq], swr.at[zq], sibling)
+
+    for zq in range(NZ):
+        rows = d_qkv[2 * zq * TOK : (2 * zq + 2) * TOK]
+
+        def columns(cols):
+            value = contract_cols(rows, wq[cols])
+            seq[2 * zq, :, cols] = value[0:TOK].astype(BF)
+            seq[2 * zq + 1, :, cols] = value[TOK:].astype(BF)
+
+        tiles(3, 768, columns)
+        for c in swap(zq):
             c.start()
-
-    def sum_a(tq, xq):
-        for c in load(tq, xq):
-            c.wait()
-        for c in to_sibling(tq, xq):
-            c.wait_recv()
-        acc[xq, tq] = (acc[xq, tq].astype(F32) + a_buf[xq, tq].astype(F32)).astype(BF)
-
-    def small_start(a):
-        buf, total = small[a][1], small[a][3]
-        for xo in (0, 1):
-            small_load(a, xo).wait()
-            small_a(a, xo).wait_recv()
-            total[xo] = (total[xo].astype(F32) + buf[xo].astype(F32)).astype(BF)
-        small_b(a).start()
-
-    for tq in order:
-        start_a(tq, 1 - x)
-    gain_a().start()
-    for a in (1, 0):
-        for xo in (0, 1):
-            small_a(a, xo).start()
-            small_load(a, xo).start()
-    for tq in order:
-        start_a(tq, x)
-    ahead = 2
-    for tq in order[:ahead]:
-        sum_a(tq, 1 - x)
-        to_across(tq).start()
+    for zq in range(NZ):
+        swap(zq)[0].wait()
+        swapped(zq).wait_recv()
+    scatter.step(0)
+
+    hidden_load.wait()
+
+    def grad_half(half):
+        def columns(cols):
+            value = contract_rows(ring[:, pl.ds(half * 1152, 1152)], d_qkv[:, cols])
+            for i in range(16):
+                grad_q[half * 16 + i, :, cols] = value[72 * i : 72 * (i + 1)].astype(BF)
+
+        tiles(3, 256, columns)
+
+    grad_half(0)
+    scatter.step(1)
+    grad_half(1)
+    for side in (0, 1):
+        go(*[q_a(side, j) for j in range(RING)])
+    for xo in (0, 1):
+        small_a(1, xo).wait_recv()
+        oa[xo] = (oa[xo].astype(F32) + og[2 * core + xo].astype(F32)).astype(BF)
+    go(small_b(1))
+    scatter.step(2)
+
+    def q_sum(side, j):
+        i = owner(order[j], core, side_x[side])
+        q_a(side, j).wait_recv()
+        total = grad_q[i].astype(F32) + aq[side, j].astype(F32)
+        if side == 1:
+            q_b(j).wait_recv()
+            total = total + bq[j].astype(F32)
+        grad_q[i] = total.astype(BF)
+
+    for j in range(RING):
+        q_sum(0, j)
+        if j < AHEAD:
+            go(q_b(j))
+    small_b(0).wait_recv()
+    da[x] = (da[x].astype(F32) + db[...].astype(F32)).astype(BF)
+    small_c(0, 0)
+    scatter.step(3)
+
+    def q_round(j):
+        q_sum(1, j)
+        if j + AHEAD < RING:
+            go(q_b(j + AHEAD))
+        if ROUNDS[j] == 0:
+            q_c(j).start()
+        else:
+            go(q_c(j))
+
+    for j in range(4):
+        q_round(j)
+    small_b(1).wait_recv()
+    oa[x] = (oa[x].astype(F32) + ob[...].astype(F32)).astype(BF)
+    small_c(1, 0)
+
+    def own_part(cols):
+        slot = part[0:TOK, cols]
+        d_hid_o[:, cols] = slot.astype(F32)
+
+    tiles(3, 768, own_part)
+    for j in range(4, RING):
+        q_round(j)
+    scatter.finish(d_hid_o)
+    gain_in[0:1] = jnp.sum(d_hid_o[...] * normed[...], axis=0, keepdims=True)
+    go(gain_a())
     gain_a().wait_recv()
     gsum[0] = gain_in[...] + ga[RING]
-    gain_b().start()
-    small_start(1)
-    for tq in order[ahead:]:
-        sum_a(tq, 1 - x)
-    for j, tq in enumerate(order):
-        sum_a(tq, x)
-        to_across(tq).wait_recv()
-        if j + ahead < RING:
-            to_across(order[j + ahead]).start()
-        elif j + ahead == RING:
-            small_start(0)
-        if j == 0:
-            gain_b().wait_recv()
-            gsum[1] = gsum[0] + ga[RING + 1]
-            for other in others:
-                gain_c(other).start()
-        acc[x, tq] = (acc[x, tq].astype(F32) + b_buf[tq].astype(F32)).astype(BF)
-        if j < RING - 1:
-            to_member(tq).start()
-    for a in (1, 0):
-        other, total = small[a][2:4]
-        small_b(a).wait_recv()
-        total[x] = (total[x].astype(F32) + other[...].astype(F32)).astype(BF)
-        for xo in (0, 1):
-            small_a(a, xo).wait_send()
-
-    @pl.when(core == y)
-    def _():
-        for a in (0, 1):
-            small[a][5][...] = small[a][3][x].astype(F32)
-
-    @pl.when(core != y)
-    def _():
-        for a in (0, 1):
-            small_c(a).start()
-        for a in (0, 1):
-            small_c(a).wait_recv()
-            small[a][5][...] = small[a][4][...].astype(F32)
-        for a in (0, 1):
-            small_c(a).wait_send()
-
+    go(gain_b())
+    gain_b().wait_recv()
+    gsum[1] = gsum[0] + ga[RING + 1]
+    go(*[gain_c(j) for j in range(1, RING)])
     total = gsum[1]
-    for tq in others:
-        gain_c(tq, True).wait_recv()
-        total = total + ga[tq]
+    for j in range(1, RING):
+        gain_c(j).wait_recv()
+        total = total + ga[j]
     gain_o[...] = total
-    c_buf[t] = acc[x, t]
-    for tq in others:
-        to_member(tq, True).wait_recv()
-    for tq in range(RING):
-        units = pl.ds(tq * UNITS, UNITS)
-        gate_o[:, units] = c_buf[tq, :, pl.ds(0, UNITS)].astype(F32)
-        up_o[:, units] = c_buf[tq, :, pl.ds(UNITS, UNITS)].astype(F32)
-        query_o[:, pl.ds(tq * HD, HD)] = c_buf[tq, :, pl.ds(STARTS[2], HD)].astype(F32)
-    for g in range(KVH):
-        for start, result in ((STARTS[3], key_o), (STARTS[4], value_o)):
-            columns = pl.ds(start, HD)
-            result[:, pl.ds(g * HD, HD)] = c_buf[2 * g, :, columns].astype(F32) + c_buf[2 * g + 1, :, columns].astype(F32)
-
-    for j, tq in enumerate(order):
-        for xq in (0, 1):
-            for c in to_sibling(tq, xq):
-                c.wait_send()
-        to_across(tq).wait_send()
-        if j < RING - 1:
-            to_member(tq).wait_send()
-    gain_a().wait_send()
-    gain_b().wait_send()
-    for tq in others:
-        gain_c(tq).wait_send()
-    for a in (0, 1):
-        small_b(a).wait_send()
-
-
-def weights_out(gu, qkv, down, out, gains, collective_id):
+
+    for j in range(RING):
+        if ROUNDS[j] == 0:
+            gu_c(j).wait()
+            q_c(j).wait()
+        else:
+            gu_c(j, True).wait_recv()
+            q_c(j, True).wait_recv()
+    small_c(0, 1)
+    small_c(1, 1)
+    for zq in range(NZ):
+        swap(zq)[1].wait_send()
+    scatter.drain()
+    for c in pending:
+        c.wait_send()
+
+
+def backward(d_branch, gu, down, hidden, w_in, w_out, queries, keys, values, attended, inv_total, cos_tab, sine_tab,
+             normed_pre, gain_parts, collective_id):
     n = 4 * RING
-    rows, width = gu.shape[0] // n, gains.shape[1]
-    gu, qkv = gu.reshape(n, rows, 2 * UNITS), qkv.reshape(n, rows, 3 * HD)
-    down, out = down.reshape(4, -1, width), out.reshape(4, -1, width)
-    down_rows, out_rows = down.shape[1], out.shape[1]
-    wide = (RING, rows, WIDE)
-
-    def full(*shape):
-        return jax.ShapeDtypeStruct(shape, F32)
+    rows, width = d_branch.shape
+    shard = gu.shape[0] // n
+    gu = gu.reshape(n, shard, 2 * UNITS)
+    down = down.reshape(4, -1, width)
+    total, down_rows, out_rows = RING * rows, down.shape[1], w_out.shape[0] // 4
+    gain_shape = (8, width)
+
+    def out(*shape, dtype=BF):
+        return jax.ShapeDtypeStruct(shape, dtype)
+
+    def body(*refs):
+        ins, rest = refs[:14], refs[14:]
+        gains_ref, rest = rest[0], rest[1:]
+        outs, scr = rest[:6], rest[6:]
+        gain_scr = scr[0]
+        gain_scr[...] = gains_ref[...]
+        backward_kernel(*ins, gain_scr, *outs, *scr[1:])
 
     return pl.pallas_call(
-        weights_out_kernel,
+        body,
         out_shape=[
-            full(rows, FF), full(rows, FF), full(rows, H * HD), full(rows, KVH * HD), full(rows, KVH * HD),
-            full(down_rows, width), full(out_rows, width), full(*gains.shape),
+            out(rows, width, dtype=F32), out(*gain_shape, dtype=F32),
+            out(RING, shard, 2 * UNITS), out(RING, shard, 3 * HD),
+            out(down_rows, width), out(out_rows, width),
         ],
-        in_specs=[HBM] * 4 + [VMEM],
-        out_specs=[VMEM] * 8,
+        in_specs=[HBM] * 5 + [VMEM] * 10,
+        out_specs=[VMEM] * 2 + [HBM] * 4,
         scratch_shapes=[
-            pltpu.VMEM((2,) + wide, BF), pltpu.VMEM(wide, BF), pltpu.VMEM(wide, BF), pltpu.VMEM((2,) + wide, BF),
-            pltpu.VMEM((2, down_rows, width), BF), pltpu.VMEM((down_rows, width), BF), pltpu.VMEM((2, down_rows, width), BF), pltpu.VMEM((down_rows, width), BF),
-            pltpu.VMEM((2, out_rows, width), BF), pltpu.VMEM((out_rows, width), BF), pltpu.VMEM((2, out_rows, width), BF), pltpu.VMEM((out_rows, width), BF),
-            pltpu.VMEM((RING + 2,) + gains.shape, F32), pltpu.VMEM((2,) + gains.shape, F32),
-            DMA((2, RING, 3)),
-            DMA((2, RING, 2)), DMA((2, RING, 2)),
-            DMA((RING,)), DMA((RING,)),
-            DMA((RING,)), DMA((RING,)),
-            DMA((2, 4)), DMA((2, 4)),
-            DMA((RING + 2,)), DMA((RING + 2,)),
+            pltpu.VMEM(gain_shape, F32),
+            pltpu.VMEM((total, width), BF), pltpu.VMEM((RING, rows, width), BF), pltpu.VMEM((total, width), BF),
+            pltpu.VMEM((2, 4, rows, width), BF), pltpu.VMEM((width, 3 * HD), BF),
+            pltpu.VMEM((total, HD), BF), pltpu.VMEM((total, 3 * HD), BF),
+            pltpu.VMEM((total, HD), F32), pltpu.VMEM((total, HD), F32),
+            pltpu.VMEM((n, shard, 3 * HD), BF), pltpu.VMEM((2, RING, shard, 3 * HD), BF), pltpu.VMEM((RING, shard, 3 * HD), BF),
+            pltpu.VMEM((2, shard, 2 * UNITS), BF), pltpu.VMEM((2, RING, shard, 2 * UNITS), BF), pltpu.VMEM((RING, shard, 2 * UNITS), BF),
+            pltpu.VMEM((down_rows, width), BF), pltpu.VMEM((2, down_rows, width), BF), pltpu.VMEM((down_rows, width), BF),
+            pltpu.VMEM((4, out_rows, width), BF), pltpu.VMEM((2, out_rows, width), BF), pltpu.VMEM((out_rows, width), BF),
+            pltpu.VMEM((RING + 2,) + gain_shape, F32), pltpu.VMEM((2,) + gain_shape, F32),
+            DMA((21,)),
+            DMA((2, 4, SUB)), DMA((2, 4, SUB)), DMA((NZ,)), DMA((NZ,)), DMA((2, 4, SUB)), DMA((2, 4, SUB)), DMA((NZ,)), DMA((NZ,)),
+            DMA((2, RING)), DMA((2, RING)), DMA((RING,)), DMA((RING,)), DMA((RING,)), DMA((RING,)),
+            DMA((2, RING)), DMA((2, RING)), DMA((RING,)), DMA((RING,)), DMA((RING,)), DMA((RING,)),
+            DMA((2, 4)), DMA((2, 4)), DMA((RING + 2,)), DMA((RING + 2,)),
         ],
-        compiler_params=params(collective_id),
-    )(gu, qkv, down, out, gains)
+        compiler_params=params(collective_id, 60),
+    )(d_branch, gu, down, hidden, w_in, w_out, queries, keys, values, attended, inv_total, cos_tab, sine_tab, normed_pre, gain_parts)
 
 
 def attend(queries, keys, values, positions):
@@ -1020,25 +1217,6 @@
     inv_total = 1.0 / jnp.sum(weights, axis=-1, keepdims=True)
     attended = fold_rows(weights.astype(BF), values) * inv_total
     return attended, inv_total
-
-
-def attend_back(queries, keys, values, positions, attended, inv_total, d_attended):
-    raw = contract_cols(queries, keys)
-    capped = CAP * jnp.tanh(raw / CAP)
-    allowed = positions[None, :] <= positions[:, None]
-    weights = jnp.where(allowed, jnp.exp(capped), 0.0)
-    delta = jnp.sum(d_attended.astype(F32) * attended, axis=-1, keepdims=True)
-    d_probs = contract_cols(d_attended, values)
-    slope = 1.0 - capped / CAP * (capped / CAP)
-    d_raw = (weights * inv_total * (d_probs - delta) * slope).astype(BF)
-    d_query = fold_rows(d_raw, keys)
-    d_key = contract_rows(d_raw, queries)
-    weights_b = weights.astype(BF)
-    d_scaled = d_attended.astype(F32) * inv_total
-    scaled_high = d_scaled.astype(BF)
-    scaled_rest = (d_scaled - scaled_high.astype(F32)).astype(BF)
-    d_value = contract_rows(weights_b, scaled_high) + contract_rows(weights_b, scaled_rest)
-    return d_query, d_key, d_value
 
 
 def on_ring(
@@ -1087,30 +1265,22 @@
     d_middle = out_cot + norm_back(d_hidden_ffn * pre_ffn_factor, normed_mid, inv_mid)
     post_part = jnp.sum(d_middle * normed_post, axis=0)
     d_branch = norm_back(d_middle * post_factor, normed_post, inv_post).astype(BF)
-    d_branch = ring_gather(d_branch, next(ids), True)
-    out_part = contract_rows(attended_b, d_branch)
-    d_attended = contract_cols(d_branch, w_ot).astype(BF)
-    d_query, d_key, d_value = attend_back(
-        queries, keys, values, positions, attended, inv_total, d_attended
-    )
-    d_qkv = jnp.concatenate(
-        [
-            unrotate(d_query * q_scale, cos_tab, sine_tab).astype(BF),
-            unrotate(d_key, cos_tab, sine_tab).astype(BF),
-            d_value.astype(BF),
-        ],
-        axis=1,
-    )
-    d_hidden = ring_scatter(contract_cols(d_qkv, w_qkv), next(ids), True)
-    qkv_part = contract_rows(hidden, d_qkv)
-    pre_part = jnp.sum(d_hidden * normed_pre, axis=0)
+    gain_parts = jnp.stack([jnp.zeros_like(post_part), post_part, pre_ffn_part, post_ffn_part])
+    d_hidden, gain_g, gu_g, qkv_g, down_g, out_g = backward(
+        d_branch, gu_part, down_part, hidden, w_in, w_ot, queries, keys, values, attended, inv_total,
+        cos_tab, sine_tab, normed_pre, jnp.pad(gain_parts, ((0, 4), (0, 0))), next(ids),
+    )
     token_grad = d_middle + norm_back(d_hidden * pre_factor, normed_pre, inv_pre)
-    gain_parts = jnp.pad(jnp.stack([pre_part, post_part, pre_ffn_part, post_ffn_part]), ((0, 4), (0, 0)))
-    results = weights_out(
-        gu_part, qkv_part.astype(BF), down_part, out_part.astype(BF),
-        gain_parts, next(ids),
-    )
-    gate_g, up_g, query_g, key_g, value_g, down_g, out_g, gain_g = results
+
+    def spread(columns):
+        return jnp.transpose(columns, (1, 0, 2)).reshape(shard_gain, -1).astype(F32)
+
+    gate_g, up_g, query_g = spread(gu_g[..., :UNITS]), spread(gu_g[..., UNITS:]), spread(qkv_g[..., :HD])
+    heads = qkv_g[..., HD:].astype(F32).reshape(KVH, H // KVH, shard_gain, 2 * HD).sum(1)
+    key_g, value_g = (
+        jnp.transpose(part, (1, 0, 2)).reshape(shard_gain, -1) for part in (heads[..., :HD], heads[..., HD:])
+    )
+    down_g, out_g = down_g.astype(F32), out_g.astype(F32)
     mine = lax.axis_index("ctx") * 4 + lax.axis_index("fsdp")
     gain_g = lax.dynamic_slice(gain_g, (0, mine * shard_gain), (4, shard_gain))
     return (

time: 775 us -> 679 us (0.88)
  Pallas kernels: 666 us -> 599 us
  matrix products: 39.9 us -> 13.5 us
    pallas_call x2 -> x1, Pallas kernels: 110 us -> 55 us  [ring_scatter(): pl.pallas_call(functools.partial(scatter_kernel, paired), out_shape=jax.S...]
    dot_general x4 -> x1, matrix products: 16.4 us -> 1.63 us  [contract_cols(): lax.dot_general(left, right, (((1,), (1,)), ((), ())), preferred_element_...]
    pallas_call x2 -> x1, Pallas kernels: 200 us -> 188 us  [backward(): pl.pallas_call(body, out_shape=[out(rows, width, dtype=F32), out(*gain_sh...]
    dot_general x5 -> x0, matrix products: 10.6 us -> none  [contract_rows(): lax.dot_general(left, right, (((0,), (0,)), ((), ())), preferred_element_...]
    unnamed x128 -> x54, local copies, waits for them, and re-layouts: 25.7 us -> 15.3 us
    unnamed x6 -> x2, other arithmetic: 8.97 us -> 0.38 us
where the time goes in v4:
time: 679 us; the launch traced here: 670 us
  Pallas kernels  599 us (88%)
  other arithmetic  29.9 us (4%)
  local copies, waits for them, and re-layouts  26.3 us (4%)
  matrix products  13.5 us (2%)
    pallas_call x1, Pallas kernels, feed_forward(): pl.pallas_call(feed_forward_kernel, out_shape=[full(rows, width, dtype=BF...  203 us
    pallas_call x1, Pallas kernels, backward(): pl.pallas_call(body, out_shape=[out(rows, width, dtype=F32), out(*gain_sh...  188 us
    pallas_call x1, Pallas kernels, weights_in(): pl.pallas_call(weights_in_kernel, out_shape=shapes, in_specs=[VMEM] * 9,...  153 us
    pallas_call x1, Pallas kernels, ring_scatter(): pl.pallas_call(functools.partial(scatter_kernel, paired), out_shape=jax.S...  55 us
    unnamed x54, local copies, waits for them, and re-layouts  15.3 us

profile of v4, /device:TPU:1, one launch (start us, length us, event | category | flops | bytes accessed | tf_op | source)
XLA Modules:
  0.0 670.3 jit_solution(7562533119317888983)
XLA Ops:
  0.7 1.3 fusion.11
  3.7 1.3 copy-done.5
  5.1 1.3 copy-done.6
  6.4 1.3 copy-done.7
  11.4 152.7 %shard_map.228 = (bf16[32,72,3072]{2,1,0:T(8,128)(2,1)}, bf16[4,288,2304]{2,1,0:T(8,128)(2,1)S(1)}, bf16[4,64,2304]{2,1,0:T(8,128)(2,1)S(1)}, f32[32,8,128]{2,1,0:T(8,128)S(1)}, bf16[8,128,2304]{2,1,0:T(8,128)(2,1)S(1)}) custom-call(bf16[72,9216]{1,0:T(8,128)(2,1)S(1)} %copy-done.5, bf16[72,9216]{1,0:T(8,128)(2,1)S(1)} %copy-done.6, ...), custom_call_target="tpu_custom_call" | custom-call | tf_op jit(solution)/shard_map/pallas_call | solution.py:788
  164.2 2.1 copy-done
  166.3 2.3 copy-done.3
  169.6 3.3 multiply_reduce_fusion
  173.2 3.5 fusion.1.refs_3_
  176.7 7.5 %fusion.2 = f32[1024,768]{1,0:T(8,128)S(1)} fusion(bf16[1024,2304]{1,0:T(8,128)(2,1)S(1)} %fusion.1.refs_3_, bf16[2304,3072]{1,0:T(8,128)(2,1)} %bitcast.75), kind=kOutput, calls=%fused_computation.7 | convolution fusion | flops 3623878656 | bytes 11403264 | tf_op jit(solution)/shard_map/dot_general | solution.py:69
  185.1 3.4 fusion.25
  189.5 1.6 fusion.4
  193.2 3.5 convolution_convert_fusion
  196.7 55.0 %shard_map.229 = f32[128,2304]{1,0:T(8,128)} custom-call(bf16[8,128,2304]{2,1,0:T(8,128)(2,1)} %bitcast.78), custom_call_target="tpu_custom_call" | custom-call | tf_op jit(solution)/shard_map/pallas_call | solution.py:327
  251.7 1.5 multiply_reduce_fusion.7
  253.3 2.7 multiply_reduce_fusion.6
  257.2 203.2 %shard_map.230 = (bf16[128,2304]{1,0:T(8,128)(2,1)}, f32[128,2304]{1,0:T(8,128)}, f32[1,2304]{1,0:T(1,128)}, bf16[1152,2304]{1,0:T(8,128)(2,1)}, bf16[2304,2304]{1,0:T(8,128)(2,1)}) custom-call(bf16[128,2304]{1,0:T(8,128)(2,1)} %multiply_convert_fusion.1.hid, f32[128,2304]{1,0:T(8,128)} %copy-done.12, f32[1,2304]{1,0:T(1,128)} %slice.87.factor, ...), custom_call_target="tpu_custom_call" | custom-call | tf_op jit(solution)/shard_map/pallas_call | solution.py:587
  460.4 2.2 multiply_reduce_fusion.2
  462.7 2.0 multiply_reduce_fusion.3
  466.6 188.4 %shard_map.231 = (f32[128,2304]{1,0:T(8,128)}, f32[8,2304]{1,0:T(8,128)}, bf16[8,72,2304]{2,1,0:T(8,128)(2,1)}, bf16[8,72,768]{2,1,0:T(8,128)(2,1)}, bf16[288,23...) custom-call(bf16[128,2304]{1,0:T(8,128)(2,1)} %multiply_convert_fusion.refs_0_, bf16[32,72,2304]{2,1,0:T(8,128)(2,1)} %bitcast.79, ...), custom_call_target="tpu_custom_call" | custom-call | tf_op jit(solution)/shard_map/pallas_call | solution.py:1182
  655.0 1.7 multiply_reduce_fusion.1
  662.8 1.7 convert_element_type.129
  665.8 1.7 copy.65
  667.5 1.7 copy.64
  (87 shorter events, 22.1 us)
Async XLA Ops:
  2.7 1.1 copy-start.1
  3.7 1.3 copy-start.5
  5.1 1.3 copy-start.6
  6.4 1.3 copy-start.7
  7.7 1.0 copy-start.8
  8.7 1.0 copy-start.9
  164.2 2.1 copy-start
  166.3 2.3 copy-start.3
  168.6 24.6 %copy-start.4 = (bf16[4,64,2304]{2,1,0:T(8,128)(2,1)}, bf16[4,64,2304]{2,1,0:T(8,128)(2,1)S(1)}, u32[]{:S(2)}) copy-start(bf16[4,64,2304]{2,1,0:T(8,128)(2,1)S(1)} %get-tuple-element.32) | copy-start | bytes 3538948
  176.7 7.5 %copy-start.15 = (bf16[1024,2304]{1,0:T(8,128)(2,1)}, bf16[1024,2304]{1,0:T(8,128)(2,1)S(1)}, u32[]{:S(2)}) copy-start(bf16[1024,2304]{1,0:T(8,128)(2,1)S(1)} %fusion.1.refs_3_) | copy-start | bytes 14155780
  188.5 2.6 copy-start.20
  192.0 4.7 copy-start.16
  251.7 1.5 copy-start.2
  256.0 1.2 copy-start.12
  257.2 205.4 %copy-start.19 = (bf16[1,128,2304]{2,1,0:T(8,128)(2,1)S(1)}, bf16[1,128,2304]{2,1,0:T(8,128)(2,1)}, u32[]{:S(2)}) copy-start(bf16[1,128,2304]{2,1,0:T(8,128)(2,1)} %param.25) | copy-start | bytes 1769476
  460.4 2.2 copy-start.13
  460.4 2.3 copy-start.14
  464.8 1.1 copy-start.25
  655.0 1.7 copy-start.17
  656.7 2.6 copy-start.24
  658.0 2.2 copy-start.22
  661.2 1.5 copy-start.21
  662.8 2.7 copy-start.18
  667.5 1.7 copy-start.23
  (2 other events, 1.8 us)

commit v5 on v4

--- a/solution.py
+++ b/solution.py
@@ -134,207 +134,6 @@
         return list(range(SUB))
     half = SUB // 2
     return list(range(half)) if direction == 0 else list(range(half, SUB))
-
-
-class RingGather:
-    def __init__(self, x_ref, ring_ref, seq_ref, loc_sem, ss, rs, sib_ss=None, sib_rs=None):
-        self.x_ref, self.ring_ref, self.seq_ref, self.loc_sem = x_ref, ring_ref, seq_ref, loc_sem
-        self.ss, self.rs, self.sib_ss, self.sib_rs = ss, rs, sib_ss, sib_rs
-        self.z, self.core, self.y, self.x = my_place()
-        self.p = ring_index(self.y, self.z)
-        self.right, self.left = (self.p + 1) % RING, (self.p + RING - 1) % RING
-        self.sibling = device(self.z, 1 - self.core, self.y, self.x)
-        self.piece = x_ref.shape[0] // SUB
-        self.pending = []
-        self.local = pltpu.make_async_copy(x_ref, ring_ref.at[self.p], loc_sem.at[RING])
-
-    def places(self):
-        near = [ring_device(self.right, self.core, self.x), ring_device(self.left, self.core, self.x)]
-        return near + ([self.sibling] if self.seq_ref is not None else [])
-
-    def origin(self, direction, step):
-        return (self.p + (RING - step if direction == 0 else step)) % RING
-
-    def copy(self, direction, step, k):
-        q = self.origin(direction, step)
-        rows = pl.ds(k * self.piece, self.piece)
-        src = self.x_ref.at[rows] if step == 0 else self.ring_ref.at[q, rows]
-        return remote(
-            src,
-            self.ring_ref.at[q, rows],
-            self.ss.at[direction, step, k],
-            self.rs.at[direction, step, k],
-            ring_device(self.right if direction == 0 else self.left, self.core, self.x),
-        )
-
-    def place(self, q, act):
-        if self.seq_ref is None:
-            return
-        yq, zq = ring_yz(q)
-        src, dst = self.ring_ref.at[q], self.seq_ref.at[2 * zq + self.core]
-
-        @pl.when(yq == self.core)
-        def _():
-            act(pltpu.make_async_copy(src, dst, self.loc_sem.at[q]))
-
-        @pl.when(yq != self.core)
-        def _():
-            act(remote(src, dst, self.sib_ss.at[zq], self.sib_rs.at[zq], self.sibling))
-
-    def step(self, step):
-        if step == 0:
-            self.local.start()
-        for k in range(SUB):
-            for direction in (0, 1):
-                if step > 0 and (step < 3 or k in ring_parts(direction, 3, 3)):
-                    self.copy(direction, step - 1, k).wait_recv()
-                if k in ring_parts(direction, step, 3):
-                    c = self.copy(direction, step, k)
-                    c.start()
-                    self.pending.append(c)
-        if step == 1:
-            self.local.wait()
-            self.place(self.p, lambda c: c.start())
-        if step == 3:
-            for direction in (0, 1):
-                for k in range(SUB):
-                    if k not in ring_parts(direction, 3, 3):
-                        self.copy(direction, 2, k).wait_recv()
-        if step > 0:
-            for direction in (0, 1):
-                self.place(self.origin(direction, step), lambda c: c.start())
-
-    def finish(self):
-        for direction in (0, 1):
-            for k in ring_parts(direction, 3, 3):
-                self.copy(direction, 3, k).wait_recv()
-        self.place((self.p + 4) % RING, lambda c: c.start())
-        for c in self.pending:
-            c.wait_send()
-        if self.seq_ref is None:
-            return
-        for q in range(RING):
-            self.place((self.p + q) % RING, lambda c: c.wait_send() if c.is_remote else c.wait())
-        for zq in range(NZ):
-            dst = self.seq_ref.at[2 * zq + 1 - self.core]
-            remote(self.ring_ref.at[zq], dst, self.sib_ss.at[zq], self.sib_rs.at[zq], self.sibling).wait_recv()
-
-
-def gather_kernel(paired, x_ref, *refs):
-    if paired:
-        seq_ref, ring_ref, *sems = refs
-    else:
-        ring_ref, *sems = refs
-        seq_ref = None
-    ring = RingGather(x_ref, ring_ref, seq_ref, *sems)
-    greet(ring.places())
-    for step in range(4):
-        ring.step(step)
-    ring.finish()
-
-
-def ring_gather(block, collective_id, paired):
-    rows, width = block.shape
-    whole = jax.ShapeDtypeStruct((RING, rows, width), block.dtype)
-    sems = [DMA((RING + 1,)), DMA((2, 4, SUB)), DMA((2, 4, SUB))]
-    if paired:
-        sems = [pltpu.VMEM(whole.shape, whole.dtype)] + sems + [DMA((NZ,)), DMA((NZ,))]
-    out = pl.pallas_call(
-        functools.partial(gather_kernel, paired),
-        out_shape=whole,
-        in_specs=[VMEM],
-        out_specs=VMEM if paired else HBM,
-        scratch_shapes=sems,
-        compiler_params=params(collective_id),
-    )(block)
-    return out.reshape(RING * rows, width)
-
-
-def scatter_kernel(paired, part_ref, o_ref, *refs):
-    if paired:
-        mine_ref, buf, ss, rs, sib_ss, sib_rs, loc_sem = refs
-    else:
-        buf, ss, rs = refs
-        mine_ref = part_ref
-    z, core, y, x = my_place()
-    p = ring_index(y, z)
-    right, left = (p + 1) % RING, (p + RING - 1) % RING
-    sibling = device(z, 1 - core, y, x)
-    piece = o_ref.shape[0] // SUB
-    greet(
-        [ring_device(right, core, x), ring_device(left, core, x)] + ([sibling] if paired else [])
-    )
-    if paired:
-        swaps, copies = [], []
-        for zq in range(NZ):
-            q = ring_index(core, zq)
-            swaps.append(remote(part_ref.at[2 * zq + 1 - core], mine_ref.at[q], sib_ss.at[zq], sib_rs.at[zq], sibling))
-            swaps[-1].start()
-            copies.append(pltpu.make_async_copy(part_ref.at[2 * zq + core], mine_ref.at[q], loc_sem.at[zq]))
-            copies[-1].start()
-        for c in copies:
-            c.wait()
-        for zq in range(NZ):
-            q = ring_index(1 - core, zq)
-            remote(part_ref.at[zq], mine_ref.at[q], sib_ss.at[zq], sib_rs.at[zq], sibling).wait_recv()
-        for c in swaps:
-            c.wait_send()
-
-    def copy(direction, step, k, src):
-        rows = pl.ds(k * piece, piece)
-        return remote(
-            src,
-            buf.at[direction, step, rows],
-            ss.at[direction, step, k],
-            rs.at[direction, step, k],
-            ring_device(right if direction == 0 else left, core, x),
-        )
-
-    pending = []
-    for step in range(4):
-        for k in range(SUB):
-            rows = pl.ds(k * piece, piece)
-            for direction in (0, 1):
-                if k not in ring_parts(direction, step, 0):
-                    continue
-                far = 4 - step
-                q = (p + (far if direction == 0 else RING - far)) % RING
-                src = mine_ref.at[q, rows]
-                if step > 0 and k in ring_parts(direction, step - 1, 0):
-                    src = buf.at[direction, step - 1, rows]
-                    copy(direction, step - 1, k, src).wait_recv()
-                    total = src[...].astype(F32) + mine_ref[q, rows].astype(F32)
-                    src[...] = total.astype(BF)
-                c = copy(direction, step, k, src)
-                c.start()
-                pending.append(c)
-    for k in range(SUB):
-        rows = pl.ds(k * piece, piece)
-        total = mine_ref[p, rows].astype(F32)
-        for direction in (0, 1):
-            src = buf.at[direction, 3, rows]
-            copy(direction, 3, k, src).wait_recv()
-            total = total + src[...].astype(F32)
-        o_ref[rows] = total
-    for c in pending:
-        c.wait_send()
-
-
-def ring_scatter(part, collective_id, paired):
-    rows, width = part.shape[0] // RING, part.shape[1]
-    blocks = (RING, rows, width)
-    sems = [DMA((2, 4, SUB)), DMA((2, 4, SUB))]
-    return pl.pallas_call(
-        functools.partial(scatter_kernel, paired),
-        out_shape=jax.ShapeDtypeStruct((rows, width), F32),
-        in_specs=[VMEM],
-        out_specs=VMEM,
-        scratch_shapes=([pltpu.VMEM(blocks, BF)] if paired else [])
-        + [pltpu.VMEM((2, 4, rows, width), BF)]
-        + sems
-        + ([DMA((NZ,)), DMA((NZ,)), DMA((NZ,))] if paired else []),
-        compiler_params=params(collective_id),
-    )(part.astype(BF).reshape(blocks))
 
 
 TOK = 128
@@ -461,7 +260,7 @@
     scatter = [SlotScatter(part, buf, rss.at[i], rsr.at[i]) for i in range(2)]
     greet(gather[0].near)
     loads = [
-        pltpu.make_async_copy(w_hbm.at[:, pl.ds(0, 2 * UNITS)], wgu, w_sem.at[0]),
+        pltpu.make_async_copy(w_hbm, wgu, w_sem.at[0]),
         pltpu.make_async_copy(wd_hbm, wd, w_sem.at[1]),
     ]
     ha[0:TOK] = hid[...]
@@ -607,12 +406,15 @@
 
 
 WIDTHS = (UNITS, UNITS, HD, HD, HD)
-STARTS = (0, UNITS, 2 * UNITS, 2 * UNITS + HD, 2 * UNITS + 2 * HD)
-WIDE = 2 * UNITS + 3 * HD
 
 
 def member_place(t, core, x):
     return device(t // 2, core, t % 2, x)
+
+
+def slot_of(q, p):
+    d = (q - p + RING) % RING
+    return jnp.where(d == 0, 0, jnp.where(d < 4, 2 * d, jnp.where(d == 4, 7, 15 - 2 * d)))
 
 
 def partner(t, j):
@@ -629,194 +431,363 @@
     return pl.multiple_of((t if which == 2 else t // 2) * HD, 128)
 
 
-def weights_in_kernel(gate, up, query, key, value, down, out, gains, x_ref, w_ref, d_ref, o_ref, g_ref, seq_ref,
-                      ring_ref, loc, s1, r1, s2, r2, s3, r3, s4, r4, s5, r5, ring_loc, ss, rs, sib_ss, sib_rs):
+def forward_kernel(gate, up, query, key, value, down, out, block, gain_in, cos, sine,
+                   w_gu, d_ref, hidden_o, wq, wo, gain_o, q_o, k_o, v_o, att_o, inv_o, branch_o,
+                   ring, seq, seq_part, part, buf, wq_in, own, relay, ga, gsum,
+                   load, ags, agr, pls, plr, rss, rsr, sws, swr, s1, r1, s2, r2, s3, r3,
+                   q1, t1, q2, t2, q3, t3, s4, r4, s5, r5, sg, rg):
     z, core, y, x = my_place()
-    t = 2 * z + y
+    t, p = 2 * z + y, ring_index(y, z)
     sibling, across = device(z, 1 - core, y, x), device(z, core, y, 1 - x)
-
-    def slot(tq, corq, xq):
-        return (2 * (tq // 2) + corq) * 4 + 2 * (tq % 2) + xq
-
-    me = slot(t, core, x)
     member = [partner(t, j) for j in range(RING)]
+    members = [member_place(tq, core, x) for tq in member]
     plane = []
     for dc in (0, 1):
         for dy in (0, 1):
             for dx in (0, 1):
                 if (dc, dx) != (0, 0):
                     plane.append(device(z, (core + dc) % 2, (y + dy) % 2, (x + dx) % 2))
-    greet([member_place(member[j], core, x) for j in range(1, RING)] + plane)
+    greet(members[1:] + plane)
     sources = (gate, up, query, key, value)
-    ring = RingGather(x_ref, ring_ref, seq_ref, ring_loc, ss, rs, sib_ss, sib_rs)
-
-    def first(j, a, wait=False):
-        tq = member[j]
-        if a == 5:
-            src, dst = gains, g_ref.at[slot(tq, core, x) if wait else me]
-        else:
-            src = sources[a].at[:, pl.ds(column_start(a, tq), WIDTHS[a])]
-            dst = w_ref.at[slot(tq, core, x) if wait else me, :, pl.ds(STARTS[a], WIDTHS[a])]
-        return remote(src, dst, s1.at[j, a], r1.at[j, a], member_place(tq, core, x))
-
     pending = []
 
-    def go(copies):
+    def go(*copies):
         for c in copies:
             c.start()
             pending.append(c)
 
+    def owner(tq, corq, xq):
+        return (2 * (tq // 2) + corq) * 4 + 2 * (tq % 2) + xq
+
+    me = owner(t, core, x)
+
+    def columns_of(a, tq):
+        return sources[a].at[:, pl.ds(column_start(a, tq), WIDTHS[a])]
+
+    def gain_a(j):
+        return remote(gain_in, ga.at[j], sg.at[j], rg.at[j], members[j])
+
+    def gain_b(i):
+        return remote(gsum.at[i], ga.at[RING + i], sg.at[RING + i], rg.at[RING + i], (across, sibling)[i])
+
+    def q_first(j, a, wait=False):
+        tq = member[j]
+        dst = wq_in.at[owner(tq, core, x) if wait else me, :, pl.ds((a - 2) * HD, HD)]
+        return remote(columns_of(a, tq), dst, q1.at[j, a - 2], t1.at[j, a - 2], members[j])
+
+    def q_second(j, wait=False):
+        i = owner(member[j], core, 1 - x if wait else x)
+        return remote(wq_in.at[i], wq_in.at[i], q2.at[j], t2.at[j], across)
+
+    def q_third(j, flip, wait=False):
+        i = owner(member[j], 1 - core if wait else core, 1 - x if flip else x)
+        return remote(wq_in.at[i], wq_in.at[i], q3.at[j, flip], t3.at[j, flip], sibling)
+
+    def first(j, a, wait=False):
+        tq = member[j]
+        dst = w_gu.at[owner(tq, core, x) if wait else me, :, pl.ds(a * UNITS, UNITS)]
+        return remote(columns_of(a, tq), dst, s1.at[j, a], r1.at[j, a], members[j])
+
     def second(j, wait=False):
-        i = slot(member[j], core, 1 - x if wait else x)
-        return [
-            remote(w_ref.at[i], w_ref.at[i], s2.at[j, 0], r2.at[j, 0], across),
-            remote(g_ref.at[i], g_ref.at[i], s2.at[j, 1], r2.at[j, 1], across),
-        ]
+        i = owner(member[j], core, 1 - x if wait else x)
+        return remote(own if j == 0 else w_gu.at[i], w_gu.at[i], s2.at[j], r2.at[j], across)
 
     def third(j, flip, wait=False):
-        i = slot(member[j], 1 - core if wait else core, 1 - x if flip else x)
-        return [
-            remote(w_ref.at[i], w_ref.at[i], s3.at[j, flip, 0], r3.at[j, flip, 0], sibling),
-            remote(g_ref.at[i], g_ref.at[i], s3.at[j, flip, 1], r3.at[j, flip, 1], sibling),
-        ]
+        i = owner(member[j], 1 - core if wait else core, 1 - x if flip else x)
+        return remote(own if (j, flip) == (0, 0) else w_gu.at[i], w_gu.at[i], s3.at[j, flip], r3.at[j, flip], sibling)
 
     def start_round(j):
-        go([first(j, a) for a in (5, 2, 3, 4, 0, 1)])
+        go(first(j, 0), first(j, 1))
 
     def end_round(j):
-        for a in range(6):
-            first(j, a, True).wait_recv()
-        go(second(j) + third(j, 0))
+        first(j, 0, True).wait_recv()
+        first(j, 1, True).wait_recv()
+        go(second(j), third(j, 0))
 
     def end_across(j):
-        for c in second(j, True):
-            c.wait_recv()
+        second(j, True).wait_recv()
         go(third(j, 1))
 
-    ring.step(0)
-    start_round(4)
-    start_round(1)
-    locals_ = [pltpu.make_async_copy(gains, g_ref.at[me], loc.at[5])]
-    for a in range(5):
-        locals_.append(
-            pltpu.make_async_copy(
-                sources[a].at[:, pl.ds(column_start(a, t), WIDTHS[a])],
-                w_ref.at[me, :, pl.ds(STARTS[a], WIDTHS[a])],
-                loc.at[a],
-            )
-        )
+    gather = SlotGather(ring, ags, agr)
+
+    def block_of(slot):
+        if slot == 0:
+            return p
+        if slot == 7:
+            return (p + 4) % RING
+        s = (slot + 1) // 2
+        return (p + (RING - s if slot % 2 else s)) % RING
+
+    def place(slot, act):
+        yq, zq = ring_yz(block_of(slot))
+        src, dst = ring.at[pl.ds(slot * TOK, TOK)], seq.at[2 * zq + core]
+
+        @pl.when(yq == core)
+        def _():
+            c = pltpu.make_async_copy(src, dst, load.at[6 + slot])
+            c.start() if act == 0 else c.wait()
+
+        @pl.when(yq != core)
+        def _():
+            c = remote(src, dst, pls.at[zq], plr.at[zq], sibling)
+            c.start() if act == 0 else c.wait_send()
+
+    pair = ((down, d_ref), (out, wo))
+    mine = 2 * y + x
+
+    def rows_out(xq, a, act):
+        src, dst = pair[a][0], pair[a][1].at[mine]
+        to_self = (x == core) & (y == core) & (xq == x)
+
+        @pl.when(to_self)
+        def _():
+            if a == 0:
+                c = pltpu.make_async_copy(relay, dst, load.at[5])
+            else:
+                c = pltpu.make_async_copy(src, dst, load.at[4])
+            c.start() if act == 0 else c.wait()
+
+        @pl.when(jnp.logical_not(to_self))
+        def _():
+            c = remote(src, dst, s4.at[xq, a], r4.at[y, a], device(z, x, core, xq))
+            c.start() if act == 0 else c.wait_send()
+
+    def rows_on(yq, a):
+        src, dst = pair[a][0], pair[a][1].at[2 * yq + core]
+        from_self = (core == y) & (yq == y) & (core == x)
+
+        @pl.when(from_self)
+        def _():
+            if a == 0:
+                pltpu.make_async_copy(relay, dst, load.at[5]).wait()
+            else:
+                pltpu.make_async_copy(src, dst, load.at[4]).wait()
+
+        @pl.when(jnp.logical_not(from_self))
+        def _():
+            remote(src, dst, s4.at[0, a], r4.at[yq, a], sibling).wait_recv()
+
+        go(remote(dst, dst, s5.at[yq, a], r5.at[yq, a], sibling))
+
+    locals_ = [pltpu.make_async_copy(columns_of(a, t), wq_in.at[me, :, pl.ds((a - 2) * HD, HD)], load.at[a]) for a in (2, 3)]
+    locals_.append(pltpu.make_async_copy(columns_of(4, t), wq_in.at[me, :, pl.ds(2 * HD, HD)], load.at[14]))
+    locals_ += [pltpu.make_async_copy(columns_of(a, t), own.at[:, pl.ds(a * UNITS, UNITS)], load.at[a]) for a in (0, 1)]
+    relay_load = pltpu.make_async_copy(down, relay, load.at[15])
     for c in locals_:
         c.start()
-    pair = ((down, d_ref), (out, o_ref))
-    mine = 2 * y + x
+    relay_load.start()
+    ring[0:TOK] = block[...]
+    gather.step(0)
+    go(*[gain_a(j) for j in range(1, RING)])
+    for j in range(1, RING):
+        go(*[q_first(j, a) for a in (2, 3, 4)])
+    for c in locals_:
+        c.wait()
+    go(q_second(0), q_third(0, 0))
+    relay_load.wait()
+    for a in (1, 0):
+        for xq in (0, 1):
+            rows_out(xq, a, 0)
+    keep_own = pltpu.make_async_copy(own, w_gu.at[me], load.at[16])
+    keep_own.start()
+    go(second(0), third(0, 0))
+    place(0, 0)
+    total = gain_in[...]
+    for j in range(1, RING):
+        gain_a(j).wait_recv()
+        total = total + ga[j]
+    gsum[0] = total
+    go(gain_b(0))
+    gather.step(1)
+    place(1, 0)
+    place(2, 0)
+    gain_b(0).wait_recv()
+    gsum[1] = gsum[0] + ga[RING]
+    go(gain_b(1))
+    for j in range(1, RING):
+        for a in (2, 3, 4):
+            q_first(j, a, True).wait_recv()
+        go(q_second(j), q_third(j, 0))
+    for yq in (0, 1):
+        rows_on(yq, 1)
+    gather.step(2)
+    place(3, 0)
+    place(4, 0)
+    gain_b(1).wait_recv()
+    gain_o[...] = gsum[1] + ga[RING + 1]
+    for j in range(RING):
+        q_second(j, True).wait_recv()
+        go(q_third(j, 1))
+    gather.step(3)
+    place(5, 0)
+    place(6, 0)
+    start_round(4)
+    start_round(5)
+    start_round(1)
+    for yq in (0, 1):
+        rows_on(yq, 0)
+    end_across(0)
+    for j in range(RING):
+        for flip in (0, 1):
+            q_third(j, flip, True).wait_recv()
+
+    def join(g, carry):
+        pieces = [wq_in[4 * g + i].astype(F32) for i in range(4)]
+        wq[pl.ds(pl.multiple_of(288 * g, 16), 288)] = jnp.concatenate(pieces, axis=0).astype(BF)
+        return carry
+
+    lax.fori_loop(0, 8, join, 0)
+    gather.finish()
+    place(7, 0)
+    for zq in range(NZ):
+        dst = seq.at[2 * zq + 1 - core]
+        remote(dst, dst, pls.at[zq], plr.at[zq], sibling).wait_recv()
+    for slot in range(RING):
+        place(slot, 1)
+    end_round(1)
+    start_round(2)
+
+    factor = 1.0 + gain_o[0:1]
+
+    def norm(c, carry):
+        for half in range(2):
+            rows = pl.ds(half * 64, 64)
+            seq[c, rows] = (rms_parts(seq[c, rows].astype(F32))[1] * factor).astype(BF)
+        return carry
+
+    lax.fori_loop(0, RING, norm, 0)
+    keep_hidden = pltpu.make_async_copy(seq, hidden_o, load.at[17])
+    keep_hidden.start()
+    for i in range(4):
+        r = pl.ds(i * 256, 256)
+        rows = seq[2 * i : 2 * i + 2].reshape(256, -1)
+        tabs = (cos[r], sine[r])
+        q_o[r] = (rotate(fold_rows(rows, wq[:, 0:HD]), *tabs) * (HD ** (-0.5))).astype(BF)
+        k_o[r] = rotate(fold_rows(rows, wq[:, HD : 2 * HD]), *tabs).astype(BF)
+        v_o[r] = fold_rows(rows, wq[:, 2 * HD : 3 * HD]).astype(BF)
+    end_round(4)
+    start_round(6)
+    end_across(1)
+
+    def swap(zq, kept):
+        where = pl.ds(pl.multiple_of(slot_of(ring_index(core, zq), p) * TOK, TOK), TOK)
+        if kept:
+            return pltpu.make_async_copy(seq_part.at[2 * zq + core], part.at[where], load.at[18 + zq])
+        return remote(seq_part.at[2 * zq + 1 - core], part.at[where], sws.at[zq], swr.at[zq], sibling)
+
+    def swapped(zq):
+        where = pl.ds(pl.multiple_of(slot_of(ring_index(1 - core, zq), p) * TOK, TOK), TOK)
+        return remote(seq_part.at[0], part.at[where], sws.at[zq], swr.at[zq], sibling)
+
+    for yq in (0, 1):
+        remote(out, wo.at[2 * yq + 1 - core], s5.at[yq, 1], r5.at[yq, 1], sibling).wait_recv()
+    for i in range(4):
+        r, upto = pl.ds(i * 256, 256), (i + 1) * 256
+        bent = jnp.tanh(contract_cols(q_o[r], k_o[0:upto]) / CAP)
+        seen = lax.broadcasted_iota(jnp.int32, bent.shape, 1) <= i * 256 + lax.broadcasted_iota(jnp.int32, bent.shape, 0)
+        weights = jnp.where(seen, jnp.exp(CAP * bent), 0.0)
+        inverse = 1.0 / jnp.sum(weights, axis=-1, keepdims=True)
+        attended = fold_rows(weights.astype(BF), v_o[0:upto]) * inverse
+        inv_o[r] = inverse
+        att_o[r] = attended
+        attended_b = attended.astype(BF)
+
+        def columns(cols):
+            sums = fold_rows(attended_b, wo[:, :, cols].reshape(HD, 768))
+            seq_part[2 * i, :, cols] = sums[0:TOK].astype(BF)
+            seq_part[2 * i + 1, :, cols] = sums[TOK:].astype(BF)
+
+        tiles(3, 768, columns)
+        swap(i, True).start()
+        swap(i, False).start()
+        if i == 0:
+            end_round(2)
+            start_round(3)
+        if i == 2:
+            end_round(5)
+            start_round(7)
+            end_across(2)
+    for zq in range(NZ):
+        swap(zq, True).wait()
+        swapped(zq).wait_recv()
+    scatter = SlotScatter(part, buf, rss, rsr)
+    scatter.step(0)
+    end_round(3)
+    end_across(4)
+    scatter.step(1)
+    end_round(6)
+    end_across(5)
+    end_across(3)
+    scatter.step(2)
+    end_round(7)
+    end_across(6)
+    scatter.step(3)
+    branch_o[...] = part[0:TOK].astype(F32)
+    end_across(7)
+    scatter.finish(branch_o)
+
+    for j in range(RING):
+        for flip in (0, 1):
+            third(j, flip, True).wait_recv()
+    for yq in (0, 1):
+        remote(down, d_ref.at[2 * yq + 1 - core], s5.at[yq, 0], r5.at[yq, 0], sibling).wait_recv()
     for xq in (0, 1):
-        to_self = (x == core) & (y == core) & (xq == x)
-        for a, (src, dst) in enumerate(pair):
-            @pl.when(to_self)
-            def _():
-                pltpu.make_async_copy(src, dst.at[mine], s4.at[xq, a]).start()
+        for a in (0, 1):
+            to_self = (x == core) & (y == core) & (xq == x)
 
             @pl.when(jnp.logical_not(to_self))
             def _():
-                remote(src, dst.at[mine], s4.at[xq, a], r4.at[y, a], device(z, x, core, xq)).start()
-    for c in locals_:
-        c.wait()
-    go(second(0) + third(0, 0))
-    ring.step(1)
-    end_round(1)
-    start_round(2)
-    end_round(4)
-    start_round(5)
-    ring.step(2)
-    end_round(2)
-    start_round(3)
-    end_across(0)
-    end_across(1)
-    end_round(5)
-    start_round(6)
-    ring.step(3)
-    end_round(3)
-    start_round(7)
-    end_across(4)
-    for yq in (0, 1):
-        from_self = (core == y) & (yq == y) & (core == x)
-        for a, (src, dst) in enumerate(pair):
-            @pl.when(from_self)
-            def _():
-                pltpu.make_async_copy(src, dst.at[mine], s4.at[x, a]).wait()
-
-            @pl.when(jnp.logical_not(from_self))
-            def _():
-                remote(src, dst.at[2 * yq + core], s4.at[0, a], r4.at[yq, a], sibling).wait_recv()
-
-            go([remote(dst.at[2 * yq + core], dst.at[2 * yq + core], s5.at[yq, a], r5.at[yq, a], sibling)])
-    end_across(2)
-    end_across(5)
-    ring.finish()
-    end_round(6)
-    end_across(3)
-    end_round(7)
-    end_across(6)
-    end_across(7)
-    for j in range(RING):
-        for flip in (0, 1):
-            for c in third(j, flip, True):
-                c.wait_recv()
-    for yq in (0, 1):
-        for a, (src, dst) in enumerate(pair):
-            remote(src, dst.at[2 * yq + 1 - core], s5.at[yq, a], r5.at[yq, a], sibling).wait_recv()
+                remote(pair[a][0], pair[a][1].at[mine], s4.at[xq, a], r4.at[y, a], device(z, x, core, xq)).wait_send()
+    keep_own.wait()
+    keep_hidden.wait()
+    for zq in range(NZ):
+        swap(zq, False).wait_send()
+    gather.drain()
+    scatter.drain()
     for c in pending:
         c.wait_send()
-    for xq in (0, 1):
-        to_self = (x == core) & (y == core) & (xq == x)
-        for a, (src, dst) in enumerate(pair):
-            @pl.when(jnp.logical_not(to_self))
-            def _():
-                remote(src, dst.at[mine], s4.at[xq, a], r4.at[y, a], device(z, x, core, xq)).wait_send()
-
-
-def weights_in(gate, up, query, key, value, down, out, gains, block, collective_id):
+
+
+def forward(gate, up, query, key, value, down, out, block, gains, cos_tab, sine_tab, collective_id):
     n = 4 * RING
-    whole = (RING,) + block.shape
-    shapes = [
-        jax.ShapeDtypeStruct((n, gate.shape[0], WIDE), BF),
-        jax.ShapeDtypeStruct((4,) + down.shape, BF),
-        jax.ShapeDtypeStruct((4,) + out.shape, BF),
-        jax.ShapeDtypeStruct((n,) + gains.shape, gains.dtype),
-        jax.ShapeDtypeStruct(whole, BF),
-    ]
-    results = pl.pallas_call(
-        weights_in_kernel,
-        out_shape=shapes,
-        in_specs=[VMEM] * 9,
-        out_specs=[HBM] * 4 + [VMEM],
+    rows, width = block.shape
+    shard, total = gate.shape[0], RING * block.shape[0]
+
+    def full(*shape, dtype=BF):
+        return jax.ShapeDtypeStruct(shape, dtype)
+
+    blocks = (RING, rows, width)
+    return pl.pallas_call(
+        forward_kernel,
+        out_shape=[
+            full(n, shard, 2 * UNITS), full(4, *down.shape), full(*blocks), full(width, 3 * HD), full(4, *out.shape),
+            full(*gains.shape, dtype=F32), full(total, HD), full(total, HD), full(total, HD),
+            full(total, HD, dtype=F32), full(total, 1, dtype=F32), full(rows, width, dtype=F32),
+        ],
+        in_specs=[HBM] * 7 + [VMEM] * 4,
+        out_specs=[HBM] * 3 + [VMEM] * 9,
         scratch_shapes=[
-            pltpu.VMEM(whole, BF),
-            DMA((6,)),
-            DMA((RING, 6)), DMA((RING, 6)),
-            DMA((RING, 2)), DMA((RING, 2)),
-            DMA((RING, 2, 2)), DMA((RING, 2, 2)),
-            DMA((2, 2)), DMA((2, 2)),
-            DMA((2, 2)), DMA((2, 2)),
-            DMA((RING + 1,)), DMA((2, 4, SUB)), DMA((2, 4, SUB)), DMA((NZ,)), DMA((NZ,)),
+            pltpu.VMEM((total, width), BF), pltpu.VMEM(blocks, BF), pltpu.VMEM(blocks, BF), pltpu.VMEM((total, width), BF),
+            pltpu.VMEM((2, 4, rows, width), BF), pltpu.VMEM((n, shard, 3 * HD), BF),
+            pltpu.VMEM((shard, 2 * UNITS), BF), pltpu.VMEM(down.shape, BF),
+            pltpu.VMEM((RING + 2,) + gains.shape, F32), pltpu.VMEM((2,) + gains.shape, F32),
+            DMA((22,)),
+            DMA((2, 4, SUB)), DMA((2, 4, SUB)), DMA((NZ,)), DMA((NZ,)), DMA((2, 4, SUB)), DMA((2, 4, SUB)), DMA((NZ,)), DMA((NZ,)),
+            DMA((RING, 2)), DMA((RING, 2)), DMA((RING,)), DMA((RING,)), DMA((RING, 2)), DMA((RING, 2)),
+            DMA((RING, 3)), DMA((RING, 3)), DMA((RING,)), DMA((RING,)), DMA((RING, 2)), DMA((RING, 2)),
+            DMA((2, 2)), DMA((2, 2)), DMA((2, 2)), DMA((2, 2)), DMA((RING + 2,)), DMA((RING + 2,)),
         ],
-        compiler_params=params(collective_id, 32),
-    )(gate, up, query, key, value, down, out, gains, block)
-    return list(results[:4]) + [results[4].reshape(RING * block.shape[0], block.shape[1])]
+        compiler_params=params(collective_id, 60),
+    )(gate, up, query, key, value, down, out, block, gains, cos_tab, sine_tab)
 
 
 ROUNDS = (4, 5, 6, 7, 2, 3, 1, 0)
 AHEAD = 2
 
 
-def slot_of(q, p):
-    d = (q - p + RING) % RING
-    return jnp.where(d == 0, 0, jnp.where(d < 4, 2 * d, jnp.where(d == 4, 7, 15 - 2 * d)))
-
-
-def backward_kernel(d_branch, gu_in, down_in, hidden, w_hbm, wo, q_in, k_in, v_in, att, inv, cos, sine, normed, gain_in,
+def backward_kernel(d_branch, gu_in, down_in, hidden, wq, wo, q_in, k_in, v_in, att, inv, cos, sine, normed, gain_in,
                     d_hid_o, gain_o, c_gu, c_q, down_o, out_o,
-                    ring, seq, part, buf, wq, d_att, d_qkv, dk, dv, grad_q, aq, bq,
+                    ring, seq, part, buf, d_att, d_qkv, dk, dv, grad_q, aq, bq,
                     own, a_gu, b_gu, down_own, da, db, og, oa, ob, ga, gsum,
                     load, ags, agr, pls, plr, rss, rsr, sws, swr, s1, r1, s2, r2, s3, r3,
                     q1, t1, q2, t2, q3, t3, sx, rx, sg, rg):
@@ -941,7 +912,6 @@
 
     first = pltpu.make_async_copy(d_branch, ring.at[pl.ds(0, TOK)], load.at[14])
     first.start()
-    wq_load = pltpu.make_async_copy(w_hbm.at[:, pl.ds(2 * UNITS, 3 * HD)], wq, load.at[15])
     first.wait()
     gather.step(0)
     place(0, 0)
@@ -949,7 +919,6 @@
         go(*[gu_a(side, j) for j in range(RING)])
         if side == 0:
             go(small_a(0, 0), small_a(0, 1))
-    wq_load.start()
     for j in range(RING):
         if j < 2:
             gu_own(0, j).start()
@@ -1038,13 +1007,13 @@
     d_qkv[:, HD : 2 * HD] = unrotate(dk[...], cos[...], sine[...]).astype(BF)
     d_qkv[:, 2 * HD : 3 * HD] = dv[...].astype(BF)
 
-    wq_load.wait()
     scatter = SlotScatter(part, buf, rss, rsr)
 
-    def swap(zq):
+    def swap(zq, kept):
         where = pl.ds(pl.multiple_of(slot_of(ring_index(core, zq), p) * TOK, TOK), TOK)
-        keep = pltpu.make_async_copy(seq.at[2 * zq + core], part.at[where], load.at[17 + zq])
-        return keep, remote(seq.at[2 * zq + 1 - core], part.at[where], sws.at[zq], swr.at[zq], sibling)
+        if kept:
+            return pltpu.make_async_copy(seq.at[2 * zq + core], part.at[where], load.at[17 + zq])
+        return remote(seq.at[2 * zq + 1 - core], part.at[where], sws.at[zq], swr.at[zq], sibling)
 
     def swapped(zq):
         where = pl.ds(pl.multiple_of(slot_of(ring_index(1 - core, zq), p) * TOK, TOK), TOK)
@@ -1059,10 +1028,10 @@
             seq[2 * zq + 1, :, cols] = value[TOK:].astype(BF)
 
         tiles(3, 768, columns)
-        for c in swap(zq):
-            c.start()
+        swap(zq, True).start()
+        swap(zq, False).start()
     for zq in range(NZ):
-        swap(zq)[0].wait()
+        swap(zq, True).wait()
         swapped(zq).wait_recv()
     scatter.step(0)
 
@@ -1152,13 +1121,13 @@
     small_c(0, 1)
     small_c(1, 1)
     for zq in range(NZ):
-        swap(zq)[1].wait_send()
+        swap(zq, False).wait_send()
     scatter.drain()
     for c in pending:
         c.wait_send()
 
 
-def backward(d_branch, gu, down, hidden, w_in, w_out, queries, keys, values, attended, inv_total, cos_tab, sine_tab,
+def backward(d_branch, gu, down, hidden, w_qkv, w_out, queries, keys, values, attended, inv_total, cos_tab, sine_tab,
              normed_pre, gain_parts, collective_id):
     n = 4 * RING
     rows, width = d_branch.shape
@@ -1186,12 +1155,12 @@
             out(RING, shard, 2 * UNITS), out(RING, shard, 3 * HD),
             out(down_rows, width), out(out_rows, width),
         ],
-        in_specs=[HBM] * 5 + [VMEM] * 10,
+        in_specs=[HBM] * 4 + [VMEM] * 11,
         out_specs=[VMEM] * 2 + [HBM] * 4,
         scratch_shapes=[
             pltpu.VMEM(gain_shape, F32),
             pltpu.VMEM((total, width), BF), pltpu.VMEM((RING, rows, width), BF), pltpu.VMEM((total, width), BF),
-            pltpu.VMEM((2, 4, rows, width), BF), pltpu.VMEM((width, 3 * HD), BF),
+            pltpu.VMEM((2, 4, rows, width), BF),
             pltpu.VMEM((total, HD), BF), pltpu.VMEM((total, 3 * HD), BF),
             pltpu.VMEM((total, HD), F32), pltpu.VMEM((total, HD), F32),
             pltpu.VMEM((n, shard, 3 * HD), BF), pltpu.VMEM((2, RING, shard, 3 * HD), BF), pltpu.VMEM((RING, shard, 3 * HD), BF),
@@ -1206,17 +1175,7 @@
             DMA((2, 4)), DMA((2, 4)), DMA((RING + 2,)), DMA((RING + 2,)),
         ],
         compiler_params=params(collective_id, 60),
-    )(d_branch, gu, down, hidden, w_in, w_out, queries, keys, values, attended, inv_total, cos_tab, sine_tab, normed_pre, gain_parts)
-
-
-def attend(queries, keys, values, positions):
-    raw = contract_cols(queries, keys)
-    capped = CAP * jnp.tanh(raw / CAP)
-    allowed = positions[None, :] <= positions[:, None]
-    weights = jnp.where(allowed, jnp.exp(capped), 0.0)
-    inv_total = 1.0 / jnp.sum(weights, axis=-1, keepdims=True)
-    attended = fold_rows(weights.astype(BF), values) * inv_total
-    return attended, inv_total
+    )(d_branch, gu, down, hidden, w_qkv, w_out, queries, keys, values, attended, inv_total, cos_tab, sine_tab, normed_pre, gain_parts)
 
 
 def on_ring(
@@ -1224,40 +1183,27 @@
     pre_gain, post_gain, pre_ffn_gain, post_ffn_gain, out_grad,
 ):
     ids = iter(range(32))
-    n_shards = 4 * RING
     length = RING * tokens.shape[1]
     shard_gain = pre_gain.shape[0]
+    mine = lax.axis_index("ctx") * 4 + lax.axis_index("fsdp")
     gains = jnp.stack([pre_gain, post_gain, pre_ffn_gain, post_ffn_gain]).astype(F32)
-    gains = jnp.pad(gains, ((0, 4), (0, 128 - shard_gain)))
-    w_in, down_in, out_in, gains_in, sequence = weights_in(
-        w_gate, w_up, w_query, w_key, w_value, w_down, w_out, gains, tokens[0], next(ids)
-    )
-    w_in = w_in.reshape(-1, WIDE)
-    w_qkv = w_in[:, 2 * UNITS :]
+    gains = lax.dynamic_update_slice(jnp.zeros((8, D), F32), gains, (0, mine * shard_gain))
+    cos_tab, sine_tab = rope_tables(jnp.arange(length, dtype=jnp.int32), HD)
+    w_gu, down_in, hidden, w_qkv, out_in, gains, queries, keys, values, attended, inv_total, branch = forward(
+        w_gate, w_up, w_query, w_key, w_value, w_down, w_out, tokens[0], gains, cos_tab, sine_tab, next(ids)
+    )
+    w_gu, hidden = w_gu.reshape(D, 2 * UNITS), hidden.reshape(length, D)
     w_dn = down_in.reshape(UNITS, D)
     w_ot = out_in.reshape(HD, D)
-    factors = 1.0 + jnp.transpose(gains_in[:, :4, :shard_gain], (1, 0, 2)).reshape(4, D)
-    pre_factor, post_factor, pre_ffn_factor, post_ffn_factor = (factors[i] for i in range(4))
-    positions = jnp.arange(length, dtype=jnp.int32)
-    cos_tab, sine_tab = rope_tables(positions, HD)
-    q_scale = HD ** (-0.5)
-
+    pre_factor, post_factor, pre_ffn_factor, post_ffn_factor = (1.0 + gains[i] for i in range(4))
     resid_in = tokens[0].astype(F32)
     inv_pre, normed_pre = rms_parts(resid_in)
-    hidden = (rms_parts(sequence.astype(F32))[1] * pre_factor).astype(BF)
-    projected = fold_rows(hidden, w_qkv)
-    queries = (rotate(projected[:, :HD], cos_tab, sine_tab) * q_scale).astype(BF)
-    keys = rotate(projected[:, HD : 2 * HD], cos_tab, sine_tab).astype(BF)
-    values = projected[:, 2 * HD :].astype(BF)
-    attended, inv_total = attend(queries, keys, values, positions)
-    attended_b = attended.astype(BF)
-    branch = ring_scatter(fold_rows(attended_b, w_ot), next(ids), True)
     inv_post, normed_post = rms_parts(branch)
     middle = resid_in + normed_post * post_factor
     inv_mid, normed_mid = rms_parts(middle)
     hidden_ffn = (normed_mid * pre_ffn_factor).astype(BF)
     output, d_hidden_ffn, post_ffn_part, down_part, gu_part = feed_forward(
-        hidden_ffn, middle, post_ffn_factor[None], out_grad[0], w_in, w_dn, next(ids)
+        hidden_ffn, middle, post_ffn_factor[None], out_grad[0], w_gu, w_dn, next(ids)
     )
     post_ffn_part = post_ffn_part[0]
     out_cot = out_grad[0].astype(F32)
@@ -1267,7 +1213,7 @@
     d_branch = norm_back(d_middle * post_factor, normed_post, inv_post).astype(BF)
     gain_parts = jnp.stack([jnp.zeros_like(post_part), post_part, pre_ffn_part, post_ffn_part])
     d_hidden, gain_g, gu_g, qkv_g, down_g, out_g = backward(
-        d_branch, gu_part, down_part, hidden, w_in, w_ot, queries, keys, values, attended, inv_total,
+        d_branch, gu_part, down_part, hidden, w_qkv, w_ot, queries, keys, values, attended, inv_total,
         cos_tab, sine_tab, normed_pre, jnp.pad(gain_parts, ((0, 4), (0, 0))), next(ids),
     )
     token_grad = d_middle + norm_back(d_hidden * pre_factor, normed_pre, inv_pre)
@@ -1281,7 +1227,6 @@
         jnp.transpose(part, (1, 0, 2)).reshape(shard_gain, -1) for part in (heads[..., :HD], heads[..., HD:])
     )
     down_g, out_g = down_g.astype(F32), out_g.astype(F32)
-    mine = lax.axis_index("ctx") * 4 + lax.axis_index("fsdp")
     gain_g = lax.dynamic_slice(gain_g, (0, mine * shard_gain), (4, shard_gain))
     return (
         output[None], token_grad.astype(BF)[None],

time: 679 us -> 633 us (0.932)
  local copies, waits for them, and re-layouts: 26.3 us -> 10 us
  matrix products: 13.5 us -> 0 us
  other arithmetic: 29.9 us -> 19.1 us
    unnamed x54 -> x30, local copies, waits for them, and re-layouts: 15.3 us -> 1.72 us
    dot_general x4 -> x0, matrix products: 13.5 us -> none  [the longest x3 11.9 us: fold_rows(): return jnp.dot(left, right, preferred_element_type=F32)]
    pallas_call x2 -> x1, Pallas kernels: 208 us -> 200 us  [forward(): pl.pallas_call(forward_kernel, out_shape=[full(n, shard, 2 * UNITS), full...]
where the time goes in v5:
time: 633 us; the launch traced here: 628 us
  Pallas kernels  598 us (94%)
  other arithmetic  19.1 us (3%)
  local copies, waits for them, and re-layouts  10 us (2%)
    pallas_call x1, Pallas kernels, feed_forward(): pl.pallas_call(feed_forward_kernel, out_shape=[full(rows, width, dtype=BF...  210 us
    pallas_call x1, Pallas kernels, forward(): pl.pallas_call(forward_kernel, out_shape=[full(n, shard, 2 * UNITS), full...  200 us
    pallas_call x1, Pallas kernels, backward(): pl.pallas_call(body, out_shape=[out(rows, width, dtype=F32), out(*gain_sh...  189 us

profile of v5, /device:TPU:1, one launch (start us, length us, event | category | flops | bytes accessed | tf_op | source)
XLA Modules:
  0.0 628.0 jit_solution(3786982227151790034)
XLA Ops:
  0.7 0.7 maximum_convert_fusion
  2.0 3.1 multiply_sine_fusion
  5.1 199.5 %shard_map.228 = (bf16[32,72,2304]{2,1,0:T(8,128)(2,1)}, bf16[4,288,2304]{2,1,0:T(8,128)(2,1)}, bf16[8,128,2304]{2,1,0:T(8,128)(2,1)}, bf16[2304,768]{1,0:T(8,12...) custom-call(bf16[72,9216]{1,0:T(8,128)(2,1)} %gate.1, ...), custom_call_target="tpu_custom_call" | custom-call | tf_op jit(solution)/shard_map/pallas_call | solution.py:760
  204.6 1.5 multiply_reduce_fusion.6
  206.4 0.6 add_reduce_fusion
  207.0 1.5 multiply_reduce_fusion.5
  208.5 1.1 multiply_convert_fusion.1.hid
  209.7 209.7 %shard_map.229 = (bf16[128,2304]{1,0:T(8,128)(2,1)}, f32[128,2304]{1,0:T(8,128)}, f32[1,2304]{1,0:T(1,128)}, bf16[1152,2304]{1,0:T(8,128)(2,1)}, bf16[2304,2304]{1,0:T(8,128)(2,1)}) custom-call(bf16[128,2304]{1,0:T(8,128)(2,1)} %multiply_convert_fusion.1.hid, f32[128,2304]{1,0:T(8,128)} %copy-done, f32[1,2304]{1,0:T(1,128)} %get-tuple-element.74.factor, ...), custom_call_target="tpu_custom_call" | custom-call | tf_op jit(solution)/shard_map/pallas_call | solution.py:386
  419.4 2.1 multiply_reduce_fusion.1
  421.7 0.7 multiply_reduce_fusion.2
  422.5 0.6 pad.4.refs_14_
  423.2 1.1 multiply_convert_fusion.refs_0_
  424.3 188.6 %shard_map.230 = (f32[128,2304]{1,0:T(8,128)}, f32[8,2304]{1,0:T(8,128)}, bf16[8,72,2304]{2,1,0:T(8,128)(2,1)}, bf16[8,72,768]{2,1,0:T(8,128)(2,1)}, bf16[288,23...) custom-call(bf16[128,2304]{1,0:T(8,128)(2,1)} %multiply_convert_fusion.refs_0_, bf16[32,72,2304]{2,1,0:T(8,128)(2,1)} %bitcast.59, ...), custom_call_target="tpu_custom_call" | custom-call | tf_op jit(solution)/shard_map/pallas_call | solution.py:1151
  612.9 2.1 convert_bitcast_fusion
  615.0 1.7 copy.40
  616.7 1.7 copy.41
  618.4 1.7 convert_element_type.84
  620.3 0.7 copy.38
  621.0 0.7 copy.39
  621.8 0.9 copy.37
  623.6 1.2 fusion.1
  624.8 0.9 convert_element_type.77
  625.6 0.8 constant_dynamic-slice_fusion
  626.9 0.8 copy.44
  (47 shorter events, 2.8 us)
Async XLA Ops:
  2.0 3.1 copy-start.11
  5.1 201.1 %copy-start.3 = (bf16[1,128,2304]{2,1,0:T(8,128)(2,1)S(1)}, bf16[1,128,2304]{2,1,0:T(8,128)(2,1)}, u32[]{:S(2)}) copy-start(bf16[1,128,2304]{2,1,0:T(8,128)(2,1)} %param.13) | copy-start | bytes 1769476
  204.6 1.8 copy-start.12
  204.6 2.4 copy-start.2
  208.5 1.2 copy-start
  209.7 211.8 %copy-start.6 = (bf16[1,128,2304]{2,1,0:T(8,128)(2,1)S(1)}, bf16[1,128,2304]{2,1,0:T(8,128)(2,1)}, u32[]{:S(2)}) copy-start(bf16[1,128,2304]{2,1,0:T(8,128)(2,1)} %param.25) | copy-start | bytes 1769476
  419.4 2.2 copy-start.1
  419.4 2.3 copy-start.5
  421.7 0.8 copy-start.13
  616.7 1.7 copy-start.7
  618.4 1.7 copy-start.8
  621.7 1.5 copy-start.4
  623.6 1.2 copy-start.10
  624.8 2.2 copy-start.9

commit v6 on v5

--- a/solution.py
+++ b/solution.py
@@ -305,7 +305,7 @@
             value = contract_cols(dgu[pl.ds(first, count)], wgu[cols])
             dst[pl.ds(first, count), cols] = value.astype(dst.dtype)
 
-        tiles(9, 256, column)
+        tiles(3, 768, column)
 
     n_down = UNITS // TILE
 
@@ -408,6 +408,15 @@
 WIDTHS = (UNITS, UNITS, HD, HD, HD)
 
 
+SHARD = D // (4 * RING)
+PADDED = D + 128
+WINDOW = 256
+
+
+def window(i):
+    return pl.ds(pl.multiple_of((SHARD * i) // 128 * 128, 128), WINDOW)
+
+
 def member_place(t, core, x):
     return device(t // 2, core, t % 2, x)
 
@@ -468,7 +477,7 @@
         return remote(gain_in, ga.at[j], sg.at[j], rg.at[j], members[j])
 
     def gain_b(i):
-        return remote(gsum.at[i], ga.at[RING + i], sg.at[RING + i], rg.at[RING + i], (across, sibling)[i])
+        return remote(gsum.at[i], gsum.at[2 + i], sg.at[RING + i], rg.at[RING + i], (across, sibling)[i])
 
     def q_first(j, a, wait=False):
         tq = member[j]
@@ -584,25 +593,24 @@
     for c in locals_:
         c.wait()
     go(q_second(0), q_third(0, 0))
-    relay_load.wait()
-    for a in (1, 0):
-        for xq in (0, 1):
-            rows_out(xq, a, 0)
+    for xq in (0, 1):
+        rows_out(xq, 1, 0)
     keep_own = pltpu.make_async_copy(own, w_gu.at[me], load.at[16])
     keep_own.start()
     go(second(0), third(0, 0))
     place(0, 0)
-    total = gain_in[...]
+    gsum[0] = jnp.zeros(gsum.shape[1:], F32)
+    gsum[0, :, window(me)] = gain_in[...]
     for j in range(1, RING):
         gain_a(j).wait_recv()
-        total = total + ga[j]
-    gsum[0] = total
+        lanes = window(owner(member[j], core, x))
+        gsum[0, :, lanes] = gsum[0, :, lanes] + ga[j]
     go(gain_b(0))
     gather.step(1)
     place(1, 0)
     place(2, 0)
     gain_b(0).wait_recv()
-    gsum[1] = gsum[0] + ga[RING]
+    gsum[1] = gsum[0] + gsum[2]
     go(gain_b(1))
     for j in range(1, RING):
         for a in (2, 3, 4):
@@ -614,7 +622,7 @@
     place(3, 0)
     place(4, 0)
     gain_b(1).wait_recv()
-    gain_o[...] = gsum[1] + ga[RING + 1]
+    gain_o[...] = (gsum[1] + gsum[3])[:, 0:D]
     for j in range(RING):
         q_second(j, True).wait_recv()
         go(q_third(j, 1))
@@ -624,8 +632,9 @@
     start_round(4)
     start_round(5)
     start_round(1)
-    for yq in (0, 1):
-        rows_on(yq, 0)
+    relay_load.wait()
+    for xq in (0, 1):
+        rows_out(xq, 0, 0)
     end_across(0)
     for j in range(RING):
         for flip in (0, 1):
@@ -707,6 +716,8 @@
             end_round(5)
             start_round(7)
             end_across(2)
+            for yq in (0, 1):
+                rows_on(yq, 0)
     for zq in range(NZ):
         swap(zq, True).wait()
         swapped(zq).wait_recv()
@@ -761,7 +772,7 @@
         forward_kernel,
         out_shape=[
             full(n, shard, 2 * UNITS), full(4, *down.shape), full(*blocks), full(width, 3 * HD), full(4, *out.shape),
-            full(*gains.shape, dtype=F32), full(total, HD), full(total, HD), full(total, HD),
+            full(8, D, dtype=F32), full(total, HD), full(total, HD), full(total, HD),
             full(total, HD, dtype=F32), full(total, 1, dtype=F32), full(rows, width, dtype=F32),
         ],
         in_specs=[HBM] * 7 + [VMEM] * 4,
@@ -770,7 +781,7 @@
             pltpu.VMEM((total, width), BF), pltpu.VMEM(blocks, BF), pltpu.VMEM(blocks, BF), pltpu.VMEM((total, width), BF),
             pltpu.VMEM((2, 4, rows, width), BF), pltpu.VMEM((n, shard, 3 * HD), BF),
             pltpu.VMEM((shard, 2 * UNITS), BF), pltpu.VMEM(down.shape, BF),
-            pltpu.VMEM((RING + 2,) + gains.shape, F32), pltpu.VMEM((2,) + gains.shape, F32),
+            pltpu.VMEM((RING,) + gains.shape, F32), pltpu.VMEM((4, 8, PADDED), F32),
             DMA((22,)),
             DMA((2, 4, SUB)), DMA((2, 4, SUB)), DMA((NZ,)), DMA((NZ,)), DMA((2, 4, SUB)), DMA((2, 4, SUB)), DMA((NZ,)), DMA((NZ,)),
             DMA((RING, 2)), DMA((RING, 2)), DMA((RING,)), DMA((RING,)), DMA((RING, 2)), DMA((RING, 2)),
@@ -878,13 +889,14 @@
         return remote(src, dst, q3.at[j], t3.at[j], members[ROUNDS[j]])
 
     def gain_a():
-        return remote(gain_in, ga.at[RING], sg.at[RING], rg.at[RING], sibling)
+        return remote(gain_in, gsum.at[2], sg.at[RING], rg.at[RING], sibling)
 
     def gain_b():
-        return remote(gsum.at[0], ga.at[RING + 1], sg.at[RING + 1], rg.at[RING + 1], across)
+        return remote(gsum.at[0], gsum.at[3], sg.at[RING + 1], rg.at[RING + 1], across)
 
     def gain_c(j):
-        return remote(gsum.at[1], ga.at[j], sg.at[j], rg.at[j], members[j])
+        lanes = window(owner(partner(t, j), core, x))
+        return remote(gsum.at[1, :, lanes], ga.at[j], sg.at[j], rg.at[j], members[j])
 
     gather = SlotGather(ring, ags, agr)
 
@@ -1097,15 +1109,15 @@
     for j in range(4, RING):
         q_round(j)
     scatter.finish(d_hid_o)
-    gain_in[0:1] = jnp.sum(d_hid_o[...] * normed[...], axis=0, keepdims=True)
+    gain_in[0:1, 0:D] = jnp.sum(d_hid_o[...] * normed[...], axis=0, keepdims=True)
     go(gain_a())
     gain_a().wait_recv()
-    gsum[0] = gain_in[...] + ga[RING]
+    gsum[0] = gain_in[...] + gsum[2]
     go(gain_b())
     gain_b().wait_recv()
-    gsum[1] = gsum[0] + ga[RING + 1]
+    gsum[1] = gsum[0] + gsum[3]
     go(*[gain_c(j) for j in range(1, RING)])
-    total = gsum[1]
+    total = gsum[1, :, window(owner(t, core, x))]
     for j in range(1, RING):
         gain_c(j).wait_recv()
         total = total + ga[j]
@@ -1135,7 +1147,7 @@
     gu = gu.reshape(n, shard, 2 * UNITS)
     down = down.reshape(4, -1, width)
     total, down_rows, out_rows = RING * rows, down.shape[1], w_out.shape[0] // 4
-    gain_shape = (8, width)
+    gain_shape = (8, PADDED)
 
     def out(*shape, dtype=BF):
         return jax.ShapeDtypeStruct(shape, dtype)
@@ -1151,7 +1163,7 @@
     return pl.pallas_call(
         body,
         out_shape=[
-            out(rows, width, dtype=F32), out(*gain_shape, dtype=F32),
+            out(rows, width, dtype=F32), out(8, WINDOW, dtype=F32),
             out(RING, shard, 2 * UNITS), out(RING, shard, 3 * HD),
             out(down_rows, width), out(out_rows, width),
         ],
@@ -1167,7 +1179,7 @@
             pltpu.VMEM((2, shard, 2 * UNITS), BF), pltpu.VMEM((2, RING, shard, 2 * UNITS), BF), pltpu.VMEM((RING, shard, 2 * UNITS), BF),
             pltpu.VMEM((down_rows, width), BF), pltpu.VMEM((2, down_rows, width), BF), pltpu.VMEM((down_rows, width), BF),
             pltpu.VMEM((4, out_rows, width), BF), pltpu.VMEM((2, out_rows, width), BF), pltpu.VMEM((out_rows, width), BF),
-            pltpu.VMEM((RING + 2,) + gain_shape, F32), pltpu.VMEM((2,) + gain_shape, F32),
+            pltpu.VMEM((RING, 8, WINDOW), F32), pltpu.VMEM((4,) + gain_shape, F32),
             DMA((21,)),
             DMA((2, 4, SUB)), DMA((2, 4, SUB)), DMA((NZ,)), DMA((NZ,)), DMA((2, 4, SUB)), DMA((2, 4, SUB)), DMA((NZ,)), DMA((NZ,)),
             DMA((2, RING)), DMA((2, RING)), DMA((RING,)), DMA((RING,)), DMA((RING,)), DMA((RING,)),
@@ -1176,6 +1188,55 @@
         ],
         compiler_params=params(collective_id, 60),
     )(d_branch, gu, down, hidden, w_qkv, w_out, queries, keys, values, attended, inv_total, cos_tab, sine_tab, normed_pre, gain_parts)
+
+
+def results_kernel(gu, qkv, down, out, d_hidden, d_middle, normed, inverse, factor,
+                   gate_o, up_o, query_o, key_o, value_o, down_o, out_o, token_o):
+    for i in range(2):
+        units, heads = pl.ds(i * UNITS, UNITS), pl.ds(i * HD, HD)
+        gate_o[:, units] = gu[i, :, 0:UNITS].astype(F32)
+        up_o[:, units] = gu[i, :, UNITS : 2 * UNITS].astype(F32)
+        query_o[:, heads] = qkv[i, :, 0:HD].astype(F32)
+    key_o[...] = qkv[0, :, HD : 2 * HD].astype(F32) + qkv[1, :, HD : 2 * HD].astype(F32)
+    value_o[...] = qkv[0, :, 2 * HD :].astype(F32) + qkv[1, :, 2 * HD :].astype(F32)
+    down_o[...] = down[...].astype(F32)
+    out_o[...] = out[...].astype(F32)
+    back = norm_back(d_hidden[...] * factor[...], normed[...], inverse[...])
+    token_o[...] = (d_middle[...] + back).astype(BF)
+
+
+def results(gu, qkv, down, out, d_hidden, d_middle, normed, inverse, factor):
+    steps = RING // 2
+    shard, width = gu.shape[1], down.shape[1]
+    tok, down_rows, out_rows = d_hidden.shape[0] // steps, down.shape[0] // steps, out.shape[0] // steps
+
+    def rows(n, wide):
+        return pl.BlockSpec((n, wide), lambda i: (i, 0))
+
+    def columns(wide):
+        return pl.BlockSpec((shard, wide), lambda i: (0, i))
+
+    def full(*shape):
+        return jax.ShapeDtypeStruct(shape, F32)
+
+    return pl.pallas_call(
+        results_kernel,
+        grid=(steps,),
+        out_shape=[
+            full(shard, FF), full(shard, FF), full(shard, H * HD), full(shard, KVH * HD), full(shard, KVH * HD),
+            full(*down.shape), full(*out.shape), jax.ShapeDtypeStruct(d_hidden.shape, BF),
+        ],
+        in_specs=[
+            pl.BlockSpec((2, shard, 2 * UNITS), lambda i: (i, 0, 0)), pl.BlockSpec((2, shard, 3 * HD), lambda i: (i, 0, 0)),
+            rows(down_rows, width), rows(out_rows, width), rows(tok, width), rows(tok, width), rows(tok, width),
+            rows(tok, 1), pl.BlockSpec((1, width), lambda i: (0, 0)),
+        ],
+        out_specs=[
+            columns(2 * UNITS), columns(2 * UNITS), columns(2 * HD), columns(HD), columns(HD),
+            rows(down_rows, width), rows(out_rows, width), rows(tok, width),
+        ],
+        compiler_params=pltpu.CompilerParams(vmem_limit_bytes=60 * 2**20),
+    )(gu, qkv, down, out, d_hidden, d_middle, normed, inverse, factor)
 
 
 def on_ring(
@@ -1187,7 +1248,7 @@
     shard_gain = pre_gain.shape[0]
     mine = lax.axis_index("ctx") * 4 + lax.axis_index("fsdp")
     gains = jnp.stack([pre_gain, post_gain, pre_ffn_gain, post_ffn_gain]).astype(F32)
-    gains = lax.dynamic_update_slice(jnp.zeros((8, D), F32), gains, (0, mine * shard_gain))
+    gains = lax.dynamic_update_slice(jnp.zeros((8, WINDOW), F32), gains, (0, (mine * shard_gain) % 128))
     cos_tab, sine_tab = rope_tables(jnp.arange(length, dtype=jnp.int32), HD)
     w_gu, down_in, hidden, w_qkv, out_in, gains, queries, keys, values, attended, inv_total, branch = forward(
         w_gate, w_up, w_query, w_key, w_value, w_down, w_out, tokens[0], gains, cos_tab, sine_tab, next(ids)
@@ -1214,22 +1275,14 @@
     gain_parts = jnp.stack([jnp.zeros_like(post_part), post_part, pre_ffn_part, post_ffn_part])
     d_hidden, gain_g, gu_g, qkv_g, down_g, out_g = backward(
         d_branch, gu_part, down_part, hidden, w_qkv, w_ot, queries, keys, values, attended, inv_total,
-        cos_tab, sine_tab, normed_pre, jnp.pad(gain_parts, ((0, 4), (0, 0))), next(ids),
-    )
-    token_grad = d_middle + norm_back(d_hidden * pre_factor, normed_pre, inv_pre)
-
-    def spread(columns):
-        return jnp.transpose(columns, (1, 0, 2)).reshape(shard_gain, -1).astype(F32)
-
-    gate_g, up_g, query_g = spread(gu_g[..., :UNITS]), spread(gu_g[..., UNITS:]), spread(qkv_g[..., :HD])
-    heads = qkv_g[..., HD:].astype(F32).reshape(KVH, H // KVH, shard_gain, 2 * HD).sum(1)
-    key_g, value_g = (
-        jnp.transpose(part, (1, 0, 2)).reshape(shard_gain, -1) for part in (heads[..., :HD], heads[..., HD:])
-    )
-    down_g, out_g = down_g.astype(F32), out_g.astype(F32)
-    gain_g = lax.dynamic_slice(gain_g, (0, mine * shard_gain), (4, shard_gain))
+        cos_tab, sine_tab, normed_pre, jnp.pad(gain_parts, ((0, 4), (0, PADDED - D))), next(ids),
+    )
+    gate_g, up_g, query_g, key_g, value_g, down_g, out_g, token_grad = results(
+        gu_g, qkv_g, down_g, out_g, d_hidden, d_middle, normed_pre, inv_pre, pre_factor[None]
+    )
+    gain_g = lax.dynamic_slice(gain_g, (0, (mine * shard_gain) % 128), (4, shard_gain))
     return (
-        output[None], token_grad.astype(BF)[None],
+        output[None], token_grad[None],
         query_g, key_g, value_g, out_g, gate_g, up_g, down_g,
         gain_g[0], gain_g[1], gain_g[2], gain_g[3],
     )

time: 633 us -> 605 us (0.956)
  Pallas kernels: 598 us -> 581 us
    pallas_call x1, Pallas kernels: 200 us -> 189 us  [forward(): pl.pallas_call(forward_kernel, out_shape=[full(n, shard, 2 * UNITS), full...]
    pallas_call x1, Pallas kernels: 210 us -> 203 us  [feed_forward(): pl.pallas_call(feed_forward_kernel, out_shape=[full(rows, width, dtype=BF...]
    pallas_call x1 -> x2, Pallas kernels: 189 us -> 189 us  [the longest x1 181 us: backward(): pl.pallas_call(body, out_shape=[out(rows, width, dtype=F32), out(8, WINDO...]
where the time goes in v6:
time: 605 us; the launch traced here: 601 us
  Pallas kernels  581 us (96%)
  other arithmetic  13.9 us (2%)
    pallas_call x1, Pallas kernels, feed_forward(): pl.pallas_call(feed_forward_kernel, out_shape=[full(rows, width, dtype=BF...  203 us
    pallas_call x1, Pallas kernels, forward(): pl.pallas_call(forward_kernel, out_shape=[full(n, shard, 2 * UNITS), full...  189 us
    pallas_call x1, Pallas kernels, backward(): pl.pallas_call(body, out_shape=[out(rows, width, dtype=F32), out(8, WINDO...  181 us

profile of v6, /device:TPU:1, one launch (start us, length us, event | category | flops | bytes accessed | tf_op | source)
XLA Modules:
  0.0 600.6 jit_solution(5367109511983736154)
XLA Ops:
  0.7 0.7 maximum_convert_fusion
  1.4 0.6 dynamic_update_slice.3.gain_in
  2.0 3.1 multiply_sine_fusion
  5.1 189.2 %shard_map.228 = (bf16[32,72,2304]{2,1,0:T(8,128)(2,1)}, bf16[4,288,2304]{2,1,0:T(8,128)(2,1)}, bf16[8,128,2304]{2,1,0:T(8,128)(2,1)}, bf16[2304,768]{1,0:T(8,12...) custom-call(bf16[72,9216]{1,0:T(8,128)(2,1)} %gate.1, ...), custom_call_target="tpu_custom_call" | custom-call | tf_op jit(solution)/shard_map/pallas_call | solution.py:771
  194.3 1.7 slice_add_fusion
  196.0 1.4 multiply_reduce_fusion.5
  197.5 0.2 fusion
  197.7 1.6 multiply_reduce_fusion.4
  199.3 1.1 multiply_convert_fusion.1.hid
  200.4 0.1 copy-done
  200.5 203.3 %shard_map.229 = (bf16[128,2304]{1,0:T(8,128)(2,1)}, f32[128,2304]{1,0:T(8,128)}, f32[1,2304]{1,0:T(1,128)}, bf16[1152,2304]{1,0:T(8,128)(2,1)}, bf16[2304,2304]{1,0:T(8,128)(2,1)}) custom-call(bf16[128,2304]{1,0:T(8,128)(2,1)} %multiply_convert_fusion.1.hid, f32[128,2304]{1,0:T(8,128)} %copy-done, f32[1,2304]{1,0:T(1,128)} %get-tuple-element.86.factor, ...), custom_call_target="tpu_custom_call" | custom-call | tf_op jit(solution)/shard_map/pallas_call | solution.py:386
  403.7 0.0 copy-start.1
  403.7 2.1 multiply_reduce_fusion
  405.9 0.1 copy-done.5
  406.1 0.7 multiply_reduce_fusion.1
  406.8 0.1 pad_maximum_fusion
  406.9 0.8 pad.4.refs_14_
  407.7 1.1 multiply_convert_fusion.refs_0_
  408.9 181.2 %shard_map.230 = (f32[128,2304]{1,0:T(8,128)}, f32[8,256]{1,0:T(8,128)}, bf16[8,72,2304]{2,1,0:T(8,128)(2,1)}, bf16[8,72,768]{2,1,0:T(8,128)(2,1)}, bf16[288,2304]{1,0:T(8,128)(2,1)}, /*index=5*/bf16[64,2304]{1,0:T(8,128)(2,1)}) custom-call(bf16[128,2304]{1,0:T(8,128)(2,1)} %multiply_convert_fusion.refs_0_, bf16[32,72,2304]{2,1,0:T(8,128)(2,1)} %bitcast.31, ...), custom_call_target="tpu_custom_call" | custom-call | tf_op jit(solution)/shard_map/pallas_call | solution.py:1163
  590.0 0.7 copy.26.inverse
  590.8 7.6 %shard_map.231 = (f32[72,9216]{1,0:T(8,128)}, f32[72,9216]{1,0:T(8,128)}, f32[72,2048]{1,0:T(8,128)}, f32[72,1024]{1,0:T(8,128)}, f32[72,1024]{1,0:T(8,128)}, /*...) custom-call(bf16[8,72,2304]{2,1,0:T(8,128)(2,1)} %get-tuple-element.61.gu, ...), custom_call_target="tpu_custom_call" | custom-call | tf_op jit(solution)/shard_map/pallas_call | solution.py:1222
  598.3 0.8 constant_dynamic-slice_fusion
  599.1 0.5 slice_bitcast_fusion
  599.6 0.8 copy.29
  (27 shorter events, 0.1 us)
Async XLA Ops:
  2.0 3.1 copy-start.8
  5.1 192.4 %copy-start.4 = (bf16[1,128,2304]{2,1,0:T(8,128)(2,1)S(1)}, bf16[1,128,2304]{2,1,0:T(8,128)(2,1)}, u32[]{:S(2)}) copy-start(bf16[1,128,2304]{2,1,0:T(8,128)(2,1)} %param.13) | copy-start | bytes 1769476
  194.3 3.4 copy-start.2
  199.2 1.2 copy-start
  200.5 205.4 %copy-start.6 = (bf16[1,128,2304]{2,1,0:T(8,128)(2,1)S(1)}, bf16[1,128,2304]{2,1,0:T(8,128)(2,1)}, u32[]{:S(2)}) copy-start(bf16[1,128,2304]{2,1,0:T(8,128)(2,1)} %param.25) | copy-start | bytes 1769476
  403.7 2.2 copy-start.1
  403.7 2.3 copy-start.5
  406.1 0.7 copy-start.9
  406.8 2.1 copy-start.3
  590.8 8.9 %copy-start.7 = (bf16[128,2304]{1,0:T(8,128)(2,1)S(1)}, bf16[128,2304]{1,0:T(8,128)(2,1)}, u32[]{:S(2)}) copy-start(bf16[128,2304]{1,0:T(8,128)(2,1)} %get-tuple-element.48) | copy-start | bytes 1769476

commit v7 on v6

--- a/solution.py
+++ b/solution.py
@@ -2,6 +2,7 @@
 
 import jax
 import jax.numpy as jnp
+import numpy as np
 from jax import lax
 from jax.experimental import pallas as pl
 from jax.experimental.pallas import tpu as pltpu
@@ -30,6 +31,13 @@
     inv_freqs = ROPE_BASE ** (-jnp.arange(half_width, dtype=F32) * 2.0 / width)
     angles = positions.astype(F32)[:, None] * inv_freqs[None, :]
     return (jnp.cos(angles), jnp.sin(angles))
+
+
+def constant_tables(length, width):
+    exponents = -np.arange(width // 2, dtype=np.float32) * np.float32(2.0) / np.float32(width)
+    inv_freqs = np.power(np.float32(ROPE_BASE), exponents, dtype=np.float32)
+    angles = np.arange(length, dtype=np.float32)[:, None] * inv_freqs[None, :]
+    return np.cos(angles), np.sin(angles)
 
 
 def rotate(rows, cos_tab, sine_tab):
@@ -111,10 +119,12 @@
     )
 
 
-def greet(places):
+def greet(places, meanwhile=None):
     barrier = pltpu.get_barrier_semaphore()
     for place in places:
         pl.semaphore_signal(barrier, inc=1, device_id=place, device_id_type=MESH)
+    if meanwhile is not None:
+        meanwhile()
     pl.semaphore_wait(barrier, len(places))
 
 
@@ -252,21 +262,38 @@
 OWN = (0, 128)
 
 
-def feed_forward_kernel(hid, middle, factor, cot, w_hbm, wd_hbm,
-                        out_o, d_hid_o, gain_o, wd_grad, gu_grad,
-                        wgu, wd, ha, gu, act, part, buf, df, dgu, total, stage,
+def by_rows(body):
+    def step(i, carry):
+        body(pl.ds(pl.multiple_of(i * 16, 16), 16))
+        return carry
+
+    lax.fori_loop(0, TOK // 16, step, 0)
+
+
+def feed_forward_kernel(branch, block, gains, cot, w_hbm, wd_hbm,
+                        out_o, d_mid_o, d_branch_o, gain_o, wd_grad, gu_grad,
+                        wgu, wd, ha, gu, act, part, buf, df, dgu, middle, total, stage,
                         w_sem, ags, agr, rss, rsr, out_sem):
     gather = [SlotGather(b, ags.at[i], agr.at[i]) for i, b in enumerate((ha, df))]
     scatter = [SlotScatter(part, buf, rss.at[i], rsr.at[i]) for i in range(2)]
-    greet(gather[0].near)
     loads = [
         pltpu.make_async_copy(w_hbm, wgu, w_sem.at[0]),
         pltpu.make_async_copy(wd_hbm, wd, w_sem.at[1]),
     ]
-    ha[0:TOK] = hid[...]
-    gather[0].step(0)
     for c in loads:
         c.start()
+
+    def head():
+        def rows(r):
+            mid = block[r].astype(F32) + rms_parts(branch[r])[1] * (1.0 + gains[1:2])
+            middle[r] = mid
+            ha[r] = (rms_parts(mid)[1] * (1.0 + gains[2:3])).astype(BF)
+
+        by_rows(rows)
+
+    greet(gather[0].near, head)
+    gather[0].step(0)
+    gain_o[...] = jnp.zeros(gain_o.shape, F32)
     loads[0].wait()
 
     def gate_up(first, count):
@@ -344,14 +371,21 @@
     gather[0].drain()
     scatter[0].drain()
 
-    branch = total[...]
-    inverse, normed = rms_parts(branch)
-    out_cot = cot[...].astype(F32)
-    scale = factor[...]
-    df[0:TOK] = norm_back(out_cot * scale, normed, inverse).astype(BF)
+    def turn(r):
+        inverse, normed = rms_parts(total[r])
+        df[r] = norm_back(cot[r].astype(F32) * (1.0 + gains[3:4]), normed, inverse).astype(BF)
+
+    def add_gain(i, value):
+        gain_o[i : i + 1, 0:D] = gain_o[i : i + 1, 0:D] + jnp.sum(value, axis=0, keepdims=True)
+
+    def outputs(r):
+        normed = rms_parts(total[r])[1]
+        out_o[r] = (middle[r] + normed * (1.0 + gains[3:4])).astype(BF)
+        add_gain(3, cot[r].astype(F32) * normed)
+
+    by_rows(turn)
     gather[1].step(0)
-    out_o[...] = (middle[...] + normed * scale).astype(BF)
-    gain_o[...] = jnp.sum(out_cot * normed, axis=0, keepdims=True)
+    by_rows(outputs)
     active_back(*OWN)
     for step, pair in enumerate(PAIRS):
         gather[1].step(step + 1)
@@ -364,20 +398,32 @@
     for step, pair in enumerate(PAIRS[::-1]):
         hidden_part(*pair, part)
         scatter[1].step(step + 1)
-        grad_tiles(done, done + 6)
-        done += 6
-    hidden_part(*OWN, d_hid_o)
-    scatter[1].finish(d_hid_o)
+        grad_tiles(done, done + 8 + step // 2)
+        done += 8 + step // 2
+    hidden_part(*OWN, total)
     n_tiles = n_down + ha.shape[1] // TILE
     grad_tiles(done, n_tiles)
+    scatter[1].finish(total)
+
+    def tail(r):
+        inv_mid, normed_mid = rms_parts(middle[r])
+        d_hidden = total[r]
+        add_gain(2, d_hidden * normed_mid)
+        d_mid = cot[r].astype(F32) + norm_back(d_hidden * (1.0 + gains[2:3]), normed_mid, inv_mid)
+        d_mid_o[r] = d_mid
+        inv_post, normed_post = rms_parts(branch[r])
+        add_gain(1, d_mid * normed_post)
+        d_branch_o[r] = norm_back(d_mid * (1.0 + gains[1:2]), normed_post, inv_post).astype(BF)
+
+    by_rows(tail)
     for i in (n_tiles - 2, n_tiles - 1):
         grad_out(i).wait()
     gather[1].drain()
     scatter[1].drain()
 
 
-def feed_forward(hidden_ffn, middle, factor, out_grad, w_in, w_down, collective_id):
-    rows, width = hidden_ffn.shape
+def feed_forward(branch, block, gains, out_grad, w_in, w_down, collective_id):
+    rows, width = branch.shape
     total = RING * rows
 
     def full(*shape, dtype=F32):
@@ -386,23 +432,23 @@
     return pl.pallas_call(
         feed_forward_kernel,
         out_shape=[
-            full(rows, width, dtype=BF), full(rows, width), full(1, width),
+            full(rows, width, dtype=BF), full(rows, width), full(rows, width, dtype=BF), full(8, PADDED),
             full(UNITS, width, dtype=BF), full(width, 2 * UNITS, dtype=BF),
         ],
         in_specs=[VMEM] * 4 + [HBM] * 2,
-        out_specs=[VMEM] * 3 + [HBM] * 2,
+        out_specs=[VMEM] * 4 + [HBM] * 2,
         scratch_shapes=[
             pltpu.VMEM((width, 2 * UNITS), BF), pltpu.VMEM((UNITS, width), BF),
             pltpu.VMEM((total, width), BF), pltpu.VMEM((total, 2 * UNITS), F32), pltpu.VMEM((total, UNITS), BF),
             pltpu.VMEM((total, width), BF), pltpu.VMEM((2, 4, rows, width), BF),
             pltpu.VMEM((total, width), BF), pltpu.VMEM((total, 2 * UNITS), BF),
-            pltpu.VMEM((rows, width), F32), pltpu.VMEM((2, TILE, width), BF),
+            pltpu.VMEM((rows, width), F32), pltpu.VMEM((rows, width), F32), pltpu.VMEM((2, TILE, width), BF),
             DMA((2,)),
             DMA((2, 2, 4, SUB)), DMA((2, 2, 4, SUB)), DMA((2, 2, 4, SUB)), DMA((2, 2, 4, SUB)),
             DMA((2,)),
         ],
         compiler_params=params(collective_id, 60),
-    )(hidden_ffn, middle, factor, out_grad, w_in, w_down)
+    )(branch, block, gains, out_grad, w_in, w_down)
 
 
 WIDTHS = (UNITS, UNITS, HD, HD, HD)
@@ -653,8 +699,9 @@
         remote(dst, dst, pls.at[zq], plr.at[zq], sibling).wait_recv()
     for slot in range(RING):
         place(slot, 1)
+    start_round(6)
+    start_round(2)
     end_round(1)
-    start_round(2)
 
     factor = 1.0 + gain_o[0:1]
 
@@ -675,7 +722,8 @@
         k_o[r] = rotate(fold_rows(rows, wq[:, HD : 2 * HD]), *tabs).astype(BF)
         v_o[r] = fold_rows(rows, wq[:, 2 * HD : 3 * HD]).astype(BF)
     end_round(4)
-    start_round(6)
+    start_round(7)
+    start_round(3)
     end_across(1)
 
     def swap(zq, kept):
@@ -711,10 +759,8 @@
         swap(i, False).start()
         if i == 0:
             end_round(2)
-            start_round(3)
         if i == 2:
             end_round(5)
-            start_round(7)
             end_across(2)
             for yq in (0, 1):
                 rows_on(yq, 0)
@@ -796,7 +842,7 @@
 AHEAD = 2
 
 
-def backward_kernel(d_branch, gu_in, down_in, hidden, wq, wo, q_in, k_in, v_in, att, inv, cos, sine, normed, gain_in,
+def backward_kernel(d_branch, gu_in, down_in, hidden, wq, wo, q_in, k_in, v_in, att, inv, cos, sine, block_in, gain_in,
                     d_hid_o, gain_o, c_gu, c_q, down_o, out_o,
                     ring, seq, part, buf, d_att, d_qkv, dk, dv, grad_q, aq, bq,
                     own, a_gu, b_gu, down_own, da, db, og, oa, ob, ga, gsum,
@@ -1109,7 +1155,11 @@
     for j in range(4, RING):
         q_round(j)
     scatter.finish(d_hid_o)
-    gain_in[0:1, 0:D] = jnp.sum(d_hid_o[...] * normed[...], axis=0, keepdims=True)
+    def pre_gain(r):
+        value = d_hid_o[r] * rms_parts(block_in[r].astype(F32))[1]
+        gain_in[0:1, 0:D] = gain_in[0:1, 0:D] + jnp.sum(value, axis=0, keepdims=True)
+
+    by_rows(pre_gain)
     go(gain_a())
     gain_a().wait_recv()
     gsum[0] = gain_in[...] + gsum[2]
@@ -1140,7 +1190,7 @@
 
 
 def backward(d_branch, gu, down, hidden, w_qkv, w_out, queries, keys, values, attended, inv_total, cos_tab, sine_tab,
-             normed_pre, gain_parts, collective_id):
+             block, gain_parts, collective_id):
     n = 4 * RING
     rows, width = d_branch.shape
     shard = gu.shape[0] // n
@@ -1187,10 +1237,10 @@
             DMA((2, 4)), DMA((2, 4)), DMA((RING + 2,)), DMA((RING + 2,)),
         ],
         compiler_params=params(collective_id, 60),
-    )(d_branch, gu, down, hidden, w_qkv, w_out, queries, keys, values, attended, inv_total, cos_tab, sine_tab, normed_pre, gain_parts)
-
-
-def results_kernel(gu, qkv, down, out, d_hidden, d_middle, normed, inverse, factor,
+    )(d_branch, gu, down, hidden, w_qkv, w_out, queries, keys, values, attended, inv_total, cos_tab, sine_tab, block, gain_parts)
+
+
+def results_kernel(gu, qkv, down, out, d_hidden, d_middle, block, gains,
                    gate_o, up_o, query_o, key_o, value_o, down_o, out_o, token_o):
     for i in range(2):
         units, heads = pl.ds(i * UNITS, UNITS), pl.ds(i * HD, HD)
@@ -1201,11 +1251,12 @@
     value_o[...] = qkv[0, :, 2 * HD :].astype(F32) + qkv[1, :, 2 * HD :].astype(F32)
     down_o[...] = down[...].astype(F32)
     out_o[...] = out[...].astype(F32)
-    back = norm_back(d_hidden[...] * factor[...], normed[...], inverse[...])
+    inverse, normed = rms_parts(block[...].astype(F32))
+    back = norm_back(d_hidden[...] * (1.0 + gains[0:1]), normed, inverse)
     token_o[...] = (d_middle[...] + back).astype(BF)
 
 
-def results(gu, qkv, down, out, d_hidden, d_middle, normed, inverse, factor):
+def results(gu, qkv, down, out, d_hidden, d_middle, block, gains):
     steps = RING // 2
     shard, width = gu.shape[1], down.shape[1]
     tok, down_rows, out_rows = d_hidden.shape[0] // steps, down.shape[0] // steps, out.shape[0] // steps
@@ -1229,14 +1280,14 @@
         in_specs=[
             pl.BlockSpec((2, shard, 2 * UNITS), lambda i: (i, 0, 0)), pl.BlockSpec((2, shard, 3 * HD), lambda i: (i, 0, 0)),
             rows(down_rows, width), rows(out_rows, width), rows(tok, width), rows(tok, width), rows(tok, width),
-            rows(tok, 1), pl.BlockSpec((1, width), lambda i: (0, 0)),
+            pl.BlockSpec(gains.shape, lambda i: (0, 0)),
         ],
         out_specs=[
             columns(2 * UNITS), columns(2 * UNITS), columns(2 * HD), columns(HD), columns(HD),
             rows(down_rows, width), rows(out_rows, width), rows(tok, width),
         ],
         compiler_params=pltpu.CompilerParams(vmem_limit_bytes=60 * 2**20),
-    )(gu, qkv, down, out, d_hidden, d_middle, normed, inverse, factor)
+    )(gu, qkv, down, out, d_hidden, d_middle, block, gains)
 
 
 def on_ring(
@@ -1249,36 +1300,22 @@
     mine = lax.axis_index("ctx") * 4 + lax.axis_index("fsdp")
     gains = jnp.stack([pre_gain, post_gain, pre_ffn_gain, post_ffn_gain]).astype(F32)
     gains = lax.dynamic_update_slice(jnp.zeros((8, WINDOW), F32), gains, (0, (mine * shard_gain) % 128))
-    cos_tab, sine_tab = rope_tables(jnp.arange(length, dtype=jnp.int32), HD)
+    cos_tab, sine_tab = (jnp.asarray(table) for table in constant_tables(length, HD))
     w_gu, down_in, hidden, w_qkv, out_in, gains, queries, keys, values, attended, inv_total, branch = forward(
         w_gate, w_up, w_query, w_key, w_value, w_down, w_out, tokens[0], gains, cos_tab, sine_tab, next(ids)
     )
     w_gu, hidden = w_gu.reshape(D, 2 * UNITS), hidden.reshape(length, D)
     w_dn = down_in.reshape(UNITS, D)
     w_ot = out_in.reshape(HD, D)
-    pre_factor, post_factor, pre_ffn_factor, post_ffn_factor = (1.0 + gains[i] for i in range(4))
-    resid_in = tokens[0].astype(F32)
-    inv_pre, normed_pre = rms_parts(resid_in)
-    inv_post, normed_post = rms_parts(branch)
-    middle = resid_in + normed_post * post_factor
-    inv_mid, normed_mid = rms_parts(middle)
-    hidden_ffn = (normed_mid * pre_ffn_factor).astype(BF)
-    output, d_hidden_ffn, post_ffn_part, down_part, gu_part = feed_forward(
-        hidden_ffn, middle, post_ffn_factor[None], out_grad[0], w_gu, w_dn, next(ids)
-    )
-    post_ffn_part = post_ffn_part[0]
-    out_cot = out_grad[0].astype(F32)
-    pre_ffn_part = jnp.sum(d_hidden_ffn * normed_mid, axis=0)
-    d_middle = out_cot + norm_back(d_hidden_ffn * pre_ffn_factor, normed_mid, inv_mid)
-    post_part = jnp.sum(d_middle * normed_post, axis=0)
-    d_branch = norm_back(d_middle * post_factor, normed_post, inv_post).astype(BF)
-    gain_parts = jnp.stack([jnp.zeros_like(post_part), post_part, pre_ffn_part, post_ffn_part])
+    output, d_middle, d_branch, gain_parts, down_part, gu_part = feed_forward(
+        branch, tokens[0], gains, out_grad[0], w_gu, w_dn, next(ids)
+    )
     d_hidden, gain_g, gu_g, qkv_g, down_g, out_g = backward(
         d_branch, gu_part, down_part, hidden, w_qkv, w_ot, queries, keys, values, attended, inv_total,
-        cos_tab, sine_tab, normed_pre, jnp.pad(gain_parts, ((0, 4), (0, PADDED - D))), next(ids),
+        cos_tab, sine_tab, tokens[0], gain_parts, next(ids),
     )
     gate_g, up_g, query_g, key_g, value_g, down_g, out_g, token_grad = results(
-        gu_g, qkv_g, down_g, out_g, d_hidden, d_middle, normed_pre, inv_pre, pre_factor[None]
+        gu_g, qkv_g, down_g, out_g, d_hidden, d_middle, tokens[0], gains
     )
     gain_g = lax.dynamic_slice(gain_g, (0, (mine * shard_gain) % 128), (4, shard_gain))
     return (

time: 605 us -> 604 us (level)
  other arithmetic: 13.9 us -> 0.72 us
  Pallas kernels: 581 us -> 592 us
    pallas_call x1, Pallas kernels: 203 us -> 213 us  [feed_forward(): pl.pallas_call(feed_forward_kernel, out_shape=[full(rows, width, dtype=BF...]
where the time goes in v7:
time: 604 us; the launch traced here: 596 us
  Pallas kernels  592 us (98%)
    pallas_call x1, Pallas kernels, feed_forward(): pl.pallas_call(feed_forward_kernel, out_shape=[full(rows, width, dtype=BF...  213 us
    pallas_call x1, Pallas kernels, forward(): pl.pallas_call(forward_kernel, out_shape=[full(n, shard, 2 * UNITS), full...  189 us
    pallas_call x1, Pallas kernels, backward(): pl.pallas_call(body, out_shape=[out(rows, width, dtype=F32), out(8, WINDO...  182 us

profile of v7, /device:TPU:1, one launch (start us, length us, event | category | flops | bytes accessed | tf_op | source)
XLA Modules:
  0.0 596.5 jit_solution(1701091265770940383)
XLA Ops:
  0.7 0.7 maximum_convert_fusion
  1.4 0.6 dynamic_update_slice.3.gain_in
  2.0 0.0 copy-start.1
  2.0 0.6 copy-done.1
  2.6 189.1 %shard_map.246 = (bf16[32,72,2304]{2,1,0:T(8,128)(2,1)}, bf16[4,288,2304]{2,1,0:T(8,128)(2,1)}, bf16[8,128,2304]{2,1,0:T(8,128)(2,1)}, bf16[2304,768]{1,0:T(8,12...) custom-call(bf16[72,9216]{1,0:T(8,128)(2,1)} %gate.1, ...), custom_call_target="tpu_custom_call" | custom-call | tf_op jit(solution)/shard_map/pallas_call | solution.py:817
  191.7 212.6 %shard_map.247 = (bf16[128,2304]{1,0:T(8,128)(2,1)}, f32[128,2304]{1,0:T(8,128)}, bf16[128,2304]{1,0:T(8,128)(2,1)}, f32[8,2432]{1,0:T(8,128)}, bf16[1152,2304]{1,0:T(8,128)(2,1)}, /*index=5*/bf16[2304,2304]{1,0:T(8,128)(2,1)}) custom-call(f32[128,2304]{1,0:T(8,128)} %get-tuple-element.45.branch, bf16[128,2304]{1,0:T(8,128)(2,1)} %bitcast.25, ...), custom_call_target="tpu_custom_call" | custom-call | tf_op jit(solution)/shard_map/pallas_call | solution.py:432
  404.3 181.8 %shard_map.248 = (f32[128,2304]{1,0:T(8,128)}, f32[8,256]{1,0:T(8,128)}, bf16[8,72,2304]{2,1,0:T(8,128)(2,1)}, bf16[8,72,768]{2,1,0:T(8,128)(2,1)}, bf16[288,2304]{1,0:T(8,128)(2,1)}, /*index=5*/bf16[64,2304]{1,0:T(8,128)(2,1)}) custom-call(bf16[128,2304]{1,0:T(8,128)(2,1)} %get-tuple-element.50.refs_0_, bf16[32,72,2304]{2,1,0:T(8,128)(2,1)} %bitcast.23, ...), custom_call_target="tpu_custom_call" | custom-call | tf_op jit(solution)/shard_map/pallas_call | solution.py:1213
  586.1 0.8 constant_dynamic-slice_fusion
  586.9 0.5 slice_bitcast_fusion
  587.4 0.0 copy-start
  587.4 8.1 %shard_map.249 = (f32[72,9216]{1,0:T(8,128)}, f32[72,9216]{1,0:T(8,128)}, f32[72,2048]{1,0:T(8,128)}, f32[72,1024]{1,0:T(8,128)}, f32[72,1024]{1,0:T(8,128)}, /*...) custom-call(bf16[8,72,2304]{2,1,0:T(8,128)(2,1)} %get-tuple-element.62.gu, ...), custom_call_target="tpu_custom_call" | custom-call | tf_op jit(solution)/shard_map/pallas_call | solution.py:1273
  595.5 0.0 copy-done
  595.5 0.8 copy.30
  (1 shorter events, 0.0 us)
Async XLA Ops:
  2.0 0.6 copy-start.1
  587.4 8.1 %copy-start = (bf16[128,2304]{1,0:T(8,128)(2,1)S(1)}, bf16[128,2304]{1,0:T(8,128)(2,1)}, u32[]{:S(2)}) copy-start(bf16[128,2304]{1,0:T(8,128)(2,1)} %get-tuple-element.49) | copy-start | bytes 1769476

commit v8 on v7

--- a/solution.py
+++ b/solution.py
@@ -1,5 +1,3 @@
-import functools
-
 import jax
 import jax.numpy as jnp
 import numpy as np
@@ -24,13 +22,6 @@
 DMA = pltpu.SemaphoreType.DMA
 BF = jnp.bfloat16
 F32 = jnp.float32
-
-
-def rope_tables(positions, width):
-    half_width = width // 2
-    inv_freqs = ROPE_BASE ** (-jnp.arange(half_width, dtype=F32) * 2.0 / width)
-    angles = positions.astype(F32)[:, None] * inv_freqs[None, :]
-    return (jnp.cos(angles), jnp.sin(angles))
 
 
 def constant_tables(length, width):
@@ -264,10 +255,10 @@
 
 def by_rows(body):
     def step(i, carry):
-        body(pl.ds(pl.multiple_of(i * 16, 16), 16))
+        body(pl.ds(pl.multiple_of(i * 32, 32), 32))
         return carry
 
-    lax.fori_loop(0, TOK // 16, step, 0)
+    lax.fori_loop(0, TOK // 32, step, 0)
 
 
 def feed_forward_kernel(branch, block, gains, cot, w_hbm, wd_hbm,
@@ -487,8 +478,8 @@
 
 
 def forward_kernel(gate, up, query, key, value, down, out, block, gain_in, cos, sine,
-                   w_gu, d_ref, hidden_o, wq, wo, gain_o, q_o, k_o, v_o, att_o, inv_o, branch_o,
-                   ring, seq, seq_part, part, buf, wq_in, own, relay, ga, gsum,
+                   w_gu, d_ref, hidden_o, wq_h, q_h, k_h, v_h, att_h, wo, gain_o, inv_o, branch_o,
+                   wq, q_o, k_o, v_o, att_o, ring, seq, seq_part, part, buf, wq_in, own, relay, ga, gsum,
                    load, ags, agr, pls, plr, rss, rsr, sws, swr, s1, r1, s2, r2, s3, r3,
                    q1, t1, q2, t2, q3, t3, s4, r4, s5, r5, sg, rg):
     z, core, y, x = my_place()
@@ -675,9 +666,8 @@
     gather.step(3)
     place(5, 0)
     place(6, 0)
-    start_round(4)
-    start_round(5)
-    start_round(1)
+    for j in (4, 5, 1, 6, 2, 7, 3):
+        start_round(j)
     relay_load.wait()
     for xq in (0, 1):
         rows_out(xq, 0, 0)
@@ -692,6 +682,8 @@
         return carry
 
     lax.fori_loop(0, 8, join, 0)
+    results_out = [pltpu.make_async_copy(wq, wq_h, load.at[22])]
+    results_out[0].start()
     gather.finish()
     place(7, 0)
     for zq in range(NZ):
@@ -699,8 +691,6 @@
         remote(dst, dst, pls.at[zq], plr.at[zq], sibling).wait_recv()
     for slot in range(RING):
         place(slot, 1)
-    start_round(6)
-    start_round(2)
     end_round(1)
 
     factor = 1.0 + gain_o[0:1]
@@ -721,9 +711,10 @@
         q_o[r] = (rotate(fold_rows(rows, wq[:, 0:HD]), *tabs) * (HD ** (-0.5))).astype(BF)
         k_o[r] = rotate(fold_rows(rows, wq[:, HD : 2 * HD]), *tabs).astype(BF)
         v_o[r] = fold_rows(rows, wq[:, 2 * HD : 3 * HD]).astype(BF)
+    for i, (src, dst) in enumerate(((q_o, q_h), (k_o, k_h), (v_o, v_h))):
+        results_out.append(pltpu.make_async_copy(src, dst, load.at[23 + i]))
+        results_out[-1].start()
     end_round(4)
-    start_round(7)
-    start_round(3)
     end_across(1)
 
     def swap(zq, kept):
@@ -764,6 +755,8 @@
             end_across(2)
             for yq in (0, 1):
                 rows_on(yq, 0)
+    results_out.append(pltpu.make_async_copy(att_o, att_h, load.at[26]))
+    results_out[-1].start()
     for zq in range(NZ):
         swap(zq, True).wait()
         swapped(zq).wait_recv()
@@ -797,6 +790,8 @@
                 remote(pair[a][0], pair[a][1].at[mine], s4.at[xq, a], r4.at[y, a], device(z, x, core, xq)).wait_send()
     keep_own.wait()
     keep_hidden.wait()
+    for c in results_out:
+        c.wait()
     for zq in range(NZ):
         swap(zq, False).wait_send()
     gather.drain()
@@ -817,18 +812,20 @@
     return pl.pallas_call(
         forward_kernel,
         out_shape=[
-            full(n, shard, 2 * UNITS), full(4, *down.shape), full(*blocks), full(width, 3 * HD), full(4, *out.shape),
-            full(8, D, dtype=F32), full(total, HD), full(total, HD), full(total, HD),
-            full(total, HD, dtype=F32), full(total, 1, dtype=F32), full(rows, width, dtype=F32),
+            full(n, shard, 2 * UNITS), full(4, *down.shape), full(*blocks), full(width, 3 * HD),
+            full(total, HD), full(total, HD), full(total, HD), full(total, HD, dtype=F32),
+            full(4, *out.shape), full(8, D, dtype=F32), full(total, 1, dtype=F32), full(rows, width, dtype=F32),
         ],
         in_specs=[HBM] * 7 + [VMEM] * 4,
-        out_specs=[HBM] * 3 + [VMEM] * 9,
+        out_specs=[HBM] * 8 + [VMEM] * 4,
         scratch_shapes=[
+            pltpu.VMEM((width, 3 * HD), BF), pltpu.VMEM((total, HD), BF), pltpu.VMEM((total, HD), BF), pltpu.VMEM((total, HD), BF),
+            pltpu.VMEM((total, HD), F32),
             pltpu.VMEM((total, width), BF), pltpu.VMEM(blocks, BF), pltpu.VMEM(blocks, BF), pltpu.VMEM((total, width), BF),
             pltpu.VMEM((2, 4, rows, width), BF), pltpu.VMEM((n, shard, 3 * HD), BF),
             pltpu.VMEM((shard, 2 * UNITS), BF), pltpu.VMEM(down.shape, BF),
             pltpu.VMEM((RING,) + gains.shape, F32), pltpu.VMEM((4, 8, PADDED), F32),
-            DMA((22,)),
+            DMA((27,)),
             DMA((2, 4, SUB)), DMA((2, 4, SUB)), DMA((NZ,)), DMA((NZ,)), DMA((2, 4, SUB)), DMA((2, 4, SUB)), DMA((NZ,)), DMA((NZ,)),
             DMA((RING, 2)), DMA((RING, 2)), DMA((RING,)), DMA((RING,)), DMA((RING, 2)), DMA((RING, 2)),
             DMA((RING, 3)), DMA((RING, 3)), DMA((RING,)), DMA((RING,)), DMA((RING, 2)), DMA((RING, 2)),
@@ -842,7 +839,7 @@
 AHEAD = 2
 
 
-def backward_kernel(d_branch, gu_in, down_in, hidden, wq, wo, q_in, k_in, v_in, att, inv, cos, sine, block_in, gain_in,
+def backward_kernel(ready, d_branch, gu_in, down_in, hidden, wq, wo, q_in, k_in, v_in, att, inv, cos, sine, block_in, gain_in,
                     d_hid_o, gain_o, c_gu, c_q, down_o, out_o,
                     ring, seq, part, buf, d_att, d_qkv, dk, dv, grad_q, aq, bq,
                     own, a_gu, b_gu, down_own, da, db, og, oa, ob, ga, gsum,
@@ -1020,6 +1017,7 @@
     gather.drain()
     hidden_load = pltpu.make_async_copy(hidden, ring, load.at[14])
     hidden_load.start()
+    ready()
 
     for c in range(0, RING, 2):
         rows = pl.ds(c * TOK, 2 * TOK)
@@ -1206,9 +1204,20 @@
         ins, rest = refs[:14], refs[14:]
         gains_ref, rest = rest[0], rest[1:]
         outs, scr = rest[:6], rest[6:]
-        gain_scr = scr[0]
+        gain_scr, loaded, sems, scr = scr[0], scr[1:8], scr[8], scr[9:]
         gain_scr[...] = gains_ref[...]
-        backward_kernel(*ins, gain_scr, *outs, *scr[1:])
+        ins = list(ins)
+        copies = []
+        for i, place in enumerate((4, 6, 7, 8, 9, 11, 12)):
+            copies.append(pltpu.make_async_copy(ins[place], loaded[i], sems.at[i]))
+            copies[-1].start()
+            ins[place] = loaded[i]
+
+        def ready():
+            for c in copies:
+                c.wait()
+
+        backward_kernel(ready, *ins, gain_scr, *outs, *scr)
 
     return pl.pallas_call(
         body,
@@ -1217,10 +1226,13 @@
             out(RING, shard, 2 * UNITS), out(RING, shard, 3 * HD),
             out(down_rows, width), out(out_rows, width),
         ],
-        in_specs=[HBM] * 4 + [VMEM] * 11,
+        in_specs=[HBM] * 5 + [VMEM] + [HBM] * 4 + [VMEM] + [HBM] * 2 + [VMEM] * 2,
         out_specs=[VMEM] * 2 + [HBM] * 4,
         scratch_shapes=[
             pltpu.VMEM(gain_shape, F32),
+            pltpu.VMEM((width, 3 * HD), BF), pltpu.VMEM((total, HD), BF), pltpu.VMEM((total, HD), BF), pltpu.VMEM((total, HD), BF),
+            pltpu.VMEM((total, HD), F32), pltpu.VMEM((total, HD // 2), F32), pltpu.VMEM((total, HD // 2), F32),
+            DMA((7,)),
             pltpu.VMEM((total, width), BF), pltpu.VMEM((RING, rows, width), BF), pltpu.VMEM((total, width), BF),
             pltpu.VMEM((2, 4, rows, width), BF),
             pltpu.VMEM((total, HD), BF), pltpu.VMEM((total, 3 * HD), BF),
@@ -1301,7 +1313,7 @@
     gains = jnp.stack([pre_gain, post_gain, pre_ffn_gain, post_ffn_gain]).astype(F32)
     gains = lax.dynamic_update_slice(jnp.zeros((8, WINDOW), F32), gains, (0, (mine * shard_gain) % 128))
     cos_tab, sine_tab = (jnp.asarray(table) for table in constant_tables(length, HD))
-    w_gu, down_in, hidden, w_qkv, out_in, gains, queries, keys, values, attended, inv_total, branch = forward(
+    w_gu, down_in, hidden, w_qkv, queries, keys, values, attended, out_in, gains, inv_total, branch = forward(
         w_gate, w_up, w_query, w_key, w_value, w_down, w_out, tokens[0], gains, cos_tab, sine_tab, next(ids)
     )
     w_gu, hidden = w_gu.reshape(D, 2 * UNITS), hidden.reshape(length, D)

time: 604 us -> 589 us (0.975)
  Pallas kernels: 592 us -> 576 us
    pallas_call x1, Pallas kernels: 189 us -> 180 us  [forward(): pl.pallas_call(forward_kernel, out_shape=[full(n, shard, 2 * UNITS), full...]
where the time goes in v8:
time: 589 us; the launch traced here: 581 us
  Pallas kernels  576 us (98%)
    pallas_call x1, Pallas kernels, feed_forward(): pl.pallas_call(feed_forward_kernel, out_shape=[full(rows, width, dtype=BF...  209 us
    pallas_call x1, Pallas kernels, backward(): pl.pallas_call(body, out_shape=[out(rows, width, dtype=F32), out(8, WINDO...  180 us
    pallas_call x1, Pallas kernels, forward(): pl.pallas_call(forward_kernel, out_shape=[full(n, shard, 2 * UNITS), full...  180 us

profile of v8, /device:TPU:1, one launch (start us, length us, event | category | flops | bytes accessed | tf_op | source)
XLA Modules:
  0.0 581.0 jit_solution(17740780281160030902)
XLA Ops:
  0.7 0.7 maximum_convert_fusion
  1.4 0.6 dynamic_update_slice.3.gain_in
  2.0 0.0 copy-start.1
  2.0 0.6 copy-done.1
  2.6 179.6 %shard_map.246 = (bf16[32,72,2304]{2,1,0:T(8,128)(2,1)}, bf16[4,288,2304]{2,1,0:T(8,128)(2,1)}, bf16[8,128,2304]{2,1,0:T(8,128)(2,1)}, bf16[2304,768]{1,0:T(8,12...) custom-call(bf16[72,9216]{1,0:T(8,128)(2,1)} %gate.1, ...), custom_call_target="tpu_custom_call" | custom-call | tf_op jit(solution)/shard_map/pallas_call | solution.py:812
  182.2 208.6 %shard_map.247 = (bf16[128,2304]{1,0:T(8,128)(2,1)}, f32[128,2304]{1,0:T(8,128)}, bf16[128,2304]{1,0:T(8,128)(2,1)}, f32[8,2432]{1,0:T(8,128)}, bf16[1152,2304]{1,0:T(8,128)(2,1)}, /*index=5*/bf16[2304,2304]{1,0:T(8,128)(2,1)}) custom-call(f32[128,2304]{1,0:T(8,128)} %get-tuple-element.45.branch, bf16[128,2304]{1,0:T(8,128)(2,1)} %bitcast.25, ...), custom_call_target="tpu_custom_call" | custom-call | tf_op jit(solution)/shard_map/pallas_call | solution.py:423
  390.9 179.8 %shard_map.248 = (f32[128,2304]{1,0:T(8,128)}, f32[8,256]{1,0:T(8,128)}, bf16[8,72,2304]{2,1,0:T(8,128)(2,1)}, bf16[8,72,768]{2,1,0:T(8,128)(2,1)}, bf16[288,2304]{1,0:T(8,128)(2,1)}, /*index=5*/bf16[64,2304]{1,0:T(8,128)(2,1)}) custom-call(bf16[128,2304]{1,0:T(8,128)(2,1)} %get-tuple-element.50.refs_0_, bf16[32,72,2304]{2,1,0:T(8,128)(2,1)} %bitcast.23, ...), custom_call_target="tpu_custom_call" | custom-call | tf_op jit(solution)/shard_map/pallas_call | solution.py:1222
  570.6 0.8 constant_dynamic-slice_fusion
  571.4 0.5 slice_bitcast_fusion
  571.9 0.0 copy-start
  571.9 8.1 %shard_map.249 = (f32[72,9216]{1,0:T(8,128)}, f32[72,9216]{1,0:T(8,128)}, f32[72,2048]{1,0:T(8,128)}, f32[72,1024]{1,0:T(8,128)}, f32[72,1024]{1,0:T(8,128)}, /*...) custom-call(bf16[8,72,2304]{2,1,0:T(8,128)(2,1)} %get-tuple-element.62.gu, ...), custom_call_target="tpu_custom_call" | custom-call | tf_op jit(solution)/shard_map/pallas_call | solution.py:1285
  580.0 0.0 copy-done
  580.0 0.8 copy.30
  (1 shorter events, 0.0 us)
Async XLA Ops:
  2.0 0.6 copy-start.1
  571.9 8.1 %copy-start = (bf16[128,2304]{1,0:T(8,128)(2,1)S(1)}, bf16[128,2304]{1,0:T(8,128)(2,1)}, u32[]{:S(2)}) copy-start(bf16[128,2304]{1,0:T(8,128)(2,1)} %get-tuple-element.49) | copy-start | bytes 1769476

commit v9 on v8

--- a/solution.py
+++ b/solution.py
@@ -325,7 +325,16 @@
 
         tiles(3, 768, column)
 
+    def hidden_near():
+        def column(cols):
+            value = contract_cols(dgu[0 : 3 * TOK], wgu[cols])
+            total[:, cols] = value[0:TOK]
+            part[TOK : 3 * TOK, cols] = value[TOK:].astype(BF)
+
+        tiles(3, 768, column)
+
     n_down = UNITS // TILE
+    n_tiles = n_down + ha.shape[1] // TILE
 
     def grad_out(i):
         slot = i % 2
@@ -387,13 +396,14 @@
     scatter[1].step(0)
     done = 0
     for step, pair in enumerate(PAIRS[::-1]):
-        hidden_part(*pair, part)
+        if pair[0] == TOK:
+            hidden_near()
+        else:
+            hidden_part(*pair, part)
         scatter[1].step(step + 1)
-        grad_tiles(done, done + 8 + step // 2)
-        done += 8 + step // 2
-    hidden_part(*OWN, total)
-    n_tiles = n_down + ha.shape[1] // TILE
-    grad_tiles(done, n_tiles)
+        count = (8, 6, n_tiles - 14)[step]
+        grad_tiles(done, done + count)
+        done += count
     scatter[1].finish(total)
 
     def tail(r):

time: 589 us -> 583 us (0.990)
  Pallas kernels: 576 us -> 567 us
    pallas_call x1, Pallas kernels: 209 us -> 200 us  [feed_forward(): pl.pallas_call(feed_forward_kernel, out_shape=[full(rows, width, dtype=BF...]
where the time goes in v9:
time: 583 us; the launch traced here: 572 us
  Pallas kernels  567 us (97%)
    pallas_call x1, Pallas kernels, feed_forward(): pl.pallas_call(feed_forward_kernel, out_shape=[full(rows, width, dtype=BF...  200 us
    pallas_call x1, Pallas kernels, forward(): pl.pallas_call(forward_kernel, out_shape=[full(n, shard, 2 * UNITS), full...  180 us
    pallas_call x1, Pallas kernels, backward(): pl.pallas_call(body, out_shape=[out(rows, width, dtype=F32), out(8, WINDO...  179 us

profile of v9, /device:TPU:1, one launch (start us, length us, event | category | flops | bytes accessed | tf_op | source)
XLA Modules:
  0.0 571.7 jit_solution(14295813329635056284)
XLA Ops:
  0.7 0.7 maximum_convert_fusion
  1.4 0.6 dynamic_update_slice.3.gain_in
  2.0 0.0 copy-start.1
  2.0 0.6 copy-done.1
  2.6 179.6 %shard_map.246 = (bf16[32,72,2304]{2,1,0:T(8,128)(2,1)}, bf16[4,288,2304]{2,1,0:T(8,128)(2,1)}, bf16[8,128,2304]{2,1,0:T(8,128)(2,1)}, bf16[2304,768]{1,0:T(8,12...) custom-call(bf16[72,9216]{1,0:T(8,128)(2,1)} %gate.1, ...), custom_call_target="tpu_custom_call" | custom-call | tf_op jit(solution)/shard_map/pallas_call | solution.py:822
  182.2 199.5 %shard_map.247 = (bf16[128,2304]{1,0:T(8,128)(2,1)}, f32[128,2304]{1,0:T(8,128)}, bf16[128,2304]{1,0:T(8,128)(2,1)}, f32[8,2432]{1,0:T(8,128)}, bf16[1152,2304]{1,0:T(8,128)(2,1)}, /*index=5*/bf16[2304,2304]{1,0:T(8,128)(2,1)}) custom-call(f32[128,2304]{1,0:T(8,128)} %get-tuple-element.45.branch, bf16[128,2304]{1,0:T(8,128)(2,1)} %bitcast.25, ...), custom_call_target="tpu_custom_call" | custom-call | tf_op jit(solution)/shard_map/pallas_call | solution.py:433
  381.8 179.5 %shard_map.248 = (f32[128,2304]{1,0:T(8,128)}, f32[8,256]{1,0:T(8,128)}, bf16[8,72,2304]{2,1,0:T(8,128)(2,1)}, bf16[8,72,768]{2,1,0:T(8,128)(2,1)}, bf16[288,2304]{1,0:T(8,128)(2,1)}, /*index=5*/bf16[64,2304]{1,0:T(8,128)(2,1)}) custom-call(bf16[128,2304]{1,0:T(8,128)(2,1)} %get-tuple-element.50.refs_0_, bf16[32,72,2304]{2,1,0:T(8,128)(2,1)} %bitcast.23, ...), custom_call_target="tpu_custom_call" | custom-call | tf_op jit(solution)/shard_map/pallas_call | solution.py:1232
  561.3 0.8 constant_dynamic-slice_fusion
  562.0 0.5 slice_bitcast_fusion
  562.6 0.0 copy-start
  562.6 8.1 %shard_map.249 = (f32[72,9216]{1,0:T(8,128)}, f32[72,9216]{1,0:T(8,128)}, f32[72,2048]{1,0:T(8,128)}, f32[72,1024]{1,0:T(8,128)}, f32[72,1024]{1,0:T(8,128)}, /*...) custom-call(bf16[8,72,2304]{2,1,0:T(8,128)(2,1)} %get-tuple-element.62.gu, ...), custom_call_target="tpu_custom_call" | custom-call | tf_op jit(solution)/shard_map/pallas_call | solution.py:1295
  570.6 0.0 copy-done
  570.7 0.8 copy.30
  (1 shorter events, 0.0 us)
Async XLA Ops:
  2.0 0.6 copy-start.1
  562.6 8.1 %copy-start = (bf16[128,2304]{1,0:T(8,128)(2,1)S(1)}, bf16[128,2304]{1,0:T(8,128)(2,1)}, u32[]{:S(2)}) copy-start(bf16[128,2304]{1,0:T(8,128)(2,1)} %get-tuple-element.49) | copy-start | bytes 1769476

commit v10 on v9

--- a/solution.py
+++ b/solution.py
@@ -676,7 +676,7 @@
     gather.step(3)
     place(5, 0)
     place(6, 0)
-    for j in (4, 5, 1, 6, 2, 7, 3):
+    for j in (4, 1, 5, 2, 6, 3, 7):
         start_round(j)
     relay_load.wait()
     for xq in (0, 1):

time: 583 us -> 583 us (level)
  no operation moved by 1% of the time
where the time goes in v10:
time: 583 us; the launch traced here: 571 us
  Pallas kernels  566 us (97%)
    pallas_call x1, Pallas kernels, feed_forward(): pl.pallas_call(feed_forward_kernel, out_shape=[full(rows, width, dtype=BF...  199 us
    pallas_call x1, Pallas kernels, forward(): pl.pallas_call(forward_kernel, out_shape=[full(n, shard, 2 * UNITS), full...  180 us
    pallas_call x1, Pallas kernels, backward(): pl.pallas_call(body, out_shape=[out(rows, width, dtype=F32), out(8, WINDO...  179 us

profile of v10, /device:TPU:1, one launch (start us, length us, event | category | flops | bytes accessed | tf_op | source)
XLA Modules:
  0.0 571.1 jit_solution(10187975726913179463)
XLA Ops:
  0.7 0.7 maximum_convert_fusion
  1.4 0.6 dynamic_update_slice.3.gain_in
  2.0 0.0 copy-start.1
  2.0 0.6 copy-done.1
  2.6 179.6 %shard_map.246 = (bf16[32,72,2304]{2,1,0:T(8,128)(2,1)}, bf16[4,288,2304]{2,1,0:T(8,128)(2,1)}, bf16[8,128,2304]{2,1,0:T(8,128)(2,1)}, bf16[2304,768]{1,0:T(8,12...) custom-call(bf16[72,9216]{1,0:T(8,128)(2,1)} %gate.1, ...), custom_call_target="tpu_custom_call" | custom-call | tf_op jit(solution)/shard_map/pallas_call | solution.py:822
  182.2 199.3 %shard_map.247 = (bf16[128,2304]{1,0:T(8,128)(2,1)}, f32[128,2304]{1,0:T(8,128)}, bf16[128,2304]{1,0:T(8,128)(2,1)}, f32[8,2432]{1,0:T(8,128)}, bf16[1152,2304]{1,0:T(8,128)(2,1)}, /*index=5*/bf16[2304,2304]{1,0:T(8,128)(2,1)}) custom-call(f32[128,2304]{1,0:T(8,128)} %get-tuple-element.45.branch, bf16[128,2304]{1,0:T(8,128)(2,1)} %bitcast.25, ...), custom_call_target="tpu_custom_call" | custom-call | tf_op jit(solution)/shard_map/pallas_call | solution.py:433
  381.5 179.3 %shard_map.248 = (f32[128,2304]{1,0:T(8,128)}, f32[8,256]{1,0:T(8,128)}, bf16[8,72,2304]{2,1,0:T(8,128)(2,1)}, bf16[8,72,768]{2,1,0:T(8,128)(2,1)}, bf16[288,2304]{1,0:T(8,128)(2,1)}, /*index=5*/bf16[64,2304]{1,0:T(8,128)(2,1)}) custom-call(bf16[128,2304]{1,0:T(8,128)(2,1)} %get-tuple-element.50.refs_0_, bf16[32,72,2304]{2,1,0:T(8,128)(2,1)} %bitcast.23, ...), custom_call_target="tpu_custom_call" | custom-call | tf_op jit(solution)/shard_map/pallas_call | solution.py:1232
  560.8 0.8 constant_dynamic-slice_fusion
  561.5 0.5 slice_bitcast_fusion
  562.1 0.0 copy-start
  562.1 8.1 %shard_map.249 = (f32[72,9216]{1,0:T(8,128)}, f32[72,9216]{1,0:T(8,128)}, f32[72,2048]{1,0:T(8,128)}, f32[72,1024]{1,0:T(8,128)}, f32[72,1024]{1,0:T(8,128)}, /*...) custom-call(bf16[8,72,2304]{2,1,0:T(8,128)(2,1)} %get-tuple-element.62.gu, ...), custom_call_target="tpu_custom_call" | custom-call | tf_op jit(solution)/shard_map/pallas_call | solution.py:1295
  570.1 0.0 copy-done
  570.1 0.8 copy.30
  (1 shorter events, 0.0 us)
Async XLA Ops:
  2.0 0.6 copy-start.1
  562.1 8.1 %copy-start = (bf16[128,2304]{1,0:T(8,128)(2,1)S(1)}, bf16[128,2304]{1,0:T(8,128)(2,1)}, u32[]{:S(2)}) copy-start(bf16[128,2304]{1,0:T(8,128)(2,1)} %get-tuple-element.49) | copy-start | bytes 1769476
